TPU v7x, 128 devices: a whole 4x4x4 slice. The times are simulated.
128 devices in a mesh: row: 32 (over z, y, core), ch: 4 (over x).
Axes of the slice: x: 4, y: 4, z: 4, core: 2. Of those that a mesh axis runs over, the one named last changes fastest.
Arguments:
- pair: float32 [512, 512, 128], P('row'), may hold values from -6 to 6
- mask: int32 [512], replicated, may hold values 0 or 1
- in_gain: float32 [2, 128], replicated, may hold values from 0.1 to 1.9
- in_bias: float32 [2, 128], replicated, may hold values from -3 to 3
- w_proj: bfloat16 [2, 128, 4, 128], P(None, None, None, 'ch'), may hold values from -0.5 to 0.5
- w_gate: bfloat16 [2, 128, 128], replicated, may hold values from -0.5 to 0.5
- out_gain: float32 [2, 128], P(None, 'ch'), may hold values from 0.1 to 1.9
- out_bias: float32 [2, 128], P(None, 'ch'), may hold values from -3 to 3
- w_out: bfloat16 [2, 128, 128], P(None, 'ch'), may hold values from -0.5 to 0.5
Outputs:
- updated: float32 [512, 512, 128], P('row')
All inputs are finite; a program needn't handle non-finite values.
Results may differ from a plain program's by a relative error of at most 0.009.
Values may be sent and summed in bfloat16 or wider, within the bound.
No kernel may reach another device: no remote copies, remote signals or barrier semaphores. Data moves between devices by JAX's collectives and lax.ppermute only.
A program may use at most 192 MiB of HBM per device.

v0:
```python
import jax
import jax.numpy as jnp
from jax import lax
from jax.sharding import PartitionSpec as P


def layer_norm(values, gain, bias):
    mean = jnp.mean(values, -1, keepdims=True)
    var = jnp.mean(jnp.square(values - mean), -1, keepdims=True)
    return (values - mean) * lax.rsqrt(var + 1e-05) * gain + bias


def hidden_norm(mixed, gain, bias):
    width_all = mixed.shape[0] * lax.axis_size("ch")
    first_sum, second_sum = (
        lax.psum(jnp.sum(mixed, 0).astype(jnp.bfloat16), "ch").astype(jnp.float32),
        lax.psum(jnp.sum(mixed * mixed, 0).astype(jnp.bfloat16), "ch").astype(jnp.float32),
    )
    mean = (first_sum / width_all)[None]
    var = (second_sum / width_all)[None] - mean * mean
    return (
        (mixed - mean) * lax.rsqrt(var + 1e-05) * gain[:, None, None] + bias[:, None, None]
    ).astype(jnp.bfloat16)


def outgoing(left, right):
    return jnp.einsum(
        "cik,cjk->cij",
        left,
        lax.all_gather(right, "row", axis=1, tiled=True),
        preferred_element_type=jnp.float32,
    )


def incoming(left, right):
    summed = lax.psum_scatter(
        jnp.einsum("cki,ckj->icj", left, right, preferred_element_type=jnp.float32).astype(
            jnp.bfloat16
        ),
        "row",
        scatter_dimension=0,
        tiled=True,
    ).astype(jnp.float32)
    return jnp.transpose(summed, (1, 0, 2))


def on_device(pair, mask, in_gain, in_bias, w_proj, w_gate, out_gain, out_bias, w_out):
    rows, width, chans = pair.shape
    first_row = lax.axis_index("row") * rows
    mask_f = mask.astype(jnp.float32)
    row_mask = lax.dynamic_slice_in_dim(mask_f, first_row, rows)
    pair_mask = (row_mask[:, None] * mask_f[None, :])[None]
    state = pair
    for layer in range(2):
        normed = layer_norm(state, in_gain[layer], in_bias[layer]).astype(jnp.bfloat16)
        flat = normed.reshape(rows * width, chans)
        proj = jnp.einsum(
            "ctd,rqc->tdrq", w_proj[layer], normed, preferred_element_type=jnp.float32
        )
        left = (jax.nn.sigmoid(proj[0]) * proj[1] * pair_mask).astype(jnp.bfloat16)
        right = (jax.nn.sigmoid(proj[2]) * proj[3] * pair_mask).astype(jnp.bfloat16)
        if layer == 0:
            mixed = outgoing(left, right)
        else:
            mixed = incoming(left, right)
        hidden = hidden_norm(mixed, out_gain[layer], out_bias[layer])
        partial_value = jnp.einsum(
            "hrq,hc->rqc", hidden, w_out[layer], preferred_element_type=jnp.float32
        )
        change = lax.psum(partial_value, "ch")
        gate = jax.nn.sigmoid(jnp.dot(flat, w_gate[layer], preferred_element_type=jnp.float32))
        state = state + gate.reshape(rows, width, chans) * change
    return state


def solution(mesh):
    placed = (
        P("row", None, None),
        P(),
        P(),
        P(),
        P(None, None, None, "ch"),
        P(),
        P(None, "ch"),
        P(None, "ch"),
        P(None, "ch", None),
    )
    return jax.shard_map(
        on_device, mesh=mesh, in_specs=placed, out_specs=P("row", None, None), check_vma=False
    )
```

profile of v0, /device:TPU:0, one launch (start us, length us, event | category | flops | bytes accessed | tf_op | source)
XLA Modules:
  0.0 517.0 jit_solution(16454102780691256804)
XLA Ops:
  6.5 3.4 reduce_sum.72
  9.9 4.0 multiply_reduce_fusion.1
  14.0 0.1 dynamic_slice.3
  14.0 0.1 broadcast_multiply_fusion
  14.1 4.4 add_convert_fusion.1
  18.6 0.7 convolution_bitcast_fusion.1
  19.3 1.6 fusion.38
  21.0 0.0 all-reduce.5.cloned.1.call-start
  21.1 75.1 %all-gather.2.cloned.1.call-done = bf16[32,512,512]{2,0,1:T(8,128)(2,1)} async-done(((bf16[32,16,512]{2,0,1:T(8,128)(2,1)}), bf16[32,512,512]{2,0,1:T(8,128)(2,1)}) %all-gather.2.cloned.1.call-update) | async-done | bytes 16777232 | tf_op jit(solution)/shard_map/all_gather | solution.py:30
  96.2 17.6 %fusion.67 = (bf16[16,512]{1,0:T(8,128)(2,1)S(1)}, bf16[16,512]{1,0:T(8,128)(2,1)S(1)}, f32[32,16,512]{2,1,0:T(8,128)S(1)}) fusion(bf16[32,512,512]{2,0,1:T(8,128)(2,1)} %all-gather.2.cloned.1.call-done, bf16[32,16,512]{2,0,1:T(8,128)(2,1)} %get-tuple-element.15), kind=kOutput, calls=%fused_computation.107 | convolution fusion | flops 269205504 | bytes 18382848 | tf_op jit(solution)/shard_map/cik,cjk->cij/dot_general | solution.py:27
  113.8 17.0 %all-reduce.1 = (bf16[16,512]{1,0:T(8,128)(2,1)S(1)}, bf16[16,512]{1,0:T(8,128)(2,1)S(1)}) all-reduce(bf16[16,512]{1,0:T(8,128)(2,1)S(1)} %get-tuple-element.6, bf16[16,512]{1,0:T(8,128)(2,1)S(1)} %get-tuple-element.5), channel_id=1, replica_groups=mesh['row'=32,'ch'=4] {'ch'}, use_global_device_ids=true, to_apply=%region_5.0 | all-reduce | flops 16384 | bytes 65536 | tf_op jit(solution)/shard_map/psum | solution.py:17
  130.9 0.2 add_convert_fusion.2
  131.1 2.8 fusion.48
  133.9 0.0 reduce-scatter.2.cloned.1.call-start
  134.0 3.3 fusion.6
  137.2 87.5 %all-reduce.5.cloned.1.call-done = f32[16,512,128]{2,1,0:T(8,128)} async-done(((f32[16,512,128]{2,1,0:T(8,128)}), f32[16,512,128]{2,1,0:T(8,128)}) %all-reduce.5.cloned.1.call-update) | async-done | bytes 4194320 | tf_op jit(solution)/shard_map/psum | solution.py:70
  224.7 6.0 %fusion.68 = (f32[16,512]{1,0:T(8,128)S(1)}, f32[16,512,128]{2,1,0:T(8,128)S(1)}) fusion(f32[16,512,128]{2,1,0:T(8,128)} %param.9, f32[16,512,128]{2,1,0:T(8,128)} %bitcast.133, f32[16,512,128]{2,1,0:T(8,128)} %all-reduce.5.cloned.1.call-done), kind=kLoop, calls=%fused_computation.108 | loop fusion | flops 3137536 | bytes 16809984 | tf_op jit(solution)/shard_map/reduce_sum | solution.py:8
  230.7 2.4 multiply_reduce_fusion
  233.1 2.5 add_convert_fusion
  235.7 0.7 convolution_bitcast_fusion
  236.4 0.7 fusion.23
  237.0 8.1 %convert_bitcast_fusion = bf16[512,32,512]{0,2,1:T(8,128)(2,1)} fusion(bf16[32,16,512]{2,0,1:T(8,128)(2,1)S(1)} %get-tuple-element.14, bf16[32,16,512]{2,0,1:T(8,128)(2,1)S(1)} %get-tuple-element.13), kind=kOutput, calls=%fused_computation.2 | convolution fusion | flops 276824064 | bytes 17825792 | tf_op jit(solution)/shard_map/cki,ckj->icj/dot_general | solution.py:37
  245.2 28.6 %copy.54 = bf16[512,32,512]{2,1,0:T(8,128)(2,1)} copy(bf16[512,32,512]{0,2,1:T(8,128)(2,1)} %convert_bitcast_fusion) | data formatting | bytes 33554432 | tf_op jit(solution)/shard_map/convert_element_type | solution.py:37
  273.8 0.0 all-reduce.7.cloned.1.call-start
  273.9 115.3 %reduce-scatter.2.cloned.1.call-done = bf16[16,32,512]{2,1,0:T(8,128)(2,1)} async-done(((bf16[512,32,512]{2,1,0:T(8,128)(2,1)}), bf16[16,32,512]{2,1,0:T(8,128)(2,1)}) %reduce-scatter.2.cloned.1.call-update) | async-done | bytes 524304 | tf_op jit(solution)/shard_map/reduce_scatter | solution.py:36
  389.2 1.2 bitcast_reduce_fusion
  390.3 1.2 fusion.10
  391.5 17.0 %all-reduce = (bf16[16,512]{1,0:T(8,128)(2,1)S(1)}, bf16[16,512]{1,0:T(8,128)(2,1)S(1)}) all-reduce(bf16[16,512]{1,0:T(8,128)(2,1)S(1)} %fusion.10, bf16[16,512]{1,0:T(8,128)(2,1)S(1)} %bitcast_reduce_fusion), channel_id=1, replica_groups=mesh['row'=32,'ch'=4] {'ch'}, use_global_device_ids=true, to_apply=%region_13.0 | all-reduce | flops 16384 | bytes 65536 | tf_op jit(solution)/shard_map/psum | solution.py:17
  408.6 3.8 fusion.43
  412.5 3.2 fusion.7
  415.7 87.4 %all-reduce.7.cloned.1.call-done = f32[16,512,128]{2,1,0:T(8,128)} async-done(((f32[16,512,128]{2,1,0:T(8,128)}), f32[16,512,128]{2,1,0:T(8,128)}) %all-reduce.7.cloned.1.call-update) | async-done | bytes 4194320 | tf_op jit(solution)/shard_map/psum | solution.py:70
  503.1 7.4 %multiply_add_fusion = f32[16,512,128]{2,1,0:T(8,128)} fusion(f32[16,512,128]{2,1,0:T(8,128)} %copy-done, f32[16,512,128]{2,1,0:T(8,128)} %bitcast.134, f32[16,512,128]{2,1,0:T(8,128)} %all-reduce.7.cloned.1.call-done), kind=kLoop, calls=%fused_computation.11 | loop fusion | flops 2097152 | bytes 16777216 | tf_op jit(solution)/shard_map/add | solution.py:72
  (32 shorter events, 0.2 us)
Async XLA Ops:
  6.5 89.7 %all-gather.2.cloned.1.call-start = ((), (), s32[]{:S(2)}) async-start(), calls=%async_computation.1 | async-start | bytes 17301504 | tf_op jit(solution)/shard_map/all_gather | solution.py:30
  6.5 7.4 %copy-start.3 = (s32[512]{0:T(512)S(1)}, s32[512]{0:T(512)}, u32[]{:S(2)}) copy-start(s32[512]{0:T(512)} %param.10) | copy-start | bytes 6148
  6.5 7.6 %copy-start.4 = (f32[2,128]{1,0:T(2,128)S(1)}, f32[2,128]{1,0:T(2,128)}, u32[]{:S(2)}) copy-start(f32[2,128]{1,0:T(2,128)} %param.12) | copy-start | bytes 3076
  6.5 7.6 %copy-start.5 = (f32[2,128]{1,0:T(2,128)S(1)}, f32[2,128]{1,0:T(2,128)}, u32[]{:S(2)}) copy-start(f32[2,128]{1,0:T(2,128)} %param.11) | copy-start | bytes 3076
  13.9 4.7 copy-start.1
  19.3 1.7 copy-start.6
  19.3 1.7 copy-start.7
  21.0 203.7 %all-reduce.5.cloned.1.call-start = ((), (), s32[]{:S(2)}) async-start(), calls=%async_computation.2 | async-start | bytes 8388608 | tf_op jit(solution)/shard_map/psum | solution.py:70
  96.2 34.9 %copy-start.2 = (bf16[2,32,128]{2,1,0:T(8,128)(2,1)S(1)}, bf16[2,32,128]{2,1,0:T(8,128)(2,1)}, u32[]{:S(2)}) copy-start(bf16[2,32,128]{2,1,0:T(8,128)(2,1)} %param.17) | copy-start | bytes 49156
  131.1 2.9 copy-start.8
  133.9 255.3 %reduce-scatter.2.cloned.1.call-start = ((), (), s32[]{:S(2)}) async-start(), calls=%async_computation.3 | async-start | bytes 17301504 | tf_op jit(solution)/shard_map/reduce_scatter | solution.py:36
  230.7 5.0 copy-start
  273.8 229.3 %all-reduce.7.cloned.1.call-start = ((), (), s32[]{:S(2)}) async-start(), calls=%async_computation.4 | async-start | bytes 8388608 | tf_op jit(solution)/shard_map/psum | solution.py:70
Sparse Core Ops, SparseCore 0:
  21.1 75.0 all-gather.1
  134.0 90.6 all-reduce.4
  273.9 115.1 reduce-scatter.1
  412.6 90.4 all-reduce.6
where the time goes:
time: 519 us; the launch traced here: 517 us
  waiting for transfers between devices  365 us (70%)
  matrix products  40.2 us (8%)
  other arithmetic  35.1 us (7%)
  blocking collectives  34.1 us (7%)
  local copies, waits for them, and re-layouts  28.8 us (6%)
  between operations  13.4 us (3%)
    psum x2, waiting for transfers between devices, on_device(): change = lax.psum(partial_value, 'ch')  175 us
    reduce_scatter x1, waiting for transfers between devices, incoming(): lax.psum_scatter(jnp.einsum('cki,ckj->icj', left, right, preferred_elemen...  115 us
    all_gather x1, waiting for transfers between devices, outgoing(): lax.all_gather(right, 'row', axis=1, tiled=True)  75.1 us
    psum x2, blocking collectives, hidden_norm(): lax.psum(jnp.sum(mixed * mixed, 0).astype(jnp.bfloat16), 'ch')  34.1 us
    convert_element_type x1, local copies, waits for them, and re-layouts, incoming(): jnp.einsum('cki,ckj->icj', left, right, preferred_element_type=jnp.float32)  28.6 us
    dot_general x1, matrix products, outgoing(): jnp.einsum('cik,cjk->cij', left, lax.all_gather(right, 'row', axis=1, til...  17.6 us
  transfers between devices with their start and end apart: 4, of which 4 were waited for; matrix products, arithmetic and copies ran while one was open for 1% of the time, Pallas kernels for 0%

commit v1 on v0

v1 whole, which is shorter than its diff:
```python
import functools

import jax
import jax.numpy as jnp
from jax import lax
from jax.experimental import pallas as pl
from jax.experimental.pallas import tpu as pltpu
from jax.sharding import PartitionSpec as P

F32, BF16 = jnp.float32, jnp.bfloat16
N, C, T = 512, 128, 128
RB = 16
G, R = 4, 32
D = C // G
VMEM_LIMIT = 32 * 1024 * 1024

PK_PROJ, PK_OUT, PK_NORM, PK = 0, 128, 192, 224


def dot(a, b, ca=1, cb=0):
    return lax.dot_general(a, b, (((ca,), (cb,)), ((), ())), preferred_element_type=F32)


def column(row):
    return jnp.broadcast_to(row, (C, C)).T


def norm_cols(v, gain, bias):
    mean = jnp.mean(v, 0, keepdims=True)
    cent = v - mean
    var = jnp.mean(cent * cent, 0, keepdims=True)
    return cent * lax.rsqrt(var + 1e-05) * gain + bias


def sigmoid(v):
    return 0.5 * jnp.tanh(0.5 * v) + 0.5


def gated(gate, value, half_mask):
    return (jnp.tanh(0.5 * gate) + 1.0) * (value * half_mask)


def project0_kernel(ids, mask_s, pair, mask_v, in_gain, in_bias, w, out, left_s, right_s):
    gain, bias = column(in_gain[0:1, :]), column(in_bias[0:1, :])
    cols = mask_v[...] * 0.5
    row0 = ids[0] * RB
    for i in range(RB):
        zn = norm_cols(pair[i].T, gain, bias).astype(BF16)
        proj = dot(w[...], zn)
        half = cols * mask_s[row0 + i].astype(F32)
        left_s[pl.ds(i, D, stride=RB), :] = gated(proj[0:D], proj[D : 2 * D], half)
        right_s[pl.ds(i, D, stride=RB), :] = gated(proj[2 * D : 3 * D], proj[3 * D :], half)
    out[:, 0] = left_s[...].reshape(D, RB, T).astype(BF16)
    out[:, 1] = right_s[...].reshape(D, RB, T).astype(BF16)


def outgoing_kernel(a, out):
    left = a[:, 0].reshape(N, N)
    for h in range(G):
        right = a[8 * h : 8 * h + 8, 1].reshape(T, N)
        out[h] = dot(left, right, 1, 1).reshape(R, RB, T).astype(BF16)


def incoming_kernel(b, out):
    left = jnp.concatenate([b[R * h : R * h + R, 0].reshape(N, T) for h in range(G)], 1)
    for h in range(G):
        right = b[R * h : R * h + R, 1].reshape(N, T)
        out[h] = dot(left, right, 0, 0).reshape(R, RB, T).astype(BF16)


def norm_params(pk, layer):
    parts = jnp.concatenate([pk[g, PK_NORM : PK_NORM + D] for g in range(G)], 0).astype(F32)
    k = 2 * layer
    cols = [parts[:, k + j : k + j + 1] + parts[:, 4 + k + j : 5 + k + j] + parts[:, 8 + k + j : 9 + k + j] for j in (0, 1)]
    w_out = jnp.concatenate(
        [pk[g, PK_OUT + D * layer : PK_OUT + D * (layer + 1)] for g in range(G)], 0
    )
    return cols[0], cols[1], w_out.astype(F32).T.astype(BF16)


def middle_kernel(
    ids, mask_s, y, pair, mask_v, in_gain, in_bias, w_gate, pk, state, normed, out, ys, left_s, right_s
):
    gain0, bias0 = column(in_gain[0:1, :]), column(in_bias[0:1, :])
    gain1, bias1 = column(in_gain[1:2, :]), column(in_bias[1:2, :])
    og, ob, w_out = norm_params(pk, 0)
    og, ob = jnp.broadcast_to(og, (C, T)), jnp.broadcast_to(ob, (C, T))
    w_g = w_gate[0].astype(F32).T.astype(BF16)
    cols = mask_v[...] * 0.5
    row0 = ids[0] * RB
    ys[...] = y[...].astype(F32).reshape(C * RB, T)
    for i in range(RB):
        hidden = norm_cols(ys[pl.ds(i, C, stride=RB), :], og, ob).astype(BF16)
        z = pair[i].T
        gate = sigmoid(dot(w_g, norm_cols(z, gain0, bias0).astype(BF16)))
        z = z + gate * dot(w_out, hidden)
        state[i] = z
        zn = norm_cols(z, gain1, bias1).astype(BF16)
        normed[i] = zn
        half = cols * mask_s[row0 + i].astype(F32)
        for g in range(G):
            proj = dot(pk[g, PK_PROJ : PK_PROJ + C], zn)
            at = pl.ds(i + g * D * RB, D, stride=RB)
            left_s[at, :] = gated(proj[0:D], proj[D : 2 * D], half)
            right_s[at, :] = gated(proj[2 * D : 3 * D], proj[3 * D :], half)
    out[:, 0] = left_s[...].reshape(C, RB, T).astype(BF16)
    out[:, 1] = right_s[...].reshape(C, RB, T).astype(BF16)


def last_kernel(y, state, normed, w_gate, pk, out, ys):
    og, ob, w_out = norm_params(pk, 1)
    og, ob = jnp.broadcast_to(og, (C, T)), jnp.broadcast_to(ob, (C, T))
    w_g = w_gate[1].astype(F32).T.astype(BF16)
    ys[...] = y[...].astype(F32).reshape(C * RB, T)
    for i in range(RB):
        hidden = norm_cols(ys[pl.ds(i, C, stride=RB), :], og, ob).astype(BF16)
        gate = sigmoid(dot(w_g, normed[i]))
        z = state[i] + gate * dot(w_out, hidden)
        out[i] = z.T.astype(BF16)


def spread_kernel(ids, own, up0, up1, down0, down1, far0, far1, out):
    step = pl.program_id(0)

    @pl.when(step == 0)
    def _():
        out[...] = own[...].astype(F32)

    @pl.when(step == 1)
    def _():
        out[0:8] = down0[...].astype(F32)
        out[8:16] = down1[...].astype(F32)

    @pl.when(step == 2)
    def _():
        out[0:8] = far0[...].astype(F32)
        out[8:16] = far1[...].astype(F32)

    @pl.when(step == 3)
    def _():
        out[0:8] = up0[...].astype(F32)
        out[8:16] = up1[...].astype(F32)


def params(**kw):
    return pltpu.CompilerParams(vmem_limit_bytes=VMEM_LIMIT, **kw)


def whole(shape):
    return pl.BlockSpec(shape, lambda *_: (0,) * len(shape))


def on_device(pair, mask, in_gain, in_bias, w_proj, w_gate, out_gain, out_bias, w_out):
    ids = jnp.stack([lax.axis_index("row"), lax.axis_index("ch")]).astype(jnp.int32)
    mask_v = mask.astype(F32)[None]
    w_t = jnp.transpose(w_proj, (0, 2, 3, 1)).reshape(2, 4 * D, C)

    nrm = jnp.stack([out_gain[0], out_bias[0], out_gain[1], out_bias[1]], 1)
    hi = nrm.astype(BF16)
    mid = (nrm - hi.astype(F32)).astype(BF16)
    low = (nrm - hi.astype(F32) - mid.astype(F32)).astype(BF16)
    nrm = jnp.pad(jnp.concatenate([hi, mid, low], 1), ((0, 0), (0, C - 12)))
    own = jnp.concatenate([w_t[1], w_out.reshape(2 * D, C), nrm], 0)
    pk = lax.all_gather(own, "ch", axis=0)

    a = pl.pallas_call(
        project0_kernel,
        out_shape=jax.ShapeDtypeStruct((D, 2, RB, N), BF16),
        grid_spec=pltpu.PrefetchScalarGridSpec(
            num_scalar_prefetch=2,
            grid=(G,),
            in_specs=[
                pl.BlockSpec((RB, T, C), lambda j, *_: (0, j, 0)),
                pl.BlockSpec((1, T), lambda j, *_: (0, j)),
                whole((2, C)),
                whole((2, C)),
                whole((4 * D, C)),
            ],
            out_specs=pl.BlockSpec((D, 2, RB, T), lambda j, *_: (0, 0, 0, j)),
            scratch_shapes=[pltpu.VMEM((D * RB, T), F32)] * 2,
        ),
        compiler_params=params(),
        name="project0",
    )(ids, mask, pair, mask_v, in_gain, in_bias, w_t[0])
    a = lax.all_to_all(a, "row", 0, 0)
    x = pl.pallas_call(
        outgoing_kernel,
        out_shape=jax.ShapeDtypeStruct((G, R, RB, T), BF16),
        compiler_params=params(),
        name="outgoing",
    )(a)
    y = lax.all_to_all(x.reshape(G * R, RB, T), ("ch", "row"), 0, 0)
    state, normed, b = pl.pallas_call(
        middle_kernel,
        out_shape=(
            jax.ShapeDtypeStruct((RB, C, T), F32),
            jax.ShapeDtypeStruct((RB, C, T), BF16),
            jax.ShapeDtypeStruct((C, 2, RB, T), BF16),
        ),
        grid_spec=pltpu.PrefetchScalarGridSpec(
            num_scalar_prefetch=2,
            grid=(1,),
            in_specs=[
                whole((C, RB, T)),
                pl.BlockSpec((RB, T, C), lambda j, ids, _: (0, ids[1], 0)),
                pl.BlockSpec((1, T), lambda j, ids, _: (0, ids[1])),
                whole((2, C)),
                whole((2, C)),
                whole((2, C, C)),
                whole((G, PK, C)),
            ],
            out_specs=(whole((RB, C, T)), whole((RB, C, T)), whole((C, 2, RB, T))),
            scratch_shapes=[pltpu.VMEM((C * RB, T), F32)] * 3,
        ),
        compiler_params=params(),
        name="middle",
    )(ids, mask, y, pair, mask_v, in_gain, in_bias, w_gate, pk)
    b = lax.all_to_all(b, ("ch", "row"), 0, 0)
    x = pl.pallas_call(
        incoming_kernel,
        out_shape=jax.ShapeDtypeStruct((G, R, RB, T), BF16),
        compiler_params=params(),
        name="incoming",
    )(b)
    y = lax.all_to_all(x.reshape(G * R, RB, T), ("ch", "row"), 0, 0)
    z = pl.pallas_call(
        last_kernel,
        out_shape=jax.ShapeDtypeStruct((RB, T, C), BF16),
        scratch_shapes=[pltpu.VMEM((C * RB, T), F32)],
        compiler_params=params(),
        name="last",
    )(y, state, normed, w_gate, pk)

    up = functools.partial(lax.ppermute, axis_name="ch", perm=[(k, (k + 1) % G) for k in range(G)])
    down = functools.partial(lax.ppermute, axis_name="ch", perm=[(k, (k - 1) % G) for k in range(G)])
    z0, z1 = z[:8], z[8:]
    up0, down1 = up(z0), down(z1)
    up1, down0 = up(z1), down(z0)
    far0, far1 = up(up0), down(down1)
    half = whole((RB // 2, T, C))
    return pl.pallas_call(
        spread_kernel,
        out_shape=jax.ShapeDtypeStruct((RB, N, C), F32),
        grid_spec=pltpu.PrefetchScalarGridSpec(
            num_scalar_prefetch=1,
            grid=(G,),
            in_specs=[whole((RB, T, C))] + [half] * 6,
            out_specs=pl.BlockSpec((RB, T, C), lambda s, ids: (0, lax.rem(ids[1] + s, G), 0)),
        ),
        compiler_params=params(),
        name="spread",
    )(ids, z, up0, up1, down0, down1, far0, far1)


def solution(mesh):
    placed = (
        P("row", None, None),
        P(),
        P(),
        P(),
        P(None, None, None, "ch"),
        P(),
        P(None, "ch"),
        P(None, "ch"),
        P(None, "ch", None),
    )
    return jax.shard_map(
        on_device, mesh=mesh, in_specs=placed, out_specs=P("row", None, None), check_vma=False
    )
```

time: 519 us -> 140 us (0.27)
  waiting for transfers between devices: 365 us -> 30.5 us
  matrix products: 40.2 us -> 0 us
  other arithmetic: 35.1 us -> 0.83 us
  blocking collectives: 34.1 us -> 60.7 us
  starting transfers between devices: 0.13 us -> 22.4 us
  local copies, waits for them, and re-layouts: 28.8 us -> 7.36 us
  Pallas kernels: 0 us -> 17 us
  between operations: 13.4 us -> 0.15 us
    psum x2 -> x0, waiting for transfers between devices: 175 us -> none  [on_device(): change = lax.psum(partial_value, 'ch')]
    reduce_scatter x1 -> x0, waiting for transfers between devices: 115 us -> none  [incoming(): lax.psum_scatter(jnp.einsum('cki,ckj->icj', left, right, preferred_elemen...]
    all_gather x1 -> x0, waiting for transfers between devices: 75.1 us -> none  [outgoing(): lax.all_gather(right, 'row', axis=1, tiled=True)]
    all_to_all x0 -> x2, blocking collectives: none -> 45.7 us  [the longest x1 27.8 us: on_device(): b = lax.all_to_all(b, ('ch', 'row'), 0, 0)]
    dot_general x8 -> x0, matrix products: 40.2 us -> none  [the longest x1 17.6 us: outgoing(): jnp.einsum('cik,cjk->cij', left, lax.all_gather(right, 'row', axis=1, til...]
    psum x2 -> x0, blocking collectives: 34.1 us -> none  [hidden_norm(): lax.psum(jnp.sum(mixed * mixed, 0).astype(jnp.bfloat16), 'ch')]
    convert_element_type x1 -> x0, local copies, waits for them, and re-layouts: 28.6 us -> none  [incoming(): jnp.einsum('cki,ckj->icj', left, right, preferred_element_type=jnp.float32)]
    reduce_sum x6 -> x0, other arithmetic: 18.1 us -> none  [the longest x2 9.38 us: layer_norm(): mean = jnp.mean(values, -1, keepdims=True)]
  transfers between devices with their start and end apart: 4 -> 8, of which waited for: 4 -> 5; matrix products, arithmetic and copies ran while one was open for 1% -> 0% of each run, Pallas kernels for 0% -> 0%
where the time goes in v1:
time: 140 us; the launch traced here: 139 us
  blocking collectives  60.7 us (43%)
  waiting for transfers between devices  30.5 us (22%)
  starting transfers between devices  22.4 us (16%)
  Pallas kernels  17 us (12%)
  local copies, waits for them, and re-layouts  7.36 us (5%)
    all_to_all x1, blocking collectives, on_device(): b = lax.all_to_all(b, ('ch', 'row'), 0, 0)  27.8 us
    all_to_all x1, blocking collectives, on_device(): y = lax.all_to_all(x.reshape(G * R, RB, T), ('ch', 'row'), 0, 0)  18 us
    all_to_all x1, waiting for transfers between devices, on_device(): a = lax.all_to_all(a, 'row', 0, 0)  17.3 us
    all_gather x1, blocking collectives, on_device(): pk = lax.all_gather(own, 'ch', axis=0)  15 us
    all_to_all x1, starting transfers between devices, on_device(): a = lax.all_to_all(a, 'row', 0, 0)  8.42 us
    unnamed x25, local copies, waits for them, and re-layouts  6.53 us
    all_to_all x1, starting transfers between devices, on_device(): y = lax.all_to_all(x.reshape(G * R, RB, T), ('ch', 'row'), 0, 0)  6.29 us
    pallas_call x1, Pallas kernels, on_device(): pl.pallas_call(middle_kernel, out_shape=(jax.ShapeDtypeStruct((RB, C, T),...  5.77 us
  transfers between devices with their start and end apart: 8, of which 5 were waited for; matrix products, arithmetic and copies ran while one was open for 0% of the time, Pallas kernels for 0%

profile of v1, /device:TPU:0, one launch (start us, length us, event | category | flops | bytes accessed | tf_op | source)
XLA Modules:
  0.0 139.1 jit_solution(5712776530391936425)
XLA Ops:
  0.0 0.7 convert_element_type.21
  0.7 0.8 fusion.5
  1.5 0.1 pad_add_fusion.ids
  1.6 2.2 %copy-done = f32[16,512,128]{2,1,0:T(8,128)S(1)} copy-done((f32[16,512,128]{2,1,0:T(8,128)S(1)}, f32[16,512,128]{2,1,0:T(8,128)}, u32[]{:S(2)}) %copy-start) | copy-done | bytes 4194328
  3.8 0.7 copy-done.3
  4.4 0.7 copy-done.5
  5.1 0.7 copy-done.7
  5.8 4.8 %project0.1 = bf16[32,2,16,512]{3,2,1,0:T(8,128)(2,1)} custom-call(s32[2]{0:T(128)S(1)} %pad_add_fusion.ids, s32[512]{0:T(512)S(1)} %copy-done.3, f32[16,512,128]{2,1,0:T(8,128)S(1)} %copy-done, f32[1,512]{1,0:T(1,128)S(1)} %bitcast.22, f32[2,128]{1,0:T(2,128)S(1)} %copy-done.5, f32[2,128]{1,0:T(2,128)S(1)} %copy-done.7, bf16[128,128]{1,0:T(8,128)(2,1)S(1)} %bitcast.21), custom_call_target="tpu_custom_call" | custom-call | tf_op jit(solution)/shard_map/project0/pallas_call | solution.py:166
  10.6 8.4 %all-to-all-start = ((bf16[32,2,16,512]{3,2,1,0:T(8,128)(2,1)}), bf16[32,2,16,512]{3,2,1,0:T(8,128)(2,1)S(1)}, u32[]{:S(2)}, u32[]{:S(2)}) async-start(bf16[32,2,16,512]{3,2,1,0:T(8,128)(2,1)} %project0.1), calls=%async_computation | async-start | bytes 2097152 | tf_op jit(solution)/shard_map/all_to_all | solution.py:185
  19.1 17.3 %all-to-all-done.a = bf16[32,2,16,512]{3,2,1,0:T(8,128)(2,1)S(1)} async-done(((bf16[32,2,16,512]{3,2,1,0:T(8,128)(2,1)}), bf16[32,2,16,512]{3,2,1,0:T(8,128)(2,1)S(1)}, u32[]{:S(2)}, u32[]{:S(2)}) %all-to-all-start) | async-done | bytes 1048608 | tf_op jit(solution)/shard_map/all_to_all | solution.py:185
  36.4 1.5 %outgoing.1 = bf16[4,32,16,128]{3,2,1,0:T(8,128)(2,1)} custom-call(bf16[32,2,16,512]{3,2,1,0:T(8,128)(2,1)S(1)} %all-to-all-done.a), custom_call_target="tpu_custom_call" | custom-call | tf_op jit(solution)/shard_map/outgoing/pallas_call | solution.py:186
  37.9 6.3 %all-to-all-start.1 = ((bf16[128,16,128]{2,1,0:T(8,128)(2,1)}), bf16[128,16,128]{2,1,0:T(8,128)(2,1)S(1)}, u32[]{:S(2)}, u32[]{:S(2)}) async-start(bf16[128,16,128]{2,1,0:T(8,128)(2,1)} %bitcast.5), calls=%async_computation.1 | async-start | bytes 1048576 | tf_op jit(solution)/shard_map/all_to_all | solution.py:192
  44.2 0.1 copy.11
  44.4 15.0 %all-gather = bf16[896,128]{1,0:T(8,128)(2,1)S(1)} all-gather(bf16[224,128]{1,0:T(8,128)(2,1)S(1)} %fusion.1), channel_id=2, replica_groups=mesh['row'=32,'ch'=4] {'ch'}, dimensions={0}, use_global_device_ids=true | all-gather | bytes 286720 | tf_op jit(solution)/shard_map/all_gather | solution.py:164
  59.4 0.0 copy-start.1
  59.4 2.2 %copy-done.1 = f32[16,512,128]{2,1,0:T(8,128)S(1)} copy-done((f32[16,512,128]{2,1,0:T(8,128)S(1)}, f32[16,512,128]{2,1,0:T(8,128)}, u32[]{:S(2)}) %copy-start.1) | copy-done | bytes 4194328
  61.6 5.8 %middle.1 = (f32[16,128,128]{2,1,0:T(8,128)S(1)}, bf16[16,128,128]{2,1,0:T(8,128)(2,1)S(1)}, bf16[128,2,16,128]{3,2,1,0:T(8,128)(2,1)S(1)}) custom-call(s32[2]{0:T(128)S(1)} %pad_add_fusion.ids, s32[512]{0:T(512)S(1)} %copy-done.4, bf16[128,16,128]{2,1,0:T(8,128)(2,1)S(1)} %all-to-all-done.1.y, f32[16,512,128]{2,1,0:T(8,128)S(1)} %copy-done.1, ...), custom_call_target="tpu_custom_call" | custom-call | tf_op jit(solution)/shard_map/middle/pallas_call | solution.py:193
  67.4 27.8 %all_to_all.20.b = bf16[128,2,16,128]{3,2,1,0:T(8,128)(2,1)S(1)} all-to-all(bf16[128,2,16,128]{3,2,1,0:T(8,128)(2,1)S(1)} %get-tuple-element.8), channel_id=1, replica_groups=mesh['row'=32,'ch'=4] {'ch','row'}, dimensions={0} | all-to-all | bytes 2097152 | tf_op jit(solution)/shard_map/all_to_all | solution.py:218
  95.2 0.7 incoming.1
  95.9 18.0 %all_to_all.21.y = bf16[128,16,128]{2,1,0:T(8,128)(2,1)S(1)} all-to-all(bf16[128,16,128]{2,1,0:T(8,128)(2,1)S(1)} %bitcast.18), channel_id=1, replica_groups=mesh['row'=32,'ch'=4] {'ch','row'}, dimensions={0} | all-to-all | bytes 1048576 | tf_op jit(solution)/shard_map/all_to_all | solution.py:225
  113.8 1.2 last.1.own
  115.1 1.2 collective-permute-start.3
  116.3 0.9 collective-permute-start
  117.2 0.6 collective-permute-start.1
  117.8 2.7 %collective-permute-start.2 = (bf16[8,128,128]{2,1,0:T(8,128)(2,1)S(1)}, bf16[8,128,128]{2,1,0:T(8,128)(2,1)S(1)}, u32[]{:S(2)}, u32[]{:S(2)}) collective-permute-start(bf16[8,128,128]{2,1,0:T(8,128)(2,1)S(1)} %get-tuple-element.12), channel_id=1, source_target_pairs={{0,3},{1,0},{2,1},{3,2},{4,7},{5,4},{6,5},{7,6},{8,11},{9,8},{10,9... | collective-permute-start | bytes 786440 | tf_op jit(solution)/shard_map/ppermute | solution.py:238
  120.4 4.0 %collective-permute-done.3.down1 = bf16[8,128,128]{2,1,0:T(8,128)(2,1)S(1)} collective-permute-done((bf16[8,128,128]{2,1,0:T(8,128)(2,1)S(1)}, bf16[8,128,128]{2,1,0:T(8,128)(2,1)S(1)}, u32[]{:S(2)}, u32[]{:S(2)}) %collective-permute-start.3) | collective-permute-done | bytes 262176 | tf_op jit(solution)/shard_map/ppermute | solution.py:237
  124.4 2.4 %collective-permute-start.5 = (bf16[8,128,128]{2,1,0:T(8,128)(2,1)S(1)}, bf16[8,128,128]{2,1,0:T(8,128)(2,1)S(1)}, u32[]{:S(2)}, u32[]{:S(2)}) collective-permute-start(bf16[8,128,128]{2,1,0:T(8,128)(2,1)S(1)} %collective-permute-done.3.down1), channel_id=1, source_target_pairs={{0,3},{1,0},{2,1},{3,2},{4,7},{5,4},{6,5},{7,6},{8,11},{9,8},{10,9... | collective-permute-start | bytes 786440 | tf_op jit(solution)/shard_map/ppermute | solution.py:239
  126.8 5.6 %collective-permute-done.1.up1 = bf16[8,128,128]{2,1,0:T(8,128)(2,1)S(1)} collective-permute-done((bf16[8,128,128]{2,1,0:T(8,128)(2,1)S(1)}, bf16[8,128,128]{2,1,0:T(8,128)(2,1)S(1)}, u32[]{:S(2)}, u32[]{:S(2)}) %collective-permute-start.1) | collective-permute-done | bytes 262176 | tf_op jit(solution)/shard_map/ppermute | solution.py:238
  132.4 0.0 collective-permute-done.2.down0
  132.4 1.6 %collective-permute-done.5.far1 = bf16[8,128,128]{2,1,0:T(8,128)(2,1)S(1)} collective-permute-done((bf16[8,128,128]{2,1,0:T(8,128)(2,1)S(1)}, bf16[8,128,128]{2,1,0:T(8,128)(2,1)S(1)}, u32[]{:S(2)}, u32[]{:S(2)}) %collective-permute-start.5) | collective-permute-done | bytes 262176 | tf_op jit(solution)/shard_map/ppermute | solution.py:239
  134.0 2.0 %collective-permute-done.4.far0 = bf16[8,128,128]{2,1,0:T(8,128)(2,1)S(1)} collective-permute-done((bf16[8,128,128]{2,1,0:T(8,128)(2,1)S(1)}, bf16[8,128,128]{2,1,0:T(8,128)(2,1)S(1)}, u32[]{:S(2)}, u32[]{:S(2)}) %collective-permute-start.4) | collective-permute-done | bytes 262176 | tf_op jit(solution)/shard_map/ppermute | solution.py:239
  136.0 3.0 %spread.1 = f32[16,512,128]{2,1,0:T(8,128)} custom-call(s32[2]{0:T(128)S(1)} %pad_add_fusion.ids, bf16[16,128,128]{2,1,0:T(8,128)(2,1)S(1)} %last.1.own, bf16[8,128,128]{2,1,0:T(8,128)(2,1)S(1)} %collective-permute-done.up0, bf16[8,128,128]{2,1,0:T(8,128)(2,1)S(1)} %collective-permute-done.1.up1, bf16[8,128,128]{2,1,0:T(8,128)(2,1)S(1)} %collective-permute-done.2.down0, ...), custom_call_target="tpu_custom_call" | custom-call | tf_op jit(solution)/shard_map/spread/pallas_call | solution.py:241
  (27 shorter events, 0.1 us)
Async XLA Ops:
  0.0 19.1 %copy-start.10 = (f32[2,32]{1,0:T(2,128)S(1)}, f32[2,32]{1,0:T(2,128)}, u32[]{:S(2)}) copy-start(f32[2,32]{1,0:T(2,128)} %param.16) | copy-start | bytes 772
  0.0 19.1 %copy-start.11 = (f32[2,32]{1,0:T(2,128)S(1)}, f32[2,32]{1,0:T(2,128)}, u32[]{:S(2)}) copy-start(f32[2,32]{1,0:T(2,128)} %param.15) | copy-start | bytes 772
  1.6 2.2 %copy-start = (f32[16,512,128]{2,1,0:T(8,128)S(1)}, f32[16,512,128]{2,1,0:T(8,128)}, u32[]{:S(2)}) copy-start(f32[16,512,128]{2,1,0:T(8,128)} %pair.3) | copy-start | bytes 12582916
  3.8 0.7 copy-start.3
  4.4 0.7 copy-start.5
  5.1 0.7 copy-start.7
  5.8 38.5 %copy-start.9 = (bf16[2,32,128]{2,1,0:T(8,128)(2,1)S(1)}, bf16[2,32,128]{2,1,0:T(8,128)(2,1)}, u32[]{:S(2)}) copy-start(bf16[2,32,128]{2,1,0:T(8,128)(2,1)} %param.17) | copy-start | bytes 49156
  5.8 53.6 %copy-start.2 = (bf16[2,128,128]{2,1,0:T(8,128)(2,1)S(1)}, bf16[2,128,128]{2,1,0:T(8,128)(2,1)}, u32[]{:S(2)}) copy-start(bf16[2,128,128]{2,1,0:T(8,128)(2,1)} %w_gate.3) | copy-start | bytes 196612
  5.8 53.6 %copy-start.4 = (s32[512]{0:T(512)S(1)}, s32[512]{0:T(512)}, u32[]{:S(2)}) copy-start(s32[512]{0:T(512)} %mask_s.3) | copy-start | bytes 6148
  5.8 53.6 %copy-start.6 = (f32[2,128]{1,0:T(2,128)S(1)}, f32[2,128]{1,0:T(2,128)}, u32[]{:S(2)}) copy-start(f32[2,128]{1,0:T(2,128)} %in_gain.3) | copy-start | bytes 3076
  5.8 53.6 %copy-start.8 = (f32[2,128]{1,0:T(2,128)S(1)}, f32[2,128]{1,0:T(2,128)}, u32[]{:S(2)}) copy-start(f32[2,128]{1,0:T(2,128)} %in_bias.3) | copy-start | bytes 3076
  10.6 25.8 %all-to-all-start = ((bf16[32,2,16,512]{3,2,1,0:T(8,128)(2,1)}), bf16[32,2,16,512]{3,2,1,0:T(8,128)(2,1)S(1)}, u32[]{:S(2)}, u32[]{:S(2)}) async-start(bf16[32,2,16,512]{3,2,1,0:T(8,128)(2,1)} %project0.1), calls=%async_computation | async-start | bytes 2097152 | tf_op jit(solution)/shard_map/all_to_all | solution.py:185
  37.9 21.5 %all-to-all-start.1 = ((bf16[128,16,128]{2,1,0:T(8,128)(2,1)}), bf16[128,16,128]{2,1,0:T(8,128)(2,1)S(1)}, u32[]{:S(2)}, u32[]{:S(2)}) async-start(bf16[128,16,128]{2,1,0:T(8,128)(2,1)} %bitcast.5), calls=%async_computation.1 | async-start | bytes 1048576 | tf_op jit(solution)/shard_map/all_to_all | solution.py:192
  59.4 2.2 %copy-start.1 = (f32[16,512,128]{2,1,0:T(8,128)S(1)}, f32[16,512,128]{2,1,0:T(8,128)}, u32[]{:S(2)}) copy-start(f32[16,512,128]{2,1,0:T(8,128)} %pair.3) | copy-start | bytes 12582916
  115.1 9.3 %collective-permute-start.3 = (bf16[8,128,128]{2,1,0:T(8,128)(2,1)S(1)}, bf16[8,128,128]{2,1,0:T(8,128)(2,1)S(1)}, u32[]{:S(2)}, u32[]{:S(2)}) collective-permute-start(bf16[8,128,128]{2,1,0:T(8,128)(2,1)S(1)} %get-tuple-element.11), channel_id=1, source_target_pairs={{0,3},{1,0},{2,1},{3,2},{4,7},{5,4},{6,5},{7,6},{8,11},{9,8},{10,9... | collective-permute-start | bytes 786440 | tf_op jit(solution)/shard_map/ppermute | solution.py:237
  116.3 10.5 %collective-permute-start = (bf16[8,128,128]{2,1,0:T(8,128)(2,1)S(1)}, bf16[8,128,128]{2,1,0:T(8,128)(2,1)S(1)}, u32[]{:S(2)}, u32[]{:S(2)}) collective-permute-start(bf16[8,128,128]{2,1,0:T(8,128)(2,1)S(1)} %get-tuple-element.12), channel_id=1, source_target_pairs={{0,1},{1,2},{2,3},{3,0},{4,5},{5,6},{6,7},{7,4},{8,9},{9,10},{10,1... | collective-permute-start | bytes 786440 | tf_op jit(solution)/shard_map/ppermute | solution.py:237
  117.2 15.2 %collective-permute-start.1 = (bf16[8,128,128]{2,1,0:T(8,128)(2,1)S(1)}, bf16[8,128,128]{2,1,0:T(8,128)(2,1)S(1)}, u32[]{:S(2)}, u32[]{:S(2)}) collective-permute-start(bf16[8,128,128]{2,1,0:T(8,128)(2,1)S(1)} %get-tuple-element.11), channel_id=1, source_target_pairs={{0,1},{1,2},{2,3},{3,0},{4,5},{5,6},{6,7},{7,4},{8,9},{9,10},{10,1... | collective-permute-start | bytes 786440 | tf_op jit(solution)/shard_map/ppermute | solution.py:238
  117.8 14.6 %collective-permute-start.2 = (bf16[8,128,128]{2,1,0:T(8,128)(2,1)S(1)}, bf16[8,128,128]{2,1,0:T(8,128)(2,1)S(1)}, u32[]{:S(2)}, u32[]{:S(2)}) collective-permute-start(bf16[8,128,128]{2,1,0:T(8,128)(2,1)S(1)} %get-tuple-element.12), channel_id=1, source_target_pairs={{0,3},{1,0},{2,1},{3,2},{4,7},{5,4},{6,5},{7,6},{8,11},{9,8},{10,9... | collective-permute-start | bytes 786440 | tf_op jit(solution)/shard_map/ppermute | solution.py:238
  124.4 9.6 %collective-permute-start.5 = (bf16[8,128,128]{2,1,0:T(8,128)(2,1)S(1)}, bf16[8,128,128]{2,1,0:T(8,128)(2,1)S(1)}, u32[]{:S(2)}, u32[]{:S(2)}) collective-permute-start(bf16[8,128,128]{2,1,0:T(8,128)(2,1)S(1)} %collective-permute-done.3.down1), channel_id=1, source_target_pairs={{0,3},{1,0},{2,1},{3,2},{4,7},{5,4},{6,5},{7,6},{8,11},{9,8},{10,9... | collective-permute-start | bytes 786440 | tf_op jit(solution)/shard_map/ppermute | solution.py:239
  126.8 9.3 %collective-permute-start.4 = (bf16[8,128,128]{2,1,0:T(8,128)(2,1)S(1)}, bf16[8,128,128]{2,1,0:T(8,128)(2,1)S(1)}, u32[]{:S(2)}, u32[]{:S(2)}) collective-permute-start(bf16[8,128,128]{2,1,0:T(8,128)(2,1)S(1)} %collective-permute-done.up0), channel_id=1, source_target_pairs={{0,1},{1,2},{2,3},{3,0},{4,5},{5,6},{6,7},{7,4},{8,9},{9,10},{10,1... | collective-permute-start | bytes 786440 | tf_op jit(solution)/shard_map/ppermute | solution.py:239

commit v2 on v0

v2 whole, which is shorter than its diff:
```python
import functools

import jax
import jax.numpy as jnp
from jax import lax
from jax.experimental import pallas as pl
from jax.experimental.pallas import tpu as pltpu
from jax.sharding import PartitionSpec as P

F32, BF16 = jnp.float32, jnp.bfloat16
N, C, T = 512, 128, 128
RB = 16
G, R = 4, 32
D = C // G
HB = RB // 2
HBM, VMEM = pltpu.HBM, pltpu.VMEM
VMEM_LIMIT = 32 * 1024 * 1024
WHOLE_VMEM = 60 * 1024 * 1024
MOST_VMEM = 51 * 1024 * 1024

PK_PROJ, PK_OUT, PK_NORM, PK = 0, 128, 192, 208


def dot(a, b, ca=1, cb=0):
    return lax.dot_general(a, b, (((ca,), (cb,)), ((), ())), preferred_element_type=F32)


def column(row):
    return jnp.broadcast_to(row, (C, C)).T


def norm_cols(v, gain, bias):
    mean = jnp.mean(v, 0, keepdims=True)
    cent = v - mean
    var = jnp.mean(cent * cent, 0, keepdims=True)
    return cent * lax.rsqrt(var + 1e-05) * gain + bias


def sigmoid(v):
    return 0.5 * jnp.tanh(0.5 * v) + 0.5


def gated(gate, value, half_mask):
    return (jnp.tanh(0.5 * gate) + 1.0) * (value * half_mask)


def project0_kernel(
    pair, mask, in_gain, in_bias, w, w_out, out_gain, out_bias, out, own,
    rows, mask_v, mask_s, gb, w_v, wo_v, og_v, left_s, right_s, sems,
):
    small = [
        (mask, mask_v),
        (mask, mask_s),
        (in_gain, gb.at[0]),
        (in_bias, gb.at[1]),
        (w, w_v),
        (w_out, wo_v),
        (out_gain, og_v.at[0]),
        (out_bias, og_v.at[1]),
    ]
    big = [(pair.at[i], rows.at[i]) for i in range(RB)]
    copies = [pltpu.make_async_copy(*ends, sems.at[k]) for k, ends in enumerate(small + big)]
    few = len(small)
    for copy in copies[few : few + 2] + copies[:few] + copies[few + 2 :]:
        copy.start()
    for copy in copies[:few]:
        copy.wait()
    gain, bias = column(gb[0, 0:1, :]), column(gb[1, 0:1, :])
    cols = mask_v[...].astype(F32) * 0.5
    row0 = lax.axis_index("row") * RB
    for i in range(RB):
        copies[few + i].wait()
        zn = jnp.concatenate(
            [norm_cols(rows[i, T * h : T * h + T].T, gain, bias).astype(BF16) for h in range(G)], 1
        )
        proj = dot(w_v[0], zn)
        half = cols * mask_s[0, row0 + i].astype(F32)
        left = gated(proj[0:D], proj[D : 2 * D], half)
        right = gated(proj[2 * D : 3 * D], proj[3 * D :], half)
        for h in range(G):
            left_s[h, pl.ds(i, D, stride=RB), :] = left[:, T * h : T * h + T]
            right_s[h, pl.ds(i, D, stride=RB), :] = right[:, T * h : T * h + T]
    for h in range(G):
        out[:, 0, :, T * h : T * h + T] = left_s[h].reshape(D, RB, T).astype(BF16)
        out[:, 1, :, T * h : T * h + T] = right_s[h].reshape(D, RB, T).astype(BF16)

    own[:PK_OUT] = w_v[1]
    own[PK_OUT:PK_NORM] = wo_v[...].reshape(2 * D, C)
    norms = jnp.concatenate([og_v[0], og_v[1]], 0)
    hi = norms.astype(BF16).astype(F32)
    mid = (norms - hi).astype(BF16).astype(F32)
    low = norms - hi - mid
    tile = jnp.concatenate([hi, mid, low, jnp.zeros_like(hi)], 0)
    own[PK_NORM:] = jnp.concatenate([tile, jnp.zeros((16, C - D), F32)], 1).astype(BF16)


def gate0_kernel(pair, in_gain, in_bias, w_gate, state, gate, block, sem):
    at = pl.multiple_of(lax.axis_index("ch") * T, T)
    copy = pltpu.make_async_copy(pair.at[:, pl.ds(at, T), :], block, sem)
    copy.start()
    gain, bias = column(in_gain[0:1, :]), column(in_bias[0:1, :])
    w_g = w_gate[0].astype(F32).T.astype(BF16)
    copy.wait()
    for i in range(RB):
        z = block[i].T
        state[i] = z
        gate[i] = sigmoid(dot(w_g, norm_cols(z, gain, bias).astype(BF16)))


def weights_kernel(own, up, down, far, w_proj, w_out, norms, pk):
    g = lax.axis_index("ch")
    pk[g] = own[...]
    pk[lax.rem(g + 3, G)] = up[...]
    pk[lax.rem(g + 1, G)] = down[...]
    pk[lax.rem(g + 2, G)] = far[...]
    for k in range(G):
        w_proj[k] = pk[k, PK_PROJ : PK_PROJ + C]
    for k in range(G):
        parts = pk[k, PK_NORM:].astype(F32)
        parts = parts[0:4] + parts[4:8] + parts[8:12]
        for j in range(4):
            norms[j, D * k : D * k + D] = column(parts[j : j + 1])[:D]
    for layer in range(2):
        rows = jnp.concatenate(
            [pk[k, PK_OUT + D * layer : PK_OUT + D * (layer + 1)] for k in range(G)], 0
        )
        w_out[layer] = rows.astype(F32).T.astype(BF16)


def outgoing_kernel(a, out):
    left = a[:, 0].reshape(N, N)
    for h in range(G):
        right = a[8 * h : 8 * h + 8, 1].reshape(T, N)
        out[h] = dot(left, right, 1, 1).reshape(R, RB, T).astype(BF16)


def incoming_kernel(b, out):
    left = jnp.concatenate([b[R * h : R * h + R, 0].reshape(N, T) for h in range(G)], 1)
    for h in range(G):
        right = b[R * h : R * h + R, 1].reshape(N, T)
        out[h] = dot(left, right, 0, 0).reshape(R, RB, T).astype(BF16)


def middle_kernel(
    y, z0, gate, mask, in_gain, in_bias, w_proj, w_out, norms, state, normed, out, mask_v, mask_s, ys, left_s, right_s, sems
):
    at = pl.multiple_of(lax.axis_index("ch") * T, T)
    copies = [
        pltpu.make_async_copy(mask.at[:, pl.ds(at, T)], mask_v, sems.at[0]),
        pltpu.make_async_copy(mask, mask_s, sems.at[1]),
    ]
    for copy in copies:
        copy.start()
    gain1, bias1 = column(in_gain[1:2, :]), column(in_bias[1:2, :])
    row0 = lax.axis_index("row") * RB
    ys[...] = y[...].astype(F32).reshape(C * RB, T)
    for copy in copies:
        copy.wait()
    cols = mask_v[...].astype(F32) * 0.5
    for i in range(RB):
        hidden = norm_cols(ys[pl.ds(i, C, stride=RB), :], norms[0], norms[2]).astype(BF16)
        z = z0[i] + gate[i] * dot(w_out[0], hidden)
        state[i] = z
        zn = norm_cols(z, gain1, bias1).astype(BF16)
        normed[i] = zn
        half = cols * mask_s[0, row0 + i].astype(F32)
        for g in range(G):
            proj = dot(w_proj[g], zn)
            rows = pl.ds(i + g * D * RB, D, stride=RB)
            left_s[rows, :] = gated(proj[0:D], proj[D : 2 * D], half)
            right_s[rows, :] = gated(proj[2 * D : 3 * D], proj[3 * D :], half)
    out[:, 0] = left_s[...].reshape(C, RB, T).astype(BF16)
    out[:, 1] = right_s[...].reshape(C, RB, T).astype(BF16)


def last_kernel(y, state, normed, w_gate, w_out, norms, out0, out1, ys):
    w_g = w_gate[1].astype(F32).T.astype(BF16)
    ys[...] = y[...].astype(F32).reshape(C * RB, T)
    for i in range(RB):
        hidden = norm_cols(ys[pl.ds(i, C, stride=RB), :], norms[1], norms[3]).astype(BF16)
        gate = sigmoid(dot(w_g, normed[i]))
        z = state[i] + gate * dot(w_out[1], hidden)
        out = (out0, out1)[i // HB]
        out[i % HB] = z.T.astype(BF16)


def spread_near_kernel(own0, own1, up0, up1, down0, down1, out, buf, sems):
    g = lax.axis_index("ch")
    copies = []
    for k, (shift, lo, hi) in enumerate([(0, own0, own1), (3, up0, up1), (1, down0, down1)]):
        buf[k, :HB] = lo[...].astype(F32)
        buf[k, HB:] = hi[...].astype(F32)
        at = pl.multiple_of(lax.rem(g + shift, G) * T, T)
        copies.append(pltpu.make_async_copy(buf.at[k], out.at[:, pl.ds(at, T), :], sems.at[k]))
        copies[-1].start()
    for copy in copies:
        copy.wait()


def spread_far_kernel(far0, far1, _, out, buf, sems):
    at = pl.multiple_of(lax.rem(lax.axis_index("ch") + 2, G) * T, T)
    copies = []
    for k, far in enumerate((far0, far1)):
        buf[k] = far[...].astype(F32)
        copies.append(
            pltpu.make_async_copy(buf.at[k], out.at[pl.ds(k * HB, HB), pl.ds(at, T), :], sems.at[k])
        )
        copies[-1].start()
    for copy in copies:
        copy.wait()


def params(limit=VMEM_LIMIT):
    return pltpu.CompilerParams(vmem_limit_bytes=limit)


def call(kernel, name, outs, scratch, ins, limit=VMEM_LIMIT):
    return pl.pallas_call(
        kernel,
        out_shape=outs,
        in_specs=[pl.BlockSpec(memory_space=space) for _, space in ins],
        out_specs=jax.tree.map(lambda _: pl.BlockSpec(memory_space=VMEM), outs),
        scratch_shapes=scratch,
        compiler_params=params(limit),
        name=name,
    )(*[value for value, _ in ins])


def on_device(pair, mask, in_gain, in_bias, w_proj, w_gate, out_gain, out_bias, w_out):
    arr = jax.ShapeDtypeStruct
    mask = mask[None]
    w_t = jnp.transpose(w_proj, (0, 2, 3, 1)).reshape(2, 4 * D, C)
    dma = pltpu.SemaphoreType.DMA

    a, own = call(
        project0_kernel,
        "project0",
        (arr((D, 2, RB, N), BF16), arr((PK, C), BF16)),
        [
            pltpu.VMEM((RB, N, C), F32),
            pltpu.VMEM((1, N), jnp.int32),
            pltpu.SMEM((1, N), jnp.int32),
            pltpu.VMEM((2, 2, C), F32),
            pltpu.VMEM((2, 4 * D, C), BF16),
            pltpu.VMEM((2, D, C), BF16),
            pltpu.VMEM((2, 2, D), F32),
            pltpu.VMEM((G, D * RB, T), F32),
            pltpu.VMEM((G, D * RB, T), F32),
            dma((8 + RB,)),
        ],
        [(v, HBM) for v in (pair, mask, in_gain, in_bias, w_t, w_out, out_gain, out_bias)],
        WHOLE_VMEM,
    )

    up = functools.partial(lax.ppermute, axis_name="ch", perm=[(k, (k + 1) % G) for k in range(G)])
    down = functools.partial(lax.ppermute, axis_name="ch", perm=[(k, (k - 1) % G) for k in range(G)])
    cross = functools.partial(lax.ppermute, axis_name="ch", perm=[(k, (k + 2) % G) for k in range(G)])

    a = lax.all_to_all(a, "row", 0, 0)
    w_proj1, w_out_t, norms = call(
        weights_kernel,
        "weights",
        (arr((G, C, C), BF16), arr((2, C, C), BF16), arr((4, C, T), F32)),
        [pltpu.VMEM((G, PK, C), BF16)],
        [(v, VMEM) for v in (own, up(own), down(own), cross(own))],
    )
    state, gate = call(
        gate0_kernel,
        "gate0",
        (arr((RB, C, T), F32), arr((RB, C, T), F32)),
        [pltpu.VMEM((RB, T, C), F32), dma],
        [(pair, HBM), (in_gain, VMEM), (in_bias, VMEM), (w_gate, VMEM)],
        MOST_VMEM,
    )
    a, state, gate, w_proj1, w_out_t, norms = lax.optimization_barrier(
        (a, state, gate, w_proj1, w_out_t, norms)
    )
    x = call(outgoing_kernel, "outgoing", arr((G, R, RB, T), BF16), [], [(a, VMEM)])
    y = lax.all_to_all(x.reshape(G * R, RB, T), ("ch", "row"), 0, 0)
    state, normed, b = call(
        middle_kernel,
        "middle",
        (arr((RB, C, T), F32), arr((RB, C, T), BF16), arr((C, 2, RB, T), BF16)),
        [pltpu.VMEM((1, T), jnp.int32), pltpu.SMEM((1, N), jnp.int32)]
        + [pltpu.VMEM((C * RB, T), F32)] * 3
        + [dma((2,))],
        [(y, VMEM), (state, VMEM), (gate, VMEM), (mask, HBM)]
        + [(v, VMEM) for v in (in_gain, in_bias, w_proj1, w_out_t, norms)],
    )
    b = lax.all_to_all(b, ("ch", "row"), 0, 0)
    x = call(incoming_kernel, "incoming", arr((G, R, RB, T), BF16), [], [(b, VMEM)])
    y = lax.all_to_all(x.reshape(G * R, RB, T), ("ch", "row"), 0, 0)
    half = arr((HB, T, C), BF16)
    z0, z1 = call(
        last_kernel,
        "last",
        (half, half),
        [pltpu.VMEM((C * RB, T), F32)],
        [(v, VMEM) for v in (y, state, normed, w_gate, w_out_t, norms)],
    )
    up0, down1 = up(z0), down(z1)
    up1, down0 = up(z1), down(z0)
    far0, far1 = up(up0), down(down1)
    whole = arr((RB, N, C), F32)
    near = pl.pallas_call(
        spread_near_kernel,
        out_shape=whole,
        in_specs=[pl.BlockSpec(memory_space=VMEM)] * 6,
        out_specs=pl.BlockSpec(memory_space=HBM),
        scratch_shapes=[pltpu.VMEM((3, RB, T, C), F32), dma((3,))],
        compiler_params=params(),
        name="spread_near",
    )(z0, z1, up0, up1, down0, down1)
    return pl.pallas_call(
        spread_far_kernel,
        out_shape=whole,
        in_specs=[pl.BlockSpec(memory_space=VMEM)] * 2 + [pl.BlockSpec(memory_space=HBM)],
        out_specs=pl.BlockSpec(memory_space=HBM),
        scratch_shapes=[pltpu.VMEM((2, HB, T, C), F32), dma((2,))],
        input_output_aliases={2: 0},
        compiler_params=params(),
        name="spread_far",
    )(far0, far1, near)


def solution(mesh):
    placed = (
        P("row", None, None),
        P(),
        P(),
        P(),
        P(None, None, None, "ch"),
        P(),
        P(None, "ch"),
        P(None, "ch"),
        P(None, "ch", None),
    )
    return jax.shard_map(
        on_device, mesh=mesh, in_specs=placed, out_specs=P("row", None, None), check_vma=False
    )
```

time: 519 us -> 126 us (0.24)
  waiting for transfers between devices: 365 us -> 19 us
  matrix products: 40.2 us -> 0 us
  other arithmetic: 35.1 us -> 0 us
  local copies, waits for them, and re-layouts: 28.8 us -> 1.57 us
  blocking collectives: 34.1 us -> 61.3 us
  starting transfers between devices: 0.13 us -> 22.2 us
  Pallas kernels: 0 us -> 21.7 us
  between operations: 13.4 us -> 0.28 us
    psum x2 -> x0, waiting for transfers between devices: 175 us -> none  [on_device(): change = lax.psum(partial_value, 'ch')]
    reduce_scatter x1 -> x0, waiting for transfers between devices: 115 us -> none  [incoming(): lax.psum_scatter(jnp.einsum('cki,ckj->icj', left, right, preferred_elemen...]
    all_gather x1 -> x0, waiting for transfers between devices: 75.1 us -> none  [outgoing(): lax.all_gather(right, 'row', axis=1, tiled=True)]
    all_to_all x0 -> x3, blocking collectives: none -> 61.3 us  [the longest x2 37.6 us: on_device(): y = lax.all_to_all(x.reshape(G * R, RB, T), ('ch', 'row'), 0, 0)]
    dot_general x8 -> x0, matrix products: 40.2 us -> none  [the longest x1 17.6 us: outgoing(): jnp.einsum('cik,cjk->cij', left, lax.all_gather(right, 'row', axis=1, til...]
    psum x2 -> x0, blocking collectives: 34.1 us -> none  [hidden_norm(): lax.psum(jnp.sum(mixed * mixed, 0).astype(jnp.bfloat16), 'ch')]
    convert_element_type x1 -> x0, local copies, waits for them, and re-layouts: 28.6 us -> none  [incoming(): jnp.einsum('cki,ckj->icj', left, right, preferred_element_type=jnp.float32)]
    pallas_call x0 -> x9, Pallas kernels: none -> 21.7 us  [the longest x7 19 us: call(): pl.pallas_call(kernel, out_shape=outs, in_specs=[pl.BlockSpec(memory_spac...]
  transfers between devices with their start and end apart: 4 -> 10, of which waited for: 4 -> 7; matrix products, arithmetic and copies ran while one was open for 1% -> 0% of each run, Pallas kernels for 0% -> 3%
where the time goes in v2:
time: 126 us
  blocking collectives  61.3 us (49%)
  starting transfers between devices  22.2 us (18%)
  Pallas kernels  21.7 us (17%)
  waiting for transfers between devices  19 us (15%)
  local copies, waits for them, and re-layouts  1.57 us (1%)
    all_to_all x2, blocking collectives, on_device(): y = lax.all_to_all(x.reshape(G * R, RB, T), ('ch', 'row'), 0, 0)  37.6 us
    all_to_all x1, blocking collectives, on_device(): b = lax.all_to_all(b, ('ch', 'row'), 0, 0)  23.7 us
    pallas_call x7, Pallas kernels, call(): pl.pallas_call(kernel, out_shape=outs, in_specs=[pl.BlockSpec(memory_spac...  19 us
    all_to_all x1, starting transfers between devices, on_device(): a = lax.all_to_all(a, 'row', 0, 0)  8.45 us
    all_to_all x1, waiting for transfers between devices, on_device(): a = lax.all_to_all(a, 'row', 0, 0)  6.48 us
    ppermute x2, waiting for transfers between devices, on_device(): up0, down1 = (up(z0), down(z1))  5.19 us
    ppermute x2, starting transfers between devices, on_device(): up0, down1 = (up(z0), down(z1))  3.31 us
    ppermute x2, starting transfers between devices, on_device(): far0, far1 = (up(up0), down(down1))  3.24 us
  transfers between devices with their start and end apart: 10, of which 7 were waited for; matrix products, arithmetic and copies ran while one was open for 0% of the time, Pallas kernels for 3%

profile of v2, /device:TPU:0, one launch (start us, length us, event | category | flops | bytes accessed | tf_op | source)
XLA Modules:
  0.0 126.0 jit_solution(17794200407699599747)
XLA Ops:
  0.0 8.8 %project0.1 = (bf16[32,2,16,512]{3,2,1,0:T(8,128)(2,1)}, bf16[208,128]{1,0:T(8,128)(2,1)}) custom-call(f32[16,512,128]{2,1,0:T(8,128)} %pair.3, s32[1,512]{1,0:T(1,128)} %bitcast.8, f32[2,128]{1,0:T(2,128)} %in_gain.5, f32[2,128]{1,0:T(2,128)} %in_bias.5, bf16[2,128,128]{2,1,0:T(8,128)(2,1)} %bitcast.10, bf16[2,32,128]{2,1,0:T(8,128)(2,1)} %w_out.1, ...), custom_call_target="tpu_custom_call" | custom-call | tf_op jit(solution)/shard_map/project0/pallas_call | solution.py:218
  8.8 0.0 copy-start.6
  8.8 8.5 %all-to-all-start = ((bf16[32,2,16,512]{3,2,1,0:T(8,128)(2,1)}), bf16[32,2,16,512]{3,2,1,0:T(8,128)(2,1)S(1)}, u32[]{:S(2)}, u32[]{:S(2)}) async-start(bf16[32,2,16,512]{3,2,1,0:T(8,128)(2,1)} %get-tuple-element.23), calls=%async_computation | async-start | bytes 2097152 | tf_op jit(solution)/shard_map/all_to_all | solution.py:259
  17.3 3.1 %collective-permute-start.2 = (bf16[208,128]{1,0:T(8,128)(2,1)}, bf16[208,128]{1,0:T(8,128)(2,1)S(1)}, u32[]{:S(2)}, u32[]{:S(2)}) collective-permute-start(bf16[208,128]{1,0:T(8,128)(2,1)} %get-tuple-element.26.own), channel_id=1, source_target_pairs={{0,2},{1,3},{2,0},{3,1},{4,6},{5,7},{6,4},{7,5},{8,10},{9,11},{10,... | collective-permute-start | bytes 159752 | tf_op jit(solution)/shard_map/ppermute | solution.py:265
  20.4 1.1 collective-permute-start.1
  21.5 0.9 collective-permute-start
  22.4 1.9 %gate0.1 = (f32[16,128,128]{2,1,0:T(8,128)S(1)}, f32[16,128,128]{2,1,0:T(8,128)S(1)}) custom-call(f32[16,512,128]{2,1,0:T(8,128)} %pair.3, f32[2,128]{1,0:T(2,128)S(1)} %copy-done.4, f32[2,128]{1,0:T(2,128)S(1)} %copy-done.5, bf16[2,128,128]{2,1,0:T(8,128)(2,1)S(1)} %copy-done), custom_call_target="tpu_custom_call" | custom-call | tf_op jit(solution)/shard_map/gate0/pallas_call | solution.py:218
  24.4 0.4 collective-permute-done.1.down
  24.8 2.3 %collective-permute-done.up = bf16[208,128]{1,0:T(8,128)(2,1)S(1)} collective-permute-done((bf16[208,128]{1,0:T(8,128)(2,1)}, bf16[208,128]{1,0:T(8,128)(2,1)S(1)}, u32[]{:S(2)}, u32[]{:S(2)}) %collective-permute-start) | collective-permute-done | bytes 53280 | tf_op jit(solution)/shard_map/ppermute | solution.py:265
  27.1 0.4 weights.1
  27.5 0.6 copy-done.1
  28.2 6.5 %all-to-all-done.a = bf16[32,2,16,512]{3,2,1,0:T(8,128)(2,1)S(1)} async-done(((bf16[32,2,16,512]{3,2,1,0:T(8,128)(2,1)}), bf16[32,2,16,512]{3,2,1,0:T(8,128)(2,1)S(1)}, u32[]{:S(2)}, u32[]{:S(2)}) %all-to-all-start) | async-done | bytes 1048608 | tf_op jit(solution)/shard_map/all_to_all | solution.py:259
  34.6 0.7 outgoing.1
  35.3 19.6 %all_to_all.20.y = bf16[128,16,128]{2,1,0:T(8,128)(2,1)S(1)} all-to-all(bf16[128,16,128]{2,1,0:T(8,128)(2,1)S(1)} %bitcast.6), channel_id=1, replica_groups=mesh['row'=32,'ch'=4] {'ch','row'}, dimensions={0} | all-to-all | bytes 1048576 | tf_op jit(solution)/shard_map/all_to_all | solution.py:279
  55.0 0.9 copy-done.2
  55.9 5.2 %middle.1 = (f32[16,128,128]{2,1,0:T(8,128)S(1)}, bf16[16,128,128]{2,1,0:T(8,128)(2,1)S(1)}, bf16[128,2,16,128]{3,2,1,0:T(8,128)(2,1)S(1)}) custom-call(bf16[128,16,128]{2,1,0:T(8,128)(2,1)S(1)} %all_to_all.20.y, f32[16,128,128]{2,1,0:T(8,128)S(1)} %get-tuple-element.31.z0, f32[16,128,128]{2,1,0:T(8,128)S(1)} %get-tuple-element.32.gate, ...), custom_call_target="tpu_custom_call" | custom-call | tf_op jit(solution)/shard_map/middle/pallas_call | solution.py:218
  61.1 23.7 %all_to_all.21.b = bf16[128,2,16,128]{3,2,1,0:T(8,128)(2,1)S(1)} all-to-all(bf16[128,2,16,128]{3,2,1,0:T(8,128)(2,1)S(1)} %get-tuple-element.36), channel_id=1, replica_groups=mesh['row'=32,'ch'=4] {'ch','row'}, dimensions={0} | all-to-all | bytes 2097152 | tf_op jit(solution)/shard_map/all_to_all | solution.py:290
  84.8 0.7 incoming.1
  85.5 18.0 %all_to_all.22.y = bf16[128,16,128]{2,1,0:T(8,128)(2,1)S(1)} all-to-all(bf16[128,16,128]{2,1,0:T(8,128)(2,1)S(1)} %bitcast.7), channel_id=1, replica_groups=mesh['row'=32,'ch'=4] {'ch','row'}, dimensions={0} | all-to-all | bytes 1048576 | tf_op jit(solution)/shard_map/all_to_all | solution.py:292
  103.5 1.3 %last.1 = (bf16[8,128,128]{2,1,0:T(8,128)(2,1)S(1)}, bf16[8,128,128]{2,1,0:T(8,128)(2,1)S(1)}) custom-call(bf16[128,16,128]{2,1,0:T(8,128)(2,1)S(1)} %all_to_all.22.y, f32[16,128,128]{2,1,0:T(8,128)S(1)} %get-tuple-element.37.state, bf16[16,128,128]{2,1,0:T(8,128)(2,1)S(1)} %get-tuple-element.38.normed, bf16[2,128,128]{2,1,0:T(8,128)(2,1)S(1)} %copy-done, ...), custom_call_target="tpu_custom_call" | custom-call | tf_op jit(solution)/shard_map/last/pallas_call | solution.py:218
  104.7 0.7 collective-permute-start.3
  105.4 2.7 %collective-permute-start.5 = (bf16[8,128,128]{2,1,0:T(8,128)(2,1)S(1)}, bf16[8,128,128]{2,1,0:T(8,128)(2,1)S(1)}, u32[]{:S(2)}, u32[]{:S(2)}) collective-permute-start(bf16[8,128,128]{2,1,0:T(8,128)(2,1)S(1)} %get-tuple-element.40.own1), channel_id=1, source_target_pairs={{0,3},{1,0},{2,1},{3,2},{4,7},{5,4},{6,5},{7,6},{8,11},{9,8},{10,9... | collective-permute-start | bytes 786440 | tf_op jit(solution)/shard_map/ppermute | solution.py:301
  108.0 0.0 collective-permute-start.8
  108.1 2.0 %collective-permute-start.7 = (bf16[8,128,128]{2,1,0:T(8,128)(2,1)S(1)}, bf16[8,128,128]{2,1,0:T(8,128)(2,1)S(1)}, u32[]{:S(2)}, u32[]{:S(2)}) collective-permute-start(bf16[8,128,128]{2,1,0:T(8,128)(2,1)S(1)} %get-tuple-element.40.own1), channel_id=1, source_target_pairs={{0,1},{1,2},{2,3},{3,0},{4,5},{5,6},{6,7},{7,4},{8,9},{9,10},{10,1... | collective-permute-start | bytes 786440 | tf_op jit(solution)/shard_map/ppermute | solution.py:302
  110.1 5.2 %collective-permute-done.3.up0 = bf16[8,128,128]{2,1,0:T(8,128)(2,1)S(1)} collective-permute-done((bf16[8,128,128]{2,1,0:T(8,128)(2,1)S(1)}, bf16[8,128,128]{2,1,0:T(8,128)(2,1)S(1)}, u32[]{:S(2)}, u32[]{:S(2)}) %collective-permute-start.3) | collective-permute-done | bytes 262176 | tf_op jit(solution)/shard_map/ppermute | solution.py:301
  115.3 0.0 collective-permute-start.4
  115.3 3.2 %collective-permute-start.6 = (bf16[8,128,128]{2,1,0:T(8,128)(2,1)S(1)}, bf16[8,128,128]{2,1,0:T(8,128)(2,1)S(1)}, u32[]{:S(2)}, u32[]{:S(2)}) collective-permute-start(bf16[8,128,128]{2,1,0:T(8,128)(2,1)S(1)} %collective-permute-done.5.down1), channel_id=1, source_target_pairs={{0,3},{1,0},{2,1},{3,2},{4,7},{5,4},{6,5},{7,6},{8,11},{9,8},{10,9... | collective-permute-start | bytes 786440 | tf_op jit(solution)/shard_map/ppermute | solution.py:303
  118.5 1.9 %collective-permute-done.8.down0 = bf16[8,128,128]{2,1,0:T(8,128)(2,1)S(1)} collective-permute-done((bf16[8,128,128]{2,1,0:T(8,128)(2,1)S(1)}, bf16[8,128,128]{2,1,0:T(8,128)(2,1)S(1)}, u32[]{:S(2)}, u32[]{:S(2)}) %collective-permute-start.8) | collective-permute-done | bytes 262176 | tf_op jit(solution)/shard_map/ppermute | solution.py:302
  120.4 0.5 collective-permute-done.7.up1
  120.9 1.8 %spread_near.1._ = f32[16,512,128]{2,1,0:T(8,128)} custom-call(bf16[8,128,128]{2,1,0:T(8,128)(2,1)S(1)} %get-tuple-element.39.own0, bf16[8,128,128]{2,1,0:T(8,128)(2,1)S(1)} %get-tuple-element.40.own1, bf16[8,128,128]{2,1,0:T(8,128)(2,1)S(1)} %collective-permute-done.3.up0, bf16[8,128,128]{2,1,0:T(8,128)(2,1)S(1)} %collective-permute-done.7.up1, ...), custom_call_target="tpu_custom_call" | custom-call | tf_op jit(solution)/shard_map/spread_near/pallas_call | solution.py:305
  122.6 2.2 %collective-permute-done.4.far0 = bf16[8,128,128]{2,1,0:T(8,128)(2,1)S(1)} collective-permute-done((bf16[8,128,128]{2,1,0:T(8,128)(2,1)S(1)}, bf16[8,128,128]{2,1,0:T(8,128)(2,1)S(1)}, u32[]{:S(2)}, u32[]{:S(2)}) %collective-permute-start.4) | collective-permute-done | bytes 262176 | tf_op jit(solution)/shard_map/ppermute | solution.py:303
  124.9 1.0 spread_far.1
  (14 shorter events, 0.0 us)
Async XLA Ops:
  0.0 22.4 %copy-start.5 = (f32[2,128]{1,0:T(2,128)S(1)}, f32[2,128]{1,0:T(2,128)}, u32[]{:S(2)}) copy-start(f32[2,128]{1,0:T(2,128)} %in_bias.5) | copy-start | bytes 3076
  0.0 22.4 %copy-start.4 = (f32[2,128]{1,0:T(2,128)S(1)}, f32[2,128]{1,0:T(2,128)}, u32[]{:S(2)}) copy-start(f32[2,128]{1,0:T(2,128)} %in_gain.5) | copy-start | bytes 3076
  0.0 22.4 %copy-start = (bf16[2,128,128]{2,1,0:T(8,128)(2,1)S(1)}, bf16[2,128,128]{2,1,0:T(8,128)(2,1)}, u32[]{:S(2)}) copy-start(bf16[2,128,128]{2,1,0:T(8,128)(2,1)} %w_gate.3) | copy-start | bytes 196612
  8.8 46.2 %copy-start.6 = (s32[512]{0:T(512)S(1)}, s32[512]{0:T(512)}, u32[]{:S(2)}) copy-start(s32[512]{0:T(512)} %param.10) | copy-start | bytes 6148
  8.8 25.8 %all-to-all-start = ((bf16[32,2,16,512]{3,2,1,0:T(8,128)(2,1)}), bf16[32,2,16,512]{3,2,1,0:T(8,128)(2,1)S(1)}, u32[]{:S(2)}, u32[]{:S(2)}) async-start(bf16[32,2,16,512]{3,2,1,0:T(8,128)(2,1)} %get-tuple-element.23), calls=%async_computation | async-start | bytes 2097152 | tf_op jit(solution)/shard_map/all_to_all | solution.py:259
  17.3 9.8 %copy-start.3 = (bf16[208,128]{1,0:T(8,128)(2,1)S(1)}, bf16[208,128]{1,0:T(8,128)(2,1)}, u32[]{:S(2)}) copy-start(bf16[208,128]{1,0:T(8,128)(2,1)} %get-tuple-element.26.own) | copy-start | bytes 159748
  17.3 7.1 %collective-permute-start.2 = (bf16[208,128]{1,0:T(8,128)(2,1)}, bf16[208,128]{1,0:T(8,128)(2,1)S(1)}, u32[]{:S(2)}, u32[]{:S(2)}) collective-permute-start(bf16[208,128]{1,0:T(8,128)(2,1)} %get-tuple-element.26.own), channel_id=1, source_target_pairs={{0,2},{1,3},{2,0},{3,1},{4,6},{5,7},{6,4},{7,5},{8,10},{9,11},{10,... | collective-permute-start | bytes 159752 | tf_op jit(solution)/shard_map/ppermute | solution.py:265
  20.4 4.3 %collective-permute-start.1 = (bf16[208,128]{1,0:T(8,128)(2,1)}, bf16[208,128]{1,0:T(8,128)(2,1)S(1)}, u32[]{:S(2)}, u32[]{:S(2)}) collective-permute-start(bf16[208,128]{1,0:T(8,128)(2,1)} %get-tuple-element.26.own), channel_id=1, source_target_pairs={{0,3},{1,0},{2,1},{3,2},{4,7},{5,4},{6,5},{7,6},{8,11},{9,8},{10,9... | collective-permute-start | bytes 159752 | tf_op jit(solution)/shard_map/ppermute | solution.py:265
  21.5 5.6 %collective-permute-start = (bf16[208,128]{1,0:T(8,128)(2,1)}, bf16[208,128]{1,0:T(8,128)(2,1)S(1)}, u32[]{:S(2)}, u32[]{:S(2)}) collective-permute-start(bf16[208,128]{1,0:T(8,128)(2,1)} %get-tuple-element.26.own), channel_id=1, source_target_pairs={{0,1},{1,2},{2,3},{3,0},{4,5},{5,6},{6,7},{7,4},{8,9},{9,10},{10,1... | collective-permute-start | bytes 159752 | tf_op jit(solution)/shard_map/ppermute | solution.py:265
  27.5 0.7 copy-start.1
  55.0 0.9 copy-start.2
  104.7 10.5 %collective-permute-start.3 = (bf16[8,128,128]{2,1,0:T(8,128)(2,1)S(1)}, bf16[8,128,128]{2,1,0:T(8,128)(2,1)S(1)}, u32[]{:S(2)}, u32[]{:S(2)}) collective-permute-start(bf16[8,128,128]{2,1,0:T(8,128)(2,1)S(1)} %get-tuple-element.39.own0), channel_id=1, source_target_pairs={{0,1},{1,2},{2,3},{3,0},{4,5},{5,6},{6,7},{7,4},{8,9},{9,10},{10,1... | collective-permute-start | bytes 786440 | tf_op jit(solution)/shard_map/ppermute | solution.py:301
  105.4 9.9 %collective-permute-start.5 = (bf16[8,128,128]{2,1,0:T(8,128)(2,1)S(1)}, bf16[8,128,128]{2,1,0:T(8,128)(2,1)S(1)}, u32[]{:S(2)}, u32[]{:S(2)}) collective-permute-start(bf16[8,128,128]{2,1,0:T(8,128)(2,1)S(1)} %get-tuple-element.40.own1), channel_id=1, source_target_pairs={{0,3},{1,0},{2,1},{3,2},{4,7},{5,4},{6,5},{7,6},{8,11},{9,8},{10,9... | collective-permute-start | bytes 786440 | tf_op jit(solution)/shard_map/ppermute | solution.py:301
  108.0 12.4 %collective-permute-start.8 = (bf16[8,128,128]{2,1,0:T(8,128)(2,1)S(1)}, bf16[8,128,128]{2,1,0:T(8,128)(2,1)S(1)}, u32[]{:S(2)}, u32[]{:S(2)}) collective-permute-start(bf16[8,128,128]{2,1,0:T(8,128)(2,1)S(1)} %get-tuple-element.39.own0), channel_id=1, source_target_pairs={{0,3},{1,0},{2,1},{3,2},{4,7},{5,4},{6,5},{7,6},{8,11},{9,8},{10,9... | collective-permute-start | bytes 786440 | tf_op jit(solution)/shard_map/ppermute | solution.py:302
  108.1 12.8 %collective-permute-start.7 = (bf16[8,128,128]{2,1,0:T(8,128)(2,1)S(1)}, bf16[8,128,128]{2,1,0:T(8,128)(2,1)S(1)}, u32[]{:S(2)}, u32[]{:S(2)}) collective-permute-start(bf16[8,128,128]{2,1,0:T(8,128)(2,1)S(1)} %get-tuple-element.40.own1), channel_id=1, source_target_pairs={{0,1},{1,2},{2,3},{3,0},{4,5},{5,6},{6,7},{7,4},{8,9},{9,10},{10,1... | collective-permute-start | bytes 786440 | tf_op jit(solution)/shard_map/ppermute | solution.py:302
  115.3 9.6 %collective-permute-start.4 = (bf16[8,128,128]{2,1,0:T(8,128)(2,1)S(1)}, bf16[8,128,128]{2,1,0:T(8,128)(2,1)S(1)}, u32[]{:S(2)}, u32[]{:S(2)}) collective-permute-start(bf16[8,128,128]{2,1,0:T(8,128)(2,1)S(1)} %collective-permute-done.3.up0), channel_id=1, source_target_pairs={{0,1},{1,2},{2,3},{3,0},{4,5},{5,6},{6,7},{7,4},{8,9},{9,10},{10,1... | collective-permute-start | bytes 786440 | tf_op jit(solution)/shard_map/ppermute | solution.py:303
  115.3 9.6 %collective-permute-start.6 = (bf16[8,128,128]{2,1,0:T(8,128)(2,1)S(1)}, bf16[8,128,128]{2,1,0:T(8,128)(2,1)S(1)}, u32[]{:S(2)}, u32[]{:S(2)}) collective-permute-start(bf16[8,128,128]{2,1,0:T(8,128)(2,1)S(1)} %collective-permute-done.5.down1), channel_id=1, source_target_pairs={{0,3},{1,0},{2,1},{3,2},{4,7},{5,4},{6,5},{7,6},{8,11},{9,8},{10,9... | collective-permute-start | bytes 786440 | tf_op jit(solution)/shard_map/ppermute | solution.py:303

commit v3 on v2

--- a/solution.py
+++ b/solution.py
@@ -46,7 +46,7 @@
 
 def project0_kernel(
     pair, mask, in_gain, in_bias, w, w_out, out_gain, out_bias, out, own,
-    rows, mask_v, mask_s, gb, w_v, wo_v, og_v, left_s, right_s, sems,
+    rows, mask_v, mask_s, gb, w_v, wo_v, og_v, left_s, right_s, zn_s, sems,
 ):
     small = [
         (mask, mask_v),
@@ -58,31 +58,16 @@
         (out_gain, og_v.at[0]),
         (out_bias, og_v.at[1]),
     ]
-    big = [(pair.at[i], rows.at[i]) for i in range(RB)]
+    big = [(pair.at[:, pl.ds(T * h, T)], rows.at[h]) for h in range(G)]
     copies = [pltpu.make_async_copy(*ends, sems.at[k]) for k, ends in enumerate(small + big)]
     few = len(small)
-    for copy in copies[few : few + 2] + copies[:few] + copies[few + 2 :]:
+    for copy in copies[few : few + 1] + copies[:few] + copies[few + 1 :]:
         copy.start()
     for copy in copies[:few]:
         copy.wait()
     gain, bias = column(gb[0, 0:1, :]), column(gb[1, 0:1, :])
     cols = mask_v[...].astype(F32) * 0.5
     row0 = lax.axis_index("row") * RB
-    for i in range(RB):
-        copies[few + i].wait()
-        zn = jnp.concatenate(
-            [norm_cols(rows[i, T * h : T * h + T].T, gain, bias).astype(BF16) for h in range(G)], 1
-        )
-        proj = dot(w_v[0], zn)
-        half = cols * mask_s[0, row0 + i].astype(F32)
-        left = gated(proj[0:D], proj[D : 2 * D], half)
-        right = gated(proj[2 * D : 3 * D], proj[3 * D :], half)
-        for h in range(G):
-            left_s[h, pl.ds(i, D, stride=RB), :] = left[:, T * h : T * h + T]
-            right_s[h, pl.ds(i, D, stride=RB), :] = right[:, T * h : T * h + T]
-    for h in range(G):
-        out[:, 0, :, T * h : T * h + T] = left_s[h].reshape(D, RB, T).astype(BF16)
-        out[:, 1, :, T * h : T * h + T] = right_s[h].reshape(D, RB, T).astype(BF16)
 
     own[:PK_OUT] = w_v[1]
     own[PK_OUT:PK_NORM] = wo_v[...].reshape(2 * D, C)
@@ -93,15 +78,39 @@
     tile = jnp.concatenate([hi, mid, low, jnp.zeros_like(hi)], 0)
     own[PK_NORM:] = jnp.concatenate([tile, jnp.zeros((16, C - D), F32)], 1).astype(BF16)
 
-
-def gate0_kernel(pair, in_gain, in_bias, w_gate, state, gate, block, sem):
+    for h in range(G):
+        copies[few + h].wait()
+        for i in range(RB):
+            zn_s[h, i] = norm_cols(rows[h, i].T, gain, bias).astype(BF16)
+        for i in range(0, RB, 2):
+            proj = dot(w_v[0], jnp.concatenate([zn_s[h, i], zn_s[h, i + 1]], 1))
+            for k in (0, 1):
+                half = cols[:, T * h : T * h + T] * mask_s[0, row0 + i + k].astype(F32)
+                part = proj[:, T * k : T * k + T]
+                left_s[h, pl.ds(i + k, D, stride=RB), :] = gated(part[0:D], part[D : 2 * D], half)
+                right_s[h, pl.ds(i + k, D, stride=RB), :] = gated(part[2 * D : 3 * D], part[3 * D :], half)
+        out[:, 0, :, T * h : T * h + T] = left_s[h].reshape(D, RB, T).astype(BF16)
+        out[:, 1, :, T * h : T * h + T] = right_s[h].reshape(D, RB, T).astype(BF16)
+
+
+def gate0_kernel(pair, mask, in_gain, in_bias, w_gate, state, gate, half, in_norm, block, mask_v, mask_s, sems):
     at = pl.multiple_of(lax.axis_index("ch") * T, T)
-    copy = pltpu.make_async_copy(pair.at[:, pl.ds(at, T), :], block, sem)
-    copy.start()
+    copies = [
+        pltpu.make_async_copy(pair.at[:, pl.ds(at, T), :], block, sems.at[0]),
+        pltpu.make_async_copy(mask.at[:, pl.ds(at, T)], mask_v, sems.at[1]),
+        pltpu.make_async_copy(mask, mask_s, sems.at[2]),
+    ]
+    for copy in copies:
+        copy.start()
     gain, bias = column(in_gain[0:1, :]), column(in_bias[0:1, :])
+    in_norm[0] = column(in_gain[1:2, :])
+    in_norm[1] = column(in_bias[1:2, :])
     w_g = w_gate[0].astype(F32).T.astype(BF16)
-    copy.wait()
+    for copy in copies:
+        copy.wait()
+    row0 = lax.axis_index("row") * RB
     for i in range(RB):
+        half[i : i + 1, :] = mask_v[...].astype(F32) * (0.5 * mask_s[0, row0 + i].astype(F32))
         z = block[i].T
         state[i] = z
         gate[i] = sigmoid(dot(w_g, norm_cols(z, gain, bias).astype(BF16)))
@@ -142,33 +151,25 @@
 
 
 def middle_kernel(
-    y, z0, gate, mask, in_gain, in_bias, w_proj, w_out, norms, state, normed, out, mask_v, mask_s, ys, left_s, right_s, sems
+    y, z0, gate, half_mask, in_norm, w_proj, w_out, norms, state, normed, out, ys, left_s, right_s, hid
 ):
-    at = pl.multiple_of(lax.axis_index("ch") * T, T)
-    copies = [
-        pltpu.make_async_copy(mask.at[:, pl.ds(at, T)], mask_v, sems.at[0]),
-        pltpu.make_async_copy(mask, mask_s, sems.at[1]),
-    ]
-    for copy in copies:
-        copy.start()
-    gain1, bias1 = column(in_gain[1:2, :]), column(in_bias[1:2, :])
-    row0 = lax.axis_index("row") * RB
     ys[...] = y[...].astype(F32).reshape(C * RB, T)
-    for copy in copies:
-        copy.wait()
-    cols = mask_v[...].astype(F32) * 0.5
     for i in range(RB):
-        hidden = norm_cols(ys[pl.ds(i, C, stride=RB), :], norms[0], norms[2]).astype(BF16)
-        z = z0[i] + gate[i] * dot(w_out[0], hidden)
+        hid[i] = norm_cols(ys[pl.ds(i, C, stride=RB), :], norms[0], norms[2]).astype(BF16)
+    for i in range(RB):
+        z = z0[i] + gate[i] * dot(w_out[0], hid[i])
         state[i] = z
-        zn = norm_cols(z, gain1, bias1).astype(BF16)
-        normed[i] = zn
-        half = cols * mask_s[0, row0 + i].astype(F32)
-        for g in range(G):
-            proj = dot(w_proj[g], zn)
-            rows = pl.ds(i + g * D * RB, D, stride=RB)
-            left_s[rows, :] = gated(proj[0:D], proj[D : 2 * D], half)
-            right_s[rows, :] = gated(proj[2 * D : 3 * D], proj[3 * D :], half)
+        normed[i] = norm_cols(z, in_norm[0], in_norm[1]).astype(BF16)
+    for g in range(G):
+        for i in range(0, RB, 2):
+            half = jnp.concatenate([half_mask[i : i + 1, :], half_mask[i + 1 : i + 2, :]], 1)
+            proj = dot(w_proj[g], jnp.concatenate([normed[i], normed[i + 1]], 1))
+            left = gated(proj[0:D], proj[D : 2 * D], half)
+            right = gated(proj[2 * D : 3 * D], proj[3 * D :], half)
+            for k in (0, 1):
+                rows = pl.ds(i + k + g * D * RB, D, stride=RB)
+                left_s[rows, :] = left[:, T * k : T * k + T]
+                right_s[rows, :] = right[:, T * k : T * k + T]
     out[:, 0] = left_s[...].reshape(C, RB, T).astype(BF16)
     out[:, 1] = right_s[...].reshape(C, RB, T).astype(BF16)
 
@@ -237,7 +238,7 @@
         "project0",
         (arr((D, 2, RB, N), BF16), arr((PK, C), BF16)),
         [
-            pltpu.VMEM((RB, N, C), F32),
+            pltpu.VMEM((G, RB, T, C), F32),
             pltpu.VMEM((1, N), jnp.int32),
             pltpu.SMEM((1, N), jnp.int32),
             pltpu.VMEM((2, 2, C), F32),
@@ -246,7 +247,8 @@
             pltpu.VMEM((2, 2, D), F32),
             pltpu.VMEM((G, D * RB, T), F32),
             pltpu.VMEM((G, D * RB, T), F32),
-            dma((8 + RB,)),
+            pltpu.VMEM((G, RB, C, T), BF16),
+            dma((8 + G,)),
         ],
         [(v, HBM) for v in (pair, mask, in_gain, in_bias, w_t, w_out, out_gain, out_bias)],
         WHOLE_VMEM,
@@ -264,16 +266,21 @@
         [pltpu.VMEM((G, PK, C), BF16)],
         [(v, VMEM) for v in (own, up(own), down(own), cross(own))],
     )
-    state, gate = call(
+    state, gate, half_mask, in_norm = call(
         gate0_kernel,
         "gate0",
-        (arr((RB, C, T), F32), arr((RB, C, T), F32)),
-        [pltpu.VMEM((RB, T, C), F32), dma],
-        [(pair, HBM), (in_gain, VMEM), (in_bias, VMEM), (w_gate, VMEM)],
+        (arr((RB, C, T), F32), arr((RB, C, T), F32), arr((RB, T), F32), arr((2, C, T), F32)),
+        [
+            pltpu.VMEM((RB, T, C), F32),
+            pltpu.VMEM((1, T), jnp.int32),
+            pltpu.SMEM((1, N), jnp.int32),
+            dma((3,)),
+        ],
+        [(pair, HBM), (mask, HBM), (in_gain, VMEM), (in_bias, VMEM), (w_gate, VMEM)],
         MOST_VMEM,
     )
-    a, state, gate, w_proj1, w_out_t, norms = lax.optimization_barrier(
-        (a, state, gate, w_proj1, w_out_t, norms)
+    a, state, gate, half_mask, in_norm, w_proj1, w_out_t, norms = lax.optimization_barrier(
+        (a, state, gate, half_mask, in_norm, w_proj1, w_out_t, norms)
     )
     x = call(outgoing_kernel, "outgoing", arr((G, R, RB, T), BF16), [], [(a, VMEM)])
     y = lax.all_to_all(x.reshape(G * R, RB, T), ("ch", "row"), 0, 0)
@@ -281,11 +288,8 @@
         middle_kernel,
         "middle",
         (arr((RB, C, T), F32), arr((RB, C, T), BF16), arr((C, 2, RB, T), BF16)),
-        [pltpu.VMEM((1, T), jnp.int32), pltpu.SMEM((1, N), jnp.int32)]
-        + [pltpu.VMEM((C * RB, T), F32)] * 3
-        + [dma((2,))],
-        [(y, VMEM), (state, VMEM), (gate, VMEM), (mask, HBM)]
-        + [(v, VMEM) for v in (in_gain, in_bias, w_proj1, w_out_t, norms)],
+        [pltpu.VMEM((C * RB, T), F32)] * 3 + [pltpu.VMEM((RB, C, T), BF16)],
+        [(v, VMEM) for v in (y, state, gate, half_mask, in_norm, w_proj1, w_out_t, norms)],
     )
     b = lax.all_to_all(b, ("ch", "row"), 0, 0)
     x = call(incoming_kernel, "incoming", arr((G, R, RB, T), BF16), [], [(b, VMEM)])

time: 126 us -> 121 us (0.960)
  Pallas kernels: 21.7 us -> 15.7 us
  local copies, waits for them, and re-layouts: 1.57 us -> 3.11 us
    pallas_call x7, Pallas kernels: 19 us -> 12.9 us  [call(): pl.pallas_call(kernel, out_shape=outs, in_specs=[pl.BlockSpec(memory_spac...]
    unnamed x14 -> x18, local copies, waits for them, and re-layouts: 1.57 us -> 3.11 us
  transfers between devices with their start and end apart: 10 -> 10, of which waited for: 7 -> 6; matrix products, arithmetic and copies ran while one was open for 0% -> 0% of each run, Pallas kernels for 3% -> 3%
where the time goes in v3:
time: 121 us
  blocking collectives  61.3 us (51%)
  starting transfers between devices  22.1 us (18%)
  waiting for transfers between devices  18.3 us (15%)
  Pallas kernels  15.7 us (13%)
  local copies, waits for them, and re-layouts  3.11 us (3%)
    all_to_all x2, blocking collectives, on_device(): y = lax.all_to_all(x.reshape(G * R, RB, T), ('ch', 'row'), 0, 0)  37.6 us
    all_to_all x1, blocking collectives, on_device(): b = lax.all_to_all(b, ('ch', 'row'), 0, 0)  23.7 us
    pallas_call x7, Pallas kernels, call(): pl.pallas_call(kernel, out_shape=outs, in_specs=[pl.BlockSpec(memory_spac...  12.9 us
    all_to_all x1, starting transfers between devices, on_device(): a = lax.all_to_all(a, 'row', 0, 0)  8.44 us
    all_to_all x1, waiting for transfers between devices, on_device(): a = lax.all_to_all(a, 'row', 0, 0)  6.47 us
    ppermute x2, waiting for transfers between devices, on_device(): up0, down1 = (up(z0), down(z1))  5.19 us
    ppermute x2, starting transfers between devices, on_device(): up0, down1 = (up(z0), down(z1))  3.31 us
    ppermute x2, starting transfers between devices, on_device(): far0, far1 = (up(up0), down(down1))  3.24 us
  transfers between devices with their start and end apart: 10, of which 6 were waited for; matrix products, arithmetic and copies ran while one was open for 0% of the time, Pallas kernels for 3%

profile of v3, /device:TPU:0, one launch (start us, length us, event | category | flops | bytes accessed | tf_op | source)
XLA Modules:
  0.0 120.6 jit_solution(10056860561938238889)
XLA Ops:
  0.0 5.8 %project0.1 = (bf16[32,2,16,512]{3,2,1,0:T(8,128)(2,1)}, bf16[208,128]{1,0:T(8,128)(2,1)}) custom-call(f32[16,512,128]{2,1,0:T(8,128)} %pair.3, s32[1,512]{1,0:T(1,128)} %bitcast.8, f32[2,128]{1,0:T(2,128)} %in_gain.3, f32[2,128]{1,0:T(2,128)} %in_bias.3, bf16[2,128,128]{2,1,0:T(8,128)(2,1)} %bitcast.10, bf16[2,32,128]{2,1,0:T(8,128)(2,1)} %w_out.1, ...), custom_call_target="tpu_custom_call" | custom-call | tf_op jit(solution)/shard_map/project0/pallas_call | solution.py:219
  5.8 8.4 %all-to-all-start = ((bf16[32,2,16,512]{3,2,1,0:T(8,128)(2,1)}), bf16[32,2,16,512]{3,2,1,0:T(8,128)(2,1)S(1)}, u32[]{:S(2)}, u32[]{:S(2)}) async-start(bf16[32,2,16,512]{3,2,1,0:T(8,128)(2,1)} %get-tuple-element.27), calls=%async_computation | async-start | bytes 2097152 | tf_op jit(solution)/shard_map/all_to_all | solution.py:261
  14.3 3.1 %collective-permute-start.2 = (bf16[208,128]{1,0:T(8,128)(2,1)}, bf16[208,128]{1,0:T(8,128)(2,1)S(1)}, u32[]{:S(2)}, u32[]{:S(2)}) collective-permute-start(bf16[208,128]{1,0:T(8,128)(2,1)} %get-tuple-element.32.own), channel_id=1, source_target_pairs={{0,2},{1,3},{2,0},{3,1},{4,6},{5,7},{6,4},{7,5},{8,10},{9,11},{10,... | collective-permute-start | bytes 159752 | tf_op jit(solution)/shard_map/ppermute | solution.py:267
  17.4 1.1 collective-permute-start.1
  18.5 0.9 collective-permute-start
  19.4 2.0 %gate0.1 = (f32[16,128,128]{2,1,0:T(8,128)S(1)}, f32[16,128,128]{2,1,0:T(8,128)S(1)}, f32[16,128]{1,0:T(8,128)S(1)}, f32[2,128,128]{2,1,0:T(8,128)S(1)}) custom-call(f32[16,512,128]{2,1,0:T(8,128)} %pair.3, s32[1,512]{1,0:T(1,128)S(1)} %bitcast.9, f32[2,128]{1,0:T(2,128)S(1)} %copy-done.7, f32[2,128]{1,0:T(2,128)S(1)} %copy-done.8, ...), custom_call_target="tpu_custom_call" | custom-call | tf_op jit(solution)/shard_map/gate0/pallas_call | solution.py:219
  21.4 0.6 copy-done.1
  22.0 2.0 %collective-permute-done.up = bf16[208,128]{1,0:T(8,128)(2,1)S(1)} collective-permute-done((bf16[208,128]{1,0:T(8,128)(2,1)}, bf16[208,128]{1,0:T(8,128)(2,1)S(1)}, u32[]{:S(2)}, u32[]{:S(2)}) %collective-permute-start) | collective-permute-done | bytes 53280 | tf_op jit(solution)/shard_map/ppermute | solution.py:267
  24.1 0.4 weights.1
  24.5 0.6 copy-done.3
  25.1 6.5 %all-to-all-done.a = bf16[32,2,16,512]{3,2,1,0:T(8,128)(2,1)S(1)} async-done(((bf16[32,2,16,512]{3,2,1,0:T(8,128)(2,1)}), bf16[32,2,16,512]{3,2,1,0:T(8,128)(2,1)S(1)}, u32[]{:S(2)}, u32[]{:S(2)}) %all-to-all-start) | async-done | bytes 1048608 | tf_op jit(solution)/shard_map/all_to_all | solution.py:261
  31.6 0.7 outgoing.1
  32.3 19.6 %all_to_all.20.y = bf16[128,16,128]{2,1,0:T(8,128)(2,1)S(1)} all-to-all(bf16[128,16,128]{2,1,0:T(8,128)(2,1)S(1)} %bitcast.6), channel_id=1, replica_groups=mesh['row'=32,'ch'=4] {'ch','row'}, dimensions={0} | all-to-all | bytes 1048576 | tf_op jit(solution)/shard_map/all_to_all | solution.py:286
  52.0 0.9 copy-done.2
  52.9 0.9 copy-done.4
  53.8 2.1 %middle.1 = (f32[16,128,128]{2,1,0:T(8,128)S(1)}, bf16[16,128,128]{2,1,0:T(8,128)(2,1)S(1)}, bf16[128,2,16,128]{3,2,1,0:T(8,128)(2,1)S(1)}) custom-call(bf16[128,16,128]{2,1,0:T(8,128)(2,1)S(1)} %all_to_all.20.y, f32[16,128,128]{2,1,0:T(8,128)S(1)} %get-tuple-element.37.z0, f32[16,128,128]{2,1,0:T(8,128)S(1)} %get-tuple-element.38.gate, ...), custom_call_target="tpu_custom_call" | custom-call | tf_op jit(solution)/shard_map/middle/pallas_call | solution.py:219
  55.9 23.7 %all_to_all.21.b = bf16[128,2,16,128]{3,2,1,0:T(8,128)(2,1)S(1)} all-to-all(bf16[128,2,16,128]{3,2,1,0:T(8,128)(2,1)S(1)} %get-tuple-element.44), channel_id=1, replica_groups=mesh['row'=32,'ch'=4] {'ch','row'}, dimensions={0} | all-to-all | bytes 2097152 | tf_op jit(solution)/shard_map/all_to_all | solution.py:294
  79.6 0.7 incoming.1
  80.4 18.0 %all_to_all.22.y = bf16[128,16,128]{2,1,0:T(8,128)(2,1)S(1)} all-to-all(bf16[128,16,128]{2,1,0:T(8,128)(2,1)S(1)} %bitcast.7), channel_id=1, replica_groups=mesh['row'=32,'ch'=4] {'ch','row'}, dimensions={0} | all-to-all | bytes 1048576 | tf_op jit(solution)/shard_map/all_to_all | solution.py:296
  98.3 1.2 last.1
  99.5 0.6 collective-permute-start.3
  100.1 2.7 %collective-permute-start.5 = (bf16[8,128,128]{2,1,0:T(8,128)(2,1)S(1)}, bf16[8,128,128]{2,1,0:T(8,128)(2,1)S(1)}, u32[]{:S(2)}, u32[]{:S(2)}) collective-permute-start(bf16[8,128,128]{2,1,0:T(8,128)(2,1)S(1)} %get-tuple-element.48.own1), channel_id=1, source_target_pairs={{0,3},{1,0},{2,1},{3,2},{4,7},{5,4},{6,5},{7,6},{8,11},{9,8},{10,9... | collective-permute-start | bytes 786440 | tf_op jit(solution)/shard_map/ppermute | solution.py:305
  102.8 0.0 collective-permute-start.8
  102.8 2.0 %collective-permute-start.7 = (bf16[8,128,128]{2,1,0:T(8,128)(2,1)S(1)}, bf16[8,128,128]{2,1,0:T(8,128)(2,1)S(1)}, u32[]{:S(2)}, u32[]{:S(2)}) collective-permute-start(bf16[8,128,128]{2,1,0:T(8,128)(2,1)S(1)} %get-tuple-element.48.own1), channel_id=1, source_target_pairs={{0,1},{1,2},{2,3},{3,0},{4,5},{5,6},{6,7},{7,4},{8,9},{9,10},{10,1... | collective-permute-start | bytes 786440 | tf_op jit(solution)/shard_map/ppermute | solution.py:306
  104.8 5.2 %collective-permute-done.3.up0 = bf16[8,128,128]{2,1,0:T(8,128)(2,1)S(1)} collective-permute-done((bf16[8,128,128]{2,1,0:T(8,128)(2,1)S(1)}, bf16[8,128,128]{2,1,0:T(8,128)(2,1)S(1)}, u32[]{:S(2)}, u32[]{:S(2)}) %collective-permute-start.3) | collective-permute-done | bytes 262176 | tf_op jit(solution)/shard_map/ppermute | solution.py:305
  110.0 0.0 collective-permute-start.4
  110.0 3.2 %collective-permute-start.6 = (bf16[8,128,128]{2,1,0:T(8,128)(2,1)S(1)}, bf16[8,128,128]{2,1,0:T(8,128)(2,1)S(1)}, u32[]{:S(2)}, u32[]{:S(2)}) collective-permute-start(bf16[8,128,128]{2,1,0:T(8,128)(2,1)S(1)} %collective-permute-done.5.down1), channel_id=1, source_target_pairs={{0,3},{1,0},{2,1},{3,2},{4,7},{5,4},{6,5},{7,6},{8,11},{9,8},{10,9... | collective-permute-start | bytes 786440 | tf_op jit(solution)/shard_map/ppermute | solution.py:307
  113.2 1.9 %collective-permute-done.8.down0 = bf16[8,128,128]{2,1,0:T(8,128)(2,1)S(1)} collective-permute-done((bf16[8,128,128]{2,1,0:T(8,128)(2,1)S(1)}, bf16[8,128,128]{2,1,0:T(8,128)(2,1)S(1)}, u32[]{:S(2)}, u32[]{:S(2)}) %collective-permute-start.8) | collective-permute-done | bytes 262176 | tf_op jit(solution)/shard_map/ppermute | solution.py:306
  115.2 0.5 collective-permute-done.7.up1
  115.6 1.8 %spread_near.1._ = f32[16,512,128]{2,1,0:T(8,128)} custom-call(bf16[8,128,128]{2,1,0:T(8,128)(2,1)S(1)} %get-tuple-element.47.own0, bf16[8,128,128]{2,1,0:T(8,128)(2,1)S(1)} %get-tuple-element.48.own1, bf16[8,128,128]{2,1,0:T(8,128)(2,1)S(1)} %collective-permute-done.3.up0, bf16[8,128,128]{2,1,0:T(8,128)(2,1)S(1)} %collective-permute-done.7.up1, ...), custom_call_target="tpu_custom_call" | custom-call | tf_op jit(solution)/shard_map/spread_near/pallas_call | solution.py:309
  117.4 2.2 %collective-permute-done.4.far0 = bf16[8,128,128]{2,1,0:T(8,128)(2,1)S(1)} collective-permute-done((bf16[8,128,128]{2,1,0:T(8,128)(2,1)S(1)}, bf16[8,128,128]{2,1,0:T(8,128)(2,1)S(1)}, u32[]{:S(2)}, u32[]{:S(2)}) %collective-permute-start.4) | collective-permute-done | bytes 262176 | tf_op jit(solution)/shard_map/ppermute | solution.py:307
  119.6 1.0 spread_far.1
  (18 shorter events, 0.0 us)
Async XLA Ops:
  0.0 19.4 %copy-start.8 = (f32[2,128]{1,0:T(2,128)S(1)}, f32[2,128]{1,0:T(2,128)}, u32[]{:S(2)}) copy-start(f32[2,128]{1,0:T(2,128)} %in_bias.3) | copy-start | bytes 3076
  0.0 19.4 %copy-start.7 = (f32[2,128]{1,0:T(2,128)S(1)}, f32[2,128]{1,0:T(2,128)}, u32[]{:S(2)}) copy-start(f32[2,128]{1,0:T(2,128)} %in_gain.3) | copy-start | bytes 3076
  0.0 19.4 %copy-start.6 = (s32[512]{0:T(512)S(1)}, s32[512]{0:T(512)}, u32[]{:S(2)}) copy-start(s32[512]{0:T(512)} %param.10) | copy-start | bytes 6148
  0.0 19.4 %copy-start = (bf16[2,128,128]{2,1,0:T(8,128)(2,1)S(1)}, bf16[2,128,128]{2,1,0:T(8,128)(2,1)}, u32[]{:S(2)}) copy-start(bf16[2,128,128]{2,1,0:T(8,128)(2,1)} %w_gate.3) | copy-start | bytes 196612
  5.8 25.8 %all-to-all-start = ((bf16[32,2,16,512]{3,2,1,0:T(8,128)(2,1)}), bf16[32,2,16,512]{3,2,1,0:T(8,128)(2,1)S(1)}, u32[]{:S(2)}, u32[]{:S(2)}) async-start(bf16[32,2,16,512]{3,2,1,0:T(8,128)(2,1)} %get-tuple-element.27), calls=%async_computation | async-start | bytes 2097152 | tf_op jit(solution)/shard_map/all_to_all | solution.py:261
  14.3 9.8 %copy-start.5 = (bf16[208,128]{1,0:T(8,128)(2,1)S(1)}, bf16[208,128]{1,0:T(8,128)(2,1)}, u32[]{:S(2)}) copy-start(bf16[208,128]{1,0:T(8,128)(2,1)} %get-tuple-element.32.own) | copy-start | bytes 159748
  14.3 7.8 %collective-permute-start.2 = (bf16[208,128]{1,0:T(8,128)(2,1)}, bf16[208,128]{1,0:T(8,128)(2,1)S(1)}, u32[]{:S(2)}, u32[]{:S(2)}) collective-permute-start(bf16[208,128]{1,0:T(8,128)(2,1)} %get-tuple-element.32.own), channel_id=1, source_target_pairs={{0,2},{1,3},{2,0},{3,1},{4,6},{5,7},{6,4},{7,5},{8,10},{9,11},{10,... | collective-permute-start | bytes 159752 | tf_op jit(solution)/shard_map/ppermute | solution.py:267
  17.4 4.7 %collective-permute-start.1 = (bf16[208,128]{1,0:T(8,128)(2,1)}, bf16[208,128]{1,0:T(8,128)(2,1)S(1)}, u32[]{:S(2)}, u32[]{:S(2)}) collective-permute-start(bf16[208,128]{1,0:T(8,128)(2,1)} %get-tuple-element.32.own), channel_id=1, source_target_pairs={{0,3},{1,0},{2,1},{3,2},{4,7},{5,4},{6,5},{7,6},{8,11},{9,8},{10,9... | collective-permute-start | bytes 159752 | tf_op jit(solution)/shard_map/ppermute | solution.py:267
  18.5 5.6 %collective-permute-start = (bf16[208,128]{1,0:T(8,128)(2,1)}, bf16[208,128]{1,0:T(8,128)(2,1)S(1)}, u32[]{:S(2)}, u32[]{:S(2)}) collective-permute-start(bf16[208,128]{1,0:T(8,128)(2,1)} %get-tuple-element.32.own), channel_id=1, source_target_pairs={{0,1},{1,2},{2,3},{3,0},{4,5},{5,6},{6,7},{7,4},{8,9},{9,10},{10,1... | collective-permute-start | bytes 159752 | tf_op jit(solution)/shard_map/ppermute | solution.py:267
  21.4 0.6 copy-start.1
  24.5 0.7 copy-start.3
  52.0 0.9 copy-start.2
  52.9 0.9 copy-start.4
  99.5 10.5 %collective-permute-start.3 = (bf16[8,128,128]{2,1,0:T(8,128)(2,1)S(1)}, bf16[8,128,128]{2,1,0:T(8,128)(2,1)S(1)}, u32[]{:S(2)}, u32[]{:S(2)}) collective-permute-start(bf16[8,128,128]{2,1,0:T(8,128)(2,1)S(1)} %get-tuple-element.47.own0), channel_id=1, source_target_pairs={{0,1},{1,2},{2,3},{3,0},{4,5},{5,6},{6,7},{7,4},{8,9},{9,10},{10,1... | collective-permute-start | bytes 786440 | tf_op jit(solution)/shard_map/ppermute | solution.py:305
  100.1 9.9 %collective-permute-start.5 = (bf16[8,128,128]{2,1,0:T(8,128)(2,1)S(1)}, bf16[8,128,128]{2,1,0:T(8,128)(2,1)S(1)}, u32[]{:S(2)}, u32[]{:S(2)}) collective-permute-start(bf16[8,128,128]{2,1,0:T(8,128)(2,1)S(1)} %get-tuple-element.48.own1), channel_id=1, source_target_pairs={{0,3},{1,0},{2,1},{3,2},{4,7},{5,4},{6,5},{7,6},{8,11},{9,8},{10,9... | collective-permute-start | bytes 786440 | tf_op jit(solution)/shard_map/ppermute | solution.py:305
  102.8 12.4 %collective-permute-start.8 = (bf16[8,128,128]{2,1,0:T(8,128)(2,1)S(1)}, bf16[8,128,128]{2,1,0:T(8,128)(2,1)S(1)}, u32[]{:S(2)}, u32[]{:S(2)}) collective-permute-start(bf16[8,128,128]{2,1,0:T(8,128)(2,1)S(1)} %get-tuple-element.47.own0), channel_id=1, source_target_pairs={{0,3},{1,0},{2,1},{3,2},{4,7},{5,4},{6,5},{7,6},{8,11},{9,8},{10,9... | collective-permute-start | bytes 786440 | tf_op jit(solution)/shard_map/ppermute | solution.py:306
  102.8 12.8 %collective-permute-start.7 = (bf16[8,128,128]{2,1,0:T(8,128)(2,1)S(1)}, bf16[8,128,128]{2,1,0:T(8,128)(2,1)S(1)}, u32[]{:S(2)}, u32[]{:S(2)}) collective-permute-start(bf16[8,128,128]{2,1,0:T(8,128)(2,1)S(1)} %get-tuple-element.48.own1), channel_id=1, source_target_pairs={{0,1},{1,2},{2,3},{3,0},{4,5},{5,6},{6,7},{7,4},{8,9},{9,10},{10,1... | collective-permute-start | bytes 786440 | tf_op jit(solution)/shard_map/ppermute | solution.py:306
  110.0 9.6 %collective-permute-start.4 = (bf16[8,128,128]{2,1,0:T(8,128)(2,1)S(1)}, bf16[8,128,128]{2,1,0:T(8,128)(2,1)S(1)}, u32[]{:S(2)}, u32[]{:S(2)}) collective-permute-start(bf16[8,128,128]{2,1,0:T(8,128)(2,1)S(1)} %collective-permute-done.3.up0), channel_id=1, source_target_pairs={{0,1},{1,2},{2,3},{3,0},{4,5},{5,6},{6,7},{7,4},{8,9},{9,10},{10,1... | collective-permute-start | bytes 786440 | tf_op jit(solution)/shard_map/ppermute | solution.py:307
  110.0 9.6 %collective-permute-start.6 = (bf16[8,128,128]{2,1,0:T(8,128)(2,1)S(1)}, bf16[8,128,128]{2,1,0:T(8,128)(2,1)S(1)}, u32[]{:S(2)}, u32[]{:S(2)}) collective-permute-start(bf16[8,128,128]{2,1,0:T(8,128)(2,1)S(1)} %collective-permute-done.5.down1), channel_id=1, source_target_pairs={{0,3},{1,0},{2,1},{3,2},{4,7},{5,4},{6,5},{7,6},{8,11},{9,8},{10,9... | collective-permute-start | bytes 786440 | tf_op jit(solution)/shard_map/ppermute | solution.py:307

commit v4 on v3

--- a/solution.py
+++ b/solution.py
@@ -45,55 +45,53 @@
 
 
 def project0_kernel(
-    pair, mask, in_gain, in_bias, w, w_out, out_gain, out_bias, out, own,
-    rows, mask_v, mask_s, gb, w_v, wo_v, og_v, left_s, right_s, zn_s, sems,
+    pair, mask, in_gain, in_bias, w, out,
+    rows, mask_v, mask_s, gb, w_v, left_s, right_s, zn_s, stage, sems,
 ):
-    small = [
-        (mask, mask_v),
-        (mask, mask_s),
-        (in_gain, gb.at[0]),
-        (in_bias, gb.at[1]),
-        (w, w_v),
-        (w_out, wo_v),
-        (out_gain, og_v.at[0]),
-        (out_bias, og_v.at[1]),
-    ]
+    small = [(in_gain, gb.at[0]), (in_bias, gb.at[1]), (w.at[0], w_v), (mask, mask_v), (mask, mask_s)]
     big = [(pair.at[:, pl.ds(T * h, T)], rows.at[h]) for h in range(G)]
     copies = [pltpu.make_async_copy(*ends, sems.at[k]) for k, ends in enumerate(small + big)]
     few = len(small)
-    for copy in copies[few : few + 1] + copies[:few] + copies[few + 1 :]:
+    for copy in copies[:2] + copies[few : few + 1] + copies[2:few] + copies[few + 1 :]:
         copy.start()
-    for copy in copies[:few]:
+    for copy in copies[:2]:
         copy.wait()
     gain, bias = column(gb[0, 0:1, :]), column(gb[1, 0:1, :])
-    cols = mask_v[...].astype(F32) * 0.5
     row0 = lax.axis_index("row") * RB
-
-    own[:PK_OUT] = w_v[1]
-    own[PK_OUT:PK_NORM] = wo_v[...].reshape(2 * D, C)
-    norms = jnp.concatenate([og_v[0], og_v[1]], 0)
-    hi = norms.astype(BF16).astype(F32)
-    mid = (norms - hi).astype(BF16).astype(F32)
-    low = norms - hi - mid
-    tile = jnp.concatenate([hi, mid, low, jnp.zeros_like(hi)], 0)
-    own[PK_NORM:] = jnp.concatenate([tile, jnp.zeros((16, C - D), F32)], 1).astype(BF16)
-
-    for h in range(G):
-        copies[few + h].wait()
-        for i in range(RB):
-            zn_s[h, i] = norm_cols(rows[h, i].T, gain, bias).astype(BF16)
+    cols = None
+    for h in range(G + 1):
+        if h < G:
+            copies[few + h].wait()
+        if h == 1:
+            for copy in copies[2:few]:
+                copy.wait()
+            cols = mask_v[...].astype(F32) * 0.5
         for i in range(0, RB, 2):
-            proj = dot(w_v[0], jnp.concatenate([zn_s[h, i], zn_s[h, i + 1]], 1))
-            for k in (0, 1):
-                half = cols[:, T * h : T * h + T] * mask_s[0, row0 + i + k].astype(F32)
-                part = proj[:, T * k : T * k + T]
-                left_s[h, pl.ds(i + k, D, stride=RB), :] = gated(part[0:D], part[D : 2 * D], half)
-                right_s[h, pl.ds(i + k, D, stride=RB), :] = gated(part[2 * D : 3 * D], part[3 * D :], half)
-        out[:, 0, :, T * h : T * h + T] = left_s[h].reshape(D, RB, T).astype(BF16)
-        out[:, 1, :, T * h : T * h + T] = right_s[h].reshape(D, RB, T).astype(BF16)
-
-
-def gate0_kernel(pair, mask, in_gain, in_bias, w_gate, state, gate, half, in_norm, block, mask_v, mask_s, sems):
+            if h < G:
+                for k in (0, 1):
+                    zn_s[h, i + k] = norm_cols(rows[h, i + k].T, gain, bias).astype(BF16)
+            if h > 0:
+                e = h - 1
+                proj = dot(w_v[...], jnp.concatenate([zn_s[e, i], zn_s[e, i + 1]], 1))
+                for k in (0, 1):
+                    half = cols[:, T * e : T * e + T] * mask_s[0, row0 + i + k].astype(F32)
+                    part = proj[:, T * k : T * k + T]
+                    left_s[e, pl.ds(i + k, D, stride=RB), :] = gated(part[0:D], part[D : 2 * D], half)
+                    right_s[e, pl.ds(i + k, D, stride=RB), :] = gated(part[2 * D : 3 * D], part[3 * D :], half)
+        if h > 0:
+            stage[e, :, 0] = left_s[e].reshape(D, RB, T).astype(BF16)
+            stage[e, :, 1] = right_s[e].reshape(D, RB, T).astype(BF16)
+            copies.append(
+                pltpu.make_async_copy(stage.at[e], out.at[:, :, :, pl.ds(T * e, T)], sems.at[few + G + e])
+            )
+            copies[-1].start()
+    for copy in copies[few + G :]:
+        copy.wait()
+
+
+def gate0_kernel(
+    pair, mask, in_gain, in_bias, w_gate, w, w_out, out_gain, out_bias, state, gate, half, own, block, mask_v, mask_s, sems
+):
     at = pl.multiple_of(lax.axis_index("ch") * T, T)
     copies = [
         pltpu.make_async_copy(pair.at[:, pl.ds(at, T), :], block, sems.at[0]),
@@ -102,9 +100,15 @@
     ]
     for copy in copies:
         copy.start()
+    own[:PK_OUT] = w[1]
+    own[PK_OUT:PK_NORM] = w_out[...].reshape(2 * D, C)
+    norms = jnp.concatenate([out_gain[...], out_bias[...]], 0)
+    hi = norms.astype(BF16).astype(F32)
+    mid = (norms - hi).astype(BF16).astype(F32)
+    low = norms - hi - mid
+    tile = jnp.concatenate([hi, mid, low, jnp.zeros_like(hi)], 0)
+    own[PK_NORM:] = jnp.concatenate([tile, jnp.zeros((16, C - D), F32)], 1).astype(BF16)
     gain, bias = column(in_gain[0:1, :]), column(in_bias[0:1, :])
-    in_norm[0] = column(in_gain[1:2, :])
-    in_norm[1] = column(in_bias[1:2, :])
     w_g = w_gate[0].astype(F32).T.astype(BF16)
     for copy in copies:
         copy.wait()
@@ -116,14 +120,14 @@
         gate[i] = sigmoid(dot(w_g, norm_cols(z, gain, bias).astype(BF16)))
 
 
-def weights_kernel(own, up, down, far, w_proj, w_out, norms, pk):
+def weights_kernel(own, up, down, far, in_gain, in_bias, w, norms, pk):
     g = lax.axis_index("ch")
     pk[g] = own[...]
     pk[lax.rem(g + 3, G)] = up[...]
     pk[lax.rem(g + 1, G)] = down[...]
     pk[lax.rem(g + 2, G)] = far[...]
     for k in range(G):
-        w_proj[k] = pk[k, PK_PROJ : PK_PROJ + C]
+        w[k] = pk[k, PK_PROJ : PK_PROJ + C]
     for k in range(G):
         parts = pk[k, PK_NORM:].astype(F32)
         parts = parts[0:4] + parts[4:8] + parts[8:12]
@@ -133,7 +137,9 @@
         rows = jnp.concatenate(
             [pk[k, PK_OUT + D * layer : PK_OUT + D * (layer + 1)] for k in range(G)], 0
         )
-        w_out[layer] = rows.astype(F32).T.astype(BF16)
+        w[G + layer] = rows.astype(F32).T.astype(BF16)
+    norms[4] = column(in_gain[1:2, :])
+    norms[5] = column(in_bias[1:2, :])
 
 
 def outgoing_kernel(a, out):
@@ -151,19 +157,19 @@
 
 
 def middle_kernel(
-    y, z0, gate, half_mask, in_norm, w_proj, w_out, norms, state, normed, out, ys, left_s, right_s, hid
+    y, z0, gate, half_mask, w, norms, state, normed, out, ys, left_s, right_s, hid
 ):
     ys[...] = y[...].astype(F32).reshape(C * RB, T)
     for i in range(RB):
         hid[i] = norm_cols(ys[pl.ds(i, C, stride=RB), :], norms[0], norms[2]).astype(BF16)
     for i in range(RB):
-        z = z0[i] + gate[i] * dot(w_out[0], hid[i])
+        z = z0[i] + gate[i] * dot(w[G], hid[i])
         state[i] = z
-        normed[i] = norm_cols(z, in_norm[0], in_norm[1]).astype(BF16)
+        normed[i] = norm_cols(z, norms[4], norms[5]).astype(BF16)
     for g in range(G):
         for i in range(0, RB, 2):
             half = jnp.concatenate([half_mask[i : i + 1, :], half_mask[i + 1 : i + 2, :]], 1)
-            proj = dot(w_proj[g], jnp.concatenate([normed[i], normed[i + 1]], 1))
+            proj = dot(w[g], jnp.concatenate([normed[i], normed[i + 1]], 1))
             left = gated(proj[0:D], proj[D : 2 * D], half)
             right = gated(proj[2 * D : 3 * D], proj[3 * D :], half)
             for k in (0, 1):
@@ -174,13 +180,13 @@
     out[:, 1] = right_s[...].reshape(C, RB, T).astype(BF16)
 
 
-def last_kernel(y, state, normed, w_gate, w_out, norms, out0, out1, ys):
+def last_kernel(y, state, normed, w_gate, w, norms, out0, out1, ys):
     w_g = w_gate[1].astype(F32).T.astype(BF16)
     ys[...] = y[...].astype(F32).reshape(C * RB, T)
     for i in range(RB):
         hidden = norm_cols(ys[pl.ds(i, C, stride=RB), :], norms[1], norms[3]).astype(BF16)
         gate = sigmoid(dot(w_g, normed[i]))
-        z = state[i] + gate * dot(w_out[1], hidden)
+        z = state[i] + gate * dot(w[G + 1], hidden)
         out = (out0, out1)[i // HB]
         out[i % HB] = z.T.astype(BF16)
 
@@ -215,12 +221,12 @@
     return pltpu.CompilerParams(vmem_limit_bytes=limit)
 
 
-def call(kernel, name, outs, scratch, ins, limit=VMEM_LIMIT):
+def call(kernel, name, outs, scratch, ins, limit=VMEM_LIMIT, out_space=None):
     return pl.pallas_call(
         kernel,
         out_shape=outs,
         in_specs=[pl.BlockSpec(memory_space=space) for _, space in ins],
-        out_specs=jax.tree.map(lambda _: pl.BlockSpec(memory_space=VMEM), outs),
+        out_specs=jax.tree.map(lambda _: pl.BlockSpec(memory_space=out_space or VMEM), outs),
         scratch_shapes=scratch,
         compiler_params=params(limit),
         name=name,
@@ -233,54 +239,53 @@
     w_t = jnp.transpose(w_proj, (0, 2, 3, 1)).reshape(2, 4 * D, C)
     dma = pltpu.SemaphoreType.DMA
 
-    a, own = call(
+    a = call(
         project0_kernel,
         "project0",
-        (arr((D, 2, RB, N), BF16), arr((PK, C), BF16)),
+        arr((D, 2, RB, N), BF16),
         [
             pltpu.VMEM((G, RB, T, C), F32),
             pltpu.VMEM((1, N), jnp.int32),
             pltpu.SMEM((1, N), jnp.int32),
             pltpu.VMEM((2, 2, C), F32),
-            pltpu.VMEM((2, 4 * D, C), BF16),
-            pltpu.VMEM((2, D, C), BF16),
-            pltpu.VMEM((2, 2, D), F32),
+            pltpu.VMEM((4 * D, C), BF16),
             pltpu.VMEM((G, D * RB, T), F32),
             pltpu.VMEM((G, D * RB, T), F32),
             pltpu.VMEM((G, RB, C, T), BF16),
-            dma((8 + G,)),
+            pltpu.VMEM((G, D, 2, RB, T), BF16),
+            dma((5 + 2 * G,)),
         ],
-        [(v, HBM) for v in (pair, mask, in_gain, in_bias, w_t, w_out, out_gain, out_bias)],
+        [(v, HBM) for v in (pair, mask, in_gain, in_bias, w_t)],
         WHOLE_VMEM,
+        HBM,
     )
 
     up = functools.partial(lax.ppermute, axis_name="ch", perm=[(k, (k + 1) % G) for k in range(G)])
     down = functools.partial(lax.ppermute, axis_name="ch", perm=[(k, (k - 1) % G) for k in range(G)])
     cross = functools.partial(lax.ppermute, axis_name="ch", perm=[(k, (k + 2) % G) for k in range(G)])
 
-    a = lax.all_to_all(a, "row", 0, 0)
-    w_proj1, w_out_t, norms = call(
-        weights_kernel,
-        "weights",
-        (arr((G, C, C), BF16), arr((2, C, C), BF16), arr((4, C, T), F32)),
-        [pltpu.VMEM((G, PK, C), BF16)],
-        [(v, VMEM) for v in (own, up(own), down(own), cross(own))],
-    )
-    state, gate, half_mask, in_norm = call(
+    sent = lax.all_to_all(a, "row", 0, 0)
+    state, gate, half_mask, own = call(
         gate0_kernel,
         "gate0",
-        (arr((RB, C, T), F32), arr((RB, C, T), F32), arr((RB, T), F32), arr((2, C, T), F32)),
+        (arr((RB, C, T), F32), arr((RB, C, T), F32), arr((RB, T), F32), arr((PK, C), BF16)),
         [
             pltpu.VMEM((RB, T, C), F32),
             pltpu.VMEM((1, T), jnp.int32),
             pltpu.SMEM((1, N), jnp.int32),
             dma((3,)),
         ],
-        [(pair, HBM), (mask, HBM), (in_gain, VMEM), (in_bias, VMEM), (w_gate, VMEM)],
+        [(pair, HBM), (mask, HBM)]
+        + [(v, VMEM) for v in (in_gain, in_bias, w_gate, w_t, w_out, out_gain, out_bias)],
         MOST_VMEM,
     )
-    a, state, gate, half_mask, in_norm, w_proj1, w_out_t, norms = lax.optimization_barrier(
-        (a, state, gate, half_mask, in_norm, w_proj1, w_out_t, norms)
+    a, state, gate, half_mask, own = lax.optimization_barrier((sent, state, gate, half_mask, own))
+    w, norms = call(
+        weights_kernel,
+        "weights",
+        (arr((G + 2, C, C), BF16), arr((6, C, T), F32)),
+        [pltpu.VMEM((G, PK, C), BF16)],
+        [(v, VMEM) for v in (own, up(own), down(own), cross(own), in_gain, in_bias)],
     )
     x = call(outgoing_kernel, "outgoing", arr((G, R, RB, T), BF16), [], [(a, VMEM)])
     y = lax.all_to_all(x.reshape(G * R, RB, T), ("ch", "row"), 0, 0)
@@ -289,7 +294,7 @@
         "middle",
         (arr((RB, C, T), F32), arr((RB, C, T), BF16), arr((C, 2, RB, T), BF16)),
         [pltpu.VMEM((C * RB, T), F32)] * 3 + [pltpu.VMEM((RB, C, T), BF16)],
-        [(v, VMEM) for v in (y, state, gate, half_mask, in_norm, w_proj1, w_out_t, norms)],
+        [(v, VMEM) for v in (y, state, gate, half_mask, w, norms)],
     )
     b = lax.all_to_all(b, ("ch", "row"), 0, 0)
     x = call(incoming_kernel, "incoming", arr((G, R, RB, T), BF16), [], [(b, VMEM)])
@@ -300,7 +305,7 @@
         "last",
         (half, half),
         [pltpu.VMEM((C * RB, T), F32)],
-        [(v, VMEM) for v in (y, state, normed, w_gate, w_out_t, norms)],
+        [(v, VMEM) for v in (y, state, normed, w_gate, w, norms)],
     )
     up0, down1 = up(z0), down(z1)
     up1, down0 = up(z1), down(z0)

time: 121 us -> 121 us (level)
  blocking collectives: 61.3 us -> 42 us
  waiting for transfers between devices: 18.3 us -> 34.6 us
  starting transfers between devices: 22.1 us -> 27.9 us
  local copies, waits for them, and re-layouts: 3.11 us -> 0.03 us
    all_to_all x2 -> x1, blocking collectives: 37.6 us -> 18 us  [on_device(): y = lax.all_to_all(x.reshape(G * R, RB, T), ('ch', 'row'), 0, 0)]
    all_to_all x1 -> x2, waiting for transfers between devices: 6.47 us -> 19 us  [the longest x1 15.3 us: on_device(): sent = lax.all_to_all(a, 'row', 0, 0)]
    all_to_all x1 -> x2, starting transfers between devices: 8.44 us -> 14.7 us  [the longest x1 8.42 us: on_device(): sent = lax.all_to_all(a, 'row', 0, 0)]
    ppermute x1, waiting for transfers between devices: 0.01 us -> 5.46 us  [on_device(): cross(own)]
    unnamed x18 -> x16, local copies, waits for them, and re-layouts: 3.11 us -> 0.03 us
    ppermute x1, waiting for transfers between devices: 2.04 us -> 0.37 us  [on_device(): up(own)]
  transfers between devices with their start and end apart: 10 -> 11, of which waited for: 6 -> 8; matrix products, arithmetic and copies ran while one was open for 0% -> 0% of each run, Pallas kernels for 3% -> 3%
where the time goes in v4:
time: 121 us
  blocking collectives  42 us (35%)
  waiting for transfers between devices  34.6 us (29%)
  starting transfers between devices  27.9 us (23%)
  Pallas kernels  16.1 us (13%)
    all_to_all x1, blocking collectives, on_device(): b = lax.all_to_all(b, ('ch', 'row'), 0, 0)  24.1 us
    all_to_all x1, blocking collectives, on_device(): y = lax.all_to_all(x.reshape(G * R, RB, T), ('ch', 'row'), 0, 0)  18 us
    all_to_all x1, waiting for transfers between devices, on_device(): sent = lax.all_to_all(a, 'row', 0, 0)  15.3 us
    pallas_call x7, Pallas kernels, call(): pl.pallas_call(kernel, out_shape=outs, in_specs=[pl.BlockSpec(memory_spac...  13.3 us
    all_to_all x1, starting transfers between devices, on_device(): sent = lax.all_to_all(a, 'row', 0, 0)  8.42 us
    all_to_all x1, starting transfers between devices, on_device(): y = lax.all_to_all(x.reshape(G * R, RB, T), ('ch', 'row'), 0, 0)  6.29 us
    ppermute x1, waiting for transfers between devices, on_device(): cross(own)  5.46 us
    ppermute x2, waiting for transfers between devices, on_device(): up0, down1 = (up(z0), down(z1))  5.19 us
  transfers between devices with their start and end apart: 11, of which 8 were waited for; matrix products, arithmetic and copies ran while one was open for 0% of the time, Pallas kernels for 3%

profile of v4, /device:TPU:0, one launch (start us, length us, event | category | flops | bytes accessed | tf_op | source)
XLA Modules:
  0.0 120.8 jit_solution(6857823988822438879)
XLA Ops:
  0.0 5.2 %project0.1 = bf16[32,2,16,512]{3,2,1,0:T(8,128)(2,1)} custom-call(f32[16,512,128]{2,1,0:T(8,128)} %pair.3, s32[1,512]{1,0:T(1,128)} %bitcast.9, f32[2,128]{1,0:T(2,128)} %in_gain.5, f32[2,128]{1,0:T(2,128)} %in_bias.5, bf16[2,128,128]{2,1,0:T(8,128)(2,1)} %bitcast.7), custom_call_target="tpu_custom_call" | custom-call | tf_op jit(solution)/shard_map/project0/pallas_call | solution.py:225
  5.2 8.4 %all-to-all-start = ((bf16[32,2,16,512]{3,2,1,0:T(8,128)(2,1)}), bf16[32,2,16,512]{3,2,1,0:T(8,128)(2,1)S(1)}, u32[]{:S(2)}, u32[]{:S(2)}) async-start(bf16[32,2,16,512]{3,2,1,0:T(8,128)(2,1)} %project0.1), calls=%async_computation | async-start | bytes 2097152 | tf_op jit(solution)/shard_map/all_to_all | solution.py:267
  13.7 2.0 %gate0.1 = (f32[16,128,128]{2,1,0:T(8,128)S(1)}, f32[16,128,128]{2,1,0:T(8,128)S(1)}, f32[16,128]{1,0:T(8,128)S(1)}, bf16[208,128]{1,0:T(8,128)(2,1)S(1)}) custom-call(f32[16,512,128]{2,1,0:T(8,128)} %pair.3, s32[1,512]{1,0:T(1,128)S(1)} %bitcast.10, f32[2,128]{1,0:T(2,128)S(1)} %copy-done.3, f32[2,128]{1,0:T(2,128)S(1)} %copy-done.4, ...), custom_call_target="tpu_custom_call" | custom-call | tf_op jit(solution)/shard_map/gate0/pallas_call | solution.py:225
  15.7 15.3 %all-to-all-done.a = bf16[32,2,16,512]{3,2,1,0:T(8,128)(2,1)S(1)} async-done(((bf16[32,2,16,512]{3,2,1,0:T(8,128)(2,1)}), bf16[32,2,16,512]{3,2,1,0:T(8,128)(2,1)S(1)}, u32[]{:S(2)}, u32[]{:S(2)}) %all-to-all-start) | async-done | bytes 1048608 | tf_op jit(solution)/shard_map/all_to_all | solution.py:267
  31.0 1.5 %outgoing.1 = bf16[4,32,16,128]{3,2,1,0:T(8,128)(2,1)} custom-call(bf16[32,2,16,512]{3,2,1,0:T(8,128)(2,1)S(1)} %all-to-all-done.a), custom_call_target="tpu_custom_call" | custom-call | tf_op jit(solution)/shard_map/outgoing/pallas_call | solution.py:225
  32.5 6.3 %all-to-all-start.1 = ((bf16[128,16,128]{2,1,0:T(8,128)(2,1)}), bf16[128,16,128]{2,1,0:T(8,128)(2,1)S(1)}, u32[]{:S(2)}, u32[]{:S(2)}) async-start(bf16[128,16,128]{2,1,0:T(8,128)(2,1)} %bitcast.4), calls=%async_computation.1 | async-start | bytes 1048576 | tf_op jit(solution)/shard_map/all_to_all | solution.py:291
  38.8 2.5 %collective-permute-start.2 = (bf16[208,128]{1,0:T(8,128)(2,1)S(1)}, bf16[208,128]{1,0:T(8,128)(2,1)S(1)}, u32[]{:S(2)}, u32[]{:S(2)}) collective-permute-start(bf16[208,128]{1,0:T(8,128)(2,1)S(1)} %get-tuple-element.29.own), channel_id=1, source_target_pairs={{0,2},{1,3},{2,0},{3,1},{4,6},{5,7},{6,4},{7,5},{8,10},{9,11},{10,... | collective-permute-start | bytes 159752 | tf_op jit(solution)/shard_map/ppermute | solution.py:288
  41.3 1.2 collective-permute-start.1
  42.5 0.9 collective-permute-start
  43.4 5.5 %collective-permute-done.2.far = bf16[208,128]{1,0:T(8,128)(2,1)S(1)} collective-permute-done((bf16[208,128]{1,0:T(8,128)(2,1)S(1)}, bf16[208,128]{1,0:T(8,128)(2,1)S(1)}, u32[]{:S(2)}, u32[]{:S(2)}) %collective-permute-start.2) | collective-permute-done | bytes 53280 | tf_op jit(solution)/shard_map/ppermute | solution.py:288
  48.8 0.0 collective-permute-done.1.down
  48.8 0.4 collective-permute-done.up
  49.2 0.4 weights.1
  49.6 3.7 %all-to-all-done.1.y = bf16[128,16,128]{2,1,0:T(8,128)(2,1)S(1)} async-done(((bf16[128,16,128]{2,1,0:T(8,128)(2,1)}), bf16[128,16,128]{2,1,0:T(8,128)(2,1)S(1)}, u32[]{:S(2)}, u32[]{:S(2)}) %all-to-all-start.1) | async-done | bytes 524320 | tf_op jit(solution)/shard_map/all_to_all | solution.py:291
  53.3 2.3 %middle.1 = (f32[16,128,128]{2,1,0:T(8,128)S(1)}, bf16[16,128,128]{2,1,0:T(8,128)(2,1)S(1)}, bf16[128,2,16,128]{3,2,1,0:T(8,128)(2,1)S(1)}) custom-call(bf16[128,16,128]{2,1,0:T(8,128)(2,1)S(1)} %all-to-all-done.1.y, f32[16,128,128]{2,1,0:T(8,128)S(1)} %get-tuple-element.26.z0, f32[16,128,128]{2,1,0:T(8,128)S(1)} %get-tuple-element.27.gate, ...), custom_call_target="tpu_custom_call" | custom-call | tf_op jit(solution)/shard_map/middle/pallas_call | solution.py:225
  55.6 24.1 %all_to_all.20.b = bf16[128,2,16,128]{3,2,1,0:T(8,128)(2,1)S(1)} all-to-all(bf16[128,2,16,128]{3,2,1,0:T(8,128)(2,1)S(1)} %get-tuple-element.32), channel_id=1, replica_groups=mesh['row'=32,'ch'=4] {'ch','row'}, dimensions={0} | all-to-all | bytes 2097152 | tf_op jit(solution)/shard_map/all_to_all | solution.py:299
  79.7 0.7 incoming.1
  80.4 18.0 %all_to_all.21.y = bf16[128,16,128]{2,1,0:T(8,128)(2,1)S(1)} all-to-all(bf16[128,16,128]{2,1,0:T(8,128)(2,1)S(1)} %bitcast.6), channel_id=1, replica_groups=mesh['row'=32,'ch'=4] {'ch','row'}, dimensions={0} | all-to-all | bytes 1048576 | tf_op jit(solution)/shard_map/all_to_all | solution.py:301
  98.4 1.3 %last.1 = (bf16[8,128,128]{2,1,0:T(8,128)(2,1)S(1)}, bf16[8,128,128]{2,1,0:T(8,128)(2,1)S(1)}) custom-call(bf16[128,16,128]{2,1,0:T(8,128)(2,1)S(1)} %all_to_all.21.y, f32[16,128,128]{2,1,0:T(8,128)S(1)} %get-tuple-element.33.state, bf16[16,128,128]{2,1,0:T(8,128)(2,1)S(1)} %get-tuple-element.34.normed, bf16[2,128,128]{2,1,0:T(8,128)(2,1)S(1)} %copy-done.1, ...), custom_call_target="tpu_custom_call" | custom-call | tf_op jit(solution)/shard_map/last/pallas_call | solution.py:225
  99.6 0.7 collective-permute-start.3
  100.3 2.7 %collective-permute-start.5 = (bf16[8,128,128]{2,1,0:T(8,128)(2,1)S(1)}, bf16[8,128,128]{2,1,0:T(8,128)(2,1)S(1)}, u32[]{:S(2)}, u32[]{:S(2)}) collective-permute-start(bf16[8,128,128]{2,1,0:T(8,128)(2,1)S(1)} %get-tuple-element.36.own1), channel_id=1, source_target_pairs={{0,3},{1,0},{2,1},{3,2},{4,7},{5,4},{6,5},{7,6},{8,11},{9,8},{10,9... | collective-permute-start | bytes 786440 | tf_op jit(solution)/shard_map/ppermute | solution.py:310
  102.9 0.0 collective-permute-start.8
  103.0 2.0 %collective-permute-start.7 = (bf16[8,128,128]{2,1,0:T(8,128)(2,1)S(1)}, bf16[8,128,128]{2,1,0:T(8,128)(2,1)S(1)}, u32[]{:S(2)}, u32[]{:S(2)}) collective-permute-start(bf16[8,128,128]{2,1,0:T(8,128)(2,1)S(1)} %get-tuple-element.36.own1), channel_id=1, source_target_pairs={{0,1},{1,2},{2,3},{3,0},{4,5},{5,6},{6,7},{7,4},{8,9},{9,10},{10,1... | collective-permute-start | bytes 786440 | tf_op jit(solution)/shard_map/ppermute | solution.py:311
  105.0 5.2 %collective-permute-done.3.up0 = bf16[8,128,128]{2,1,0:T(8,128)(2,1)S(1)} collective-permute-done((bf16[8,128,128]{2,1,0:T(8,128)(2,1)S(1)}, bf16[8,128,128]{2,1,0:T(8,128)(2,1)S(1)}, u32[]{:S(2)}, u32[]{:S(2)}) %collective-permute-start.3) | collective-permute-done | bytes 262176 | tf_op jit(solution)/shard_map/ppermute | solution.py:310
  110.2 0.0 collective-permute-start.4
  110.2 0.0 collective-permute-done.5.down1
  110.2 3.2 %collective-permute-start.6 = (bf16[8,128,128]{2,1,0:T(8,128)(2,1)S(1)}, bf16[8,128,128]{2,1,0:T(8,128)(2,1)S(1)}, u32[]{:S(2)}, u32[]{:S(2)}) collective-permute-start(bf16[8,128,128]{2,1,0:T(8,128)(2,1)S(1)} %collective-permute-done.5.down1), channel_id=1, source_target_pairs={{0,3},{1,0},{2,1},{3,2},{4,7},{5,4},{6,5},{7,6},{8,11},{9,8},{10,9... | collective-permute-start | bytes 786440 | tf_op jit(solution)/shard_map/ppermute | solution.py:312
  113.4 1.9 %collective-permute-done.8.down0 = bf16[8,128,128]{2,1,0:T(8,128)(2,1)S(1)} collective-permute-done((bf16[8,128,128]{2,1,0:T(8,128)(2,1)S(1)}, bf16[8,128,128]{2,1,0:T(8,128)(2,1)S(1)}, u32[]{:S(2)}, u32[]{:S(2)}) %collective-permute-start.8) | collective-permute-done | bytes 262176 | tf_op jit(solution)/shard_map/ppermute | solution.py:311
  115.3 0.5 collective-permute-done.7.up1
  115.8 1.8 %spread_near.1._ = f32[16,512,128]{2,1,0:T(8,128)} custom-call(bf16[8,128,128]{2,1,0:T(8,128)(2,1)S(1)} %get-tuple-element.35.own0, bf16[8,128,128]{2,1,0:T(8,128)(2,1)S(1)} %get-tuple-element.36.own1, bf16[8,128,128]{2,1,0:T(8,128)(2,1)S(1)} %collective-permute-done.3.up0, bf16[8,128,128]{2,1,0:T(8,128)(2,1)S(1)} %collective-permute-done.7.up1, ...), custom_call_target="tpu_custom_call" | custom-call | tf_op jit(solution)/shard_map/spread_near/pallas_call | solution.py:314
  117.5 2.2 %collective-permute-done.4.far0 = bf16[8,128,128]{2,1,0:T(8,128)(2,1)S(1)} collective-permute-done((bf16[8,128,128]{2,1,0:T(8,128)(2,1)S(1)}, bf16[8,128,128]{2,1,0:T(8,128)(2,1)S(1)}, u32[]{:S(2)}, u32[]{:S(2)}) %collective-permute-start.4) | collective-permute-done | bytes 262176 | tf_op jit(solution)/shard_map/ppermute | solution.py:312
  119.8 1.0 spread_far.1
  (17 shorter events, 0.0 us)
Async XLA Ops:
  0.0 13.7 %copy-start.4 = (f32[2,128]{1,0:T(2,128)S(1)}, f32[2,128]{1,0:T(2,128)}, u32[]{:S(2)}) copy-start(f32[2,128]{1,0:T(2,128)} %in_bias.5) | copy-start | bytes 3076
  0.0 13.7 %copy-start.3 = (f32[2,128]{1,0:T(2,128)S(1)}, f32[2,128]{1,0:T(2,128)}, u32[]{:S(2)}) copy-start(f32[2,128]{1,0:T(2,128)} %in_gain.5) | copy-start | bytes 3076
  0.0 13.7 %copy-start = (bf16[2,128,4,32]{1,3,2,0:T(8,128)(2,1)S(1)}, bf16[2,128,4,32]{1,3,2,0:T(8,128)(2,1)}, u32[]{:S(2)}) copy-start(bf16[2,128,4,32]{1,3,2,0:T(8,128)(2,1)} %param.13) | copy-start | bytes 196612
  0.0 13.7 %copy-start.5 = (s32[512]{0:T(512)S(1)}, s32[512]{0:T(512)}, u32[]{:S(2)}) copy-start(s32[512]{0:T(512)} %param.10) | copy-start | bytes 6148
  0.0 13.7 %copy-start.1 = (bf16[2,128,128]{2,1,0:T(8,128)(2,1)S(1)}, bf16[2,128,128]{2,1,0:T(8,128)(2,1)}, u32[]{:S(2)}) copy-start(bf16[2,128,128]{2,1,0:T(8,128)(2,1)} %w_gate.3) | copy-start | bytes 196612
  0.0 13.7 %copy-start.2 = (bf16[2,32,128]{2,1,0:T(8,128)(2,1)S(1)}, bf16[2,32,128]{2,1,0:T(8,128)(2,1)}, u32[]{:S(2)}) copy-start(bf16[2,32,128]{2,1,0:T(8,128)(2,1)} %w_out.1) | copy-start | bytes 49156
  0.0 13.7 %copy-start.7 = (f32[2,32]{1,0:T(2,128)S(1)}, f32[2,32]{1,0:T(2,128)}, u32[]{:S(2)}) copy-start(f32[2,32]{1,0:T(2,128)} %out_bias.1) | copy-start | bytes 772
  0.0 13.7 %copy-start.6 = (f32[2,32]{1,0:T(2,128)S(1)}, f32[2,32]{1,0:T(2,128)}, u32[]{:S(2)}) copy-start(f32[2,32]{1,0:T(2,128)} %out_gain.1) | copy-start | bytes 772
  5.2 25.8 %all-to-all-start = ((bf16[32,2,16,512]{3,2,1,0:T(8,128)(2,1)}), bf16[32,2,16,512]{3,2,1,0:T(8,128)(2,1)S(1)}, u32[]{:S(2)}, u32[]{:S(2)}) async-start(bf16[32,2,16,512]{3,2,1,0:T(8,128)(2,1)} %project0.1), calls=%async_computation | async-start | bytes 2097152 | tf_op jit(solution)/shard_map/all_to_all | solution.py:267
  32.5 20.8 %all-to-all-start.1 = ((bf16[128,16,128]{2,1,0:T(8,128)(2,1)}), bf16[128,16,128]{2,1,0:T(8,128)(2,1)S(1)}, u32[]{:S(2)}, u32[]{:S(2)}) async-start(bf16[128,16,128]{2,1,0:T(8,128)(2,1)} %bitcast.4), calls=%async_computation.1 | async-start | bytes 1048576 | tf_op jit(solution)/shard_map/all_to_all | solution.py:291
  38.8 10.0 %collective-permute-start.2 = (bf16[208,128]{1,0:T(8,128)(2,1)S(1)}, bf16[208,128]{1,0:T(8,128)(2,1)S(1)}, u32[]{:S(2)}, u32[]{:S(2)}) collective-permute-start(bf16[208,128]{1,0:T(8,128)(2,1)S(1)} %get-tuple-element.29.own), channel_id=1, source_target_pairs={{0,2},{1,3},{2,0},{3,1},{4,6},{5,7},{6,4},{7,5},{8,10},{9,11},{10,... | collective-permute-start | bytes 159752 | tf_op jit(solution)/shard_map/ppermute | solution.py:288
  41.3 7.5 %collective-permute-start.1 = (bf16[208,128]{1,0:T(8,128)(2,1)S(1)}, bf16[208,128]{1,0:T(8,128)(2,1)S(1)}, u32[]{:S(2)}, u32[]{:S(2)}) collective-permute-start(bf16[208,128]{1,0:T(8,128)(2,1)S(1)} %get-tuple-element.29.own), channel_id=1, source_target_pairs={{0,3},{1,0},{2,1},{3,2},{4,7},{5,4},{6,5},{7,6},{8,11},{9,8},{10,9... | collective-permute-start | bytes 159752 | tf_op jit(solution)/shard_map/ppermute | solution.py:288
  42.5 6.7 %collective-permute-start = (bf16[208,128]{1,0:T(8,128)(2,1)S(1)}, bf16[208,128]{1,0:T(8,128)(2,1)S(1)}, u32[]{:S(2)}, u32[]{:S(2)}) collective-permute-start(bf16[208,128]{1,0:T(8,128)(2,1)S(1)} %get-tuple-element.29.own), channel_id=1, source_target_pairs={{0,1},{1,2},{2,3},{3,0},{4,5},{5,6},{6,7},{7,4},{8,9},{9,10},{10,1... | collective-permute-start | bytes 159752 | tf_op jit(solution)/shard_map/ppermute | solution.py:288
  99.6 10.5 %collective-permute-start.3 = (bf16[8,128,128]{2,1,0:T(8,128)(2,1)S(1)}, bf16[8,128,128]{2,1,0:T(8,128)(2,1)S(1)}, u32[]{:S(2)}, u32[]{:S(2)}) collective-permute-start(bf16[8,128,128]{2,1,0:T(8,128)(2,1)S(1)} %get-tuple-element.35.own0), channel_id=1, source_target_pairs={{0,1},{1,2},{2,3},{3,0},{4,5},{5,6},{6,7},{7,4},{8,9},{9,10},{10,1... | collective-permute-start | bytes 786440 | tf_op jit(solution)/shard_map/ppermute | solution.py:310
  100.3 9.9 %collective-permute-start.5 = (bf16[8,128,128]{2,1,0:T(8,128)(2,1)S(1)}, bf16[8,128,128]{2,1,0:T(8,128)(2,1)S(1)}, u32[]{:S(2)}, u32[]{:S(2)}) collective-permute-start(bf16[8,128,128]{2,1,0:T(8,128)(2,1)S(1)} %get-tuple-element.36.own1), channel_id=1, source_target_pairs={{0,3},{1,0},{2,1},{3,2},{4,7},{5,4},{6,5},{7,6},{8,11},{9,8},{10,9... | collective-permute-start | bytes 786440 | tf_op jit(solution)/shard_map/ppermute | solution.py:310
  102.9 12.4 %collective-permute-start.8 = (bf16[8,128,128]{2,1,0:T(8,128)(2,1)S(1)}, bf16[8,128,128]{2,1,0:T(8,128)(2,1)S(1)}, u32[]{:S(2)}, u32[]{:S(2)}) collective-permute-start(bf16[8,128,128]{2,1,0:T(8,128)(2,1)S(1)} %get-tuple-element.35.own0), channel_id=1, source_target_pairs={{0,3},{1,0},{2,1},{3,2},{4,7},{5,4},{6,5},{7,6},{8,11},{9,8},{10,9... | collective-permute-start | bytes 786440 | tf_op jit(solution)/shard_map/ppermute | solution.py:311
  103.0 12.8 %collective-permute-start.7 = (bf16[8,128,128]{2,1,0:T(8,128)(2,1)S(1)}, bf16[8,128,128]{2,1,0:T(8,128)(2,1)S(1)}, u32[]{:S(2)}, u32[]{:S(2)}) collective-permute-start(bf16[8,128,128]{2,1,0:T(8,128)(2,1)S(1)} %get-tuple-element.36.own1), channel_id=1, source_target_pairs={{0,1},{1,2},{2,3},{3,0},{4,5},{5,6},{6,7},{7,4},{8,9},{9,10},{10,1... | collective-permute-start | bytes 786440 | tf_op jit(solution)/shard_map/ppermute | solution.py:311
  110.2 9.6 %collective-permute-start.4 = (bf16[8,128,128]{2,1,0:T(8,128)(2,1)S(1)}, bf16[8,128,128]{2,1,0:T(8,128)(2,1)S(1)}, u32[]{:S(2)}, u32[]{:S(2)}) collective-permute-start(bf16[8,128,128]{2,1,0:T(8,128)(2,1)S(1)} %collective-permute-done.3.up0), channel_id=1, source_target_pairs={{0,1},{1,2},{2,3},{3,0},{4,5},{5,6},{6,7},{7,4},{8,9},{9,10},{10,1... | collective-permute-start | bytes 786440 | tf_op jit(solution)/shard_map/ppermute | solution.py:312
  110.2 9.6 %collective-permute-start.6 = (bf16[8,128,128]{2,1,0:T(8,128)(2,1)S(1)}, bf16[8,128,128]{2,1,0:T(8,128)(2,1)S(1)}, u32[]{:S(2)}, u32[]{:S(2)}) collective-permute-start(bf16[8,128,128]{2,1,0:T(8,128)(2,1)S(1)} %collective-permute-done.5.down1), channel_id=1, source_target_pairs={{0,3},{1,0},{2,1},{3,2},{4,7},{5,4},{6,5},{7,6},{8,11},{9,8},{10,9... | collective-permute-start | bytes 786440 | tf_op jit(solution)/shard_map/ppermute | solution.py:312

commit v5 on v4

--- a/solution.py
+++ b/solution.py
@@ -142,7 +142,7 @@
     norms[5] = column(in_bias[1:2, :])
 
 
-def outgoing_kernel(a, out):
+def outgoing_kernel(a, _w, _gate, out):
     left = a[:, 0].reshape(N, N)
     for h in range(G):
         right = a[8 * h : 8 * h + 8, 1].reshape(T, N)
@@ -279,7 +279,6 @@
         + [(v, VMEM) for v in (in_gain, in_bias, w_gate, w_t, w_out, out_gain, out_bias)],
         MOST_VMEM,
     )
-    a, state, gate, half_mask, own = lax.optimization_barrier((sent, state, gate, half_mask, own))
     w, norms = call(
         weights_kernel,
         "weights",
@@ -287,7 +286,13 @@
         [pltpu.VMEM((G, PK, C), BF16)],
         [(v, VMEM) for v in (own, up(own), down(own), cross(own), in_gain, in_bias)],
     )
-    x = call(outgoing_kernel, "outgoing", arr((G, R, RB, T), BF16), [], [(a, VMEM)])
+    x = call(
+        outgoing_kernel,
+        "outgoing",
+        arr((G, R, RB, T), BF16),
+        [],
+        [(sent, VMEM)] + [(v, pl.ANY) for v in (w, gate)],
+    )
     y = lax.all_to_all(x.reshape(G * R, RB, T), ("ch", "row"), 0, 0)
     state, normed, b = call(
         middle_kernel,

time: 121 us -> 119 us (0.983)
  blocking collectives: 42 us -> 61.3 us
  waiting for transfers between devices: 34.6 us -> 18.6 us
  starting transfers between devices: 27.9 us -> 22 us
    all_to_all x1 -> x2, blocking collectives: 18 us -> 37.6 us  [on_device(): y = lax.all_to_all(x.reshape(G * R, RB, T), ('ch', 'row'), 0, 0)]
    all_to_all x1, waiting for transfers between devices: 15.3 us -> 4.36 us  [on_device(): sent = lax.all_to_all(a, 'row', 0, 0)]
    all_to_all x1 -> x0, starting transfers between devices: 6.29 us -> none  [on_device(): y = lax.all_to_all(x.reshape(G * R, RB, T), ('ch', 'row'), 0, 0)]
    ppermute x1, waiting for transfers between devices: 5.46 us -> 0.58 us  [on_device(): cross(own)]
    all_to_all x1 -> x0, waiting for transfers between devices: 3.72 us -> none  [on_device(): y = lax.all_to_all(x.reshape(G * R, RB, T), ('ch', 'row'), 0, 0)]
    ppermute x1, waiting for transfers between devices: 0.37 us -> 2.35 us  [on_device(): up(own)]
    ppermute x1, waiting for transfers between devices: 0.01 us -> 1.52 us  [on_device(): down(own)]
  transfers between devices with their start and end apart: 11 -> 10, of which waited for: 8 -> 8; matrix products, arithmetic and copies ran while one was open for 0% -> 0% of each run, Pallas kernels for 3% -> 3%
where the time goes in v5:
time: 119 us; the launch traced here: 118 us
  blocking collectives  61.3 us (52%)
  starting transfers between devices  22 us (18%)
  waiting for transfers between devices  18.6 us (16%)
  Pallas kernels  15.2 us (13%)
    all_to_all x2, blocking collectives, on_device(): y = lax.all_to_all(x.reshape(G * R, RB, T), ('ch', 'row'), 0, 0)  37.6 us
    all_to_all x1, blocking collectives, on_device(): b = lax.all_to_all(b, ('ch', 'row'), 0, 0)  23.7 us
    pallas_call x7, Pallas kernels, call(): pl.pallas_call(kernel, out_shape=outs, in_specs=[pl.BlockSpec(memory_spac...  12.4 us
    all_to_all x1, starting transfers between devices, on_device(): sent = lax.all_to_all(a, 'row', 0, 0)  8.42 us
    ppermute x2, waiting for transfers between devices, on_device(): up0, down1 = (up(z0), down(z1))  5.19 us
    all_to_all x1, waiting for transfers between devices, on_device(): sent = lax.all_to_all(a, 'row', 0, 0)  4.36 us
    ppermute x2, starting transfers between devices, on_device(): up0, down1 = (up(z0), down(z1))  3.31 us
    ppermute x2, starting transfers between devices, on_device(): far0, far1 = (up(up0), down(down1))  3.24 us
  transfers between devices with their start and end apart: 10, of which 8 were waited for; matrix products, arithmetic and copies ran while one was open for 0% of the time, Pallas kernels for 3%

profile of v5, /device:TPU:0, one launch (start us, length us, event | category | flops | bytes accessed | tf_op | source)
XLA Modules:
  0.0 118.4 jit_solution(6816010860996498033)
XLA Ops:
  0.0 5.2 %project0.1 = bf16[32,2,16,512]{3,2,1,0:T(8,128)(2,1)} custom-call(f32[16,512,128]{2,1,0:T(8,128)} %pair.3, s32[1,512]{1,0:T(1,128)} %bitcast.10, f32[2,128]{1,0:T(2,128)} %in_gain.5, f32[2,128]{1,0:T(2,128)} %in_bias.5, bf16[2,128,128]{2,1,0:T(8,128)(2,1)} %bitcast.8), custom_call_target="tpu_custom_call" | custom-call | tf_op jit(solution)/shard_map/project0/pallas_call | solution.py:225
  5.2 8.4 %all-to-all-start = ((bf16[32,2,16,512]{3,2,1,0:T(8,128)(2,1)}), bf16[32,2,16,512]{3,2,1,0:T(8,128)(2,1)S(1)}, u32[]{:S(2)}, u32[]{:S(2)}) async-start(bf16[32,2,16,512]{3,2,1,0:T(8,128)(2,1)} %project0.1), calls=%async_computation | async-start | bytes 2097152 | tf_op jit(solution)/shard_map/all_to_all | solution.py:267
  13.7 2.0 %gate0.1 = (f32[16,128,128]{2,1,0:T(8,128)S(1)}, f32[16,128,128]{2,1,0:T(8,128)S(1)}, f32[16,128]{1,0:T(8,128)S(1)}, bf16[208,128]{1,0:T(8,128)(2,1)S(1)}) custom-call(f32[16,512,128]{2,1,0:T(8,128)} %pair.3, s32[1,512]{1,0:T(1,128)S(1)} %bitcast.11, f32[2,128]{1,0:T(2,128)S(1)} %copy-done.5, f32[2,128]{1,0:T(2,128)S(1)} %copy-done.6, ...), custom_call_target="tpu_custom_call" | custom-call | tf_op jit(solution)/shard_map/gate0/pallas_call | solution.py:225
  15.7 1.0 copy-done
  16.7 3.0 %collective-permute-start.2 = (bf16[208,128]{1,0:T(8,128)(2,1)S(1)}, bf16[208,128]{1,0:T(8,128)(2,1)S(1)}, u32[]{:S(2)}, u32[]{:S(2)}) collective-permute-start(bf16[208,128]{1,0:T(8,128)(2,1)S(1)} %get-tuple-element.16.own), channel_id=1, source_target_pairs={{0,2},{1,3},{2,0},{3,1},{4,6},{5,7},{6,4},{7,5},{8,10},{9,11},{10,... | collective-permute-start | bytes 159752 | tf_op jit(solution)/shard_map/ppermute | solution.py:287
  19.7 1.1 collective-permute-start.1
  20.9 0.9 collective-permute-start
  21.7 0.6 collective-permute-done.2.far
  22.3 1.5 %collective-permute-done.1.down = bf16[208,128]{1,0:T(8,128)(2,1)S(1)} collective-permute-done((bf16[208,128]{1,0:T(8,128)(2,1)S(1)}, bf16[208,128]{1,0:T(8,128)(2,1)S(1)}, u32[]{:S(2)}, u32[]{:S(2)}) %collective-permute-start.1) | collective-permute-done | bytes 53280 | tf_op jit(solution)/shard_map/ppermute | solution.py:287
  23.9 2.4 %collective-permute-done.up = bf16[208,128]{1,0:T(8,128)(2,1)S(1)} collective-permute-done((bf16[208,128]{1,0:T(8,128)(2,1)S(1)}, bf16[208,128]{1,0:T(8,128)(2,1)S(1)}, u32[]{:S(2)}, u32[]{:S(2)}) %collective-permute-start) | collective-permute-done | bytes 53280 | tf_op jit(solution)/shard_map/ppermute | solution.py:287
  26.2 0.4 weights.1
  26.6 4.4 %all-to-all-done.a = bf16[32,2,16,512]{3,2,1,0:T(8,128)(2,1)S(1)} async-done(((bf16[32,2,16,512]{3,2,1,0:T(8,128)(2,1)}), bf16[32,2,16,512]{3,2,1,0:T(8,128)(2,1)S(1)}, u32[]{:S(2)}, u32[]{:S(2)}) %all-to-all-start) | async-done | bytes 1048608 | tf_op jit(solution)/shard_map/all_to_all | solution.py:267
  31.0 0.7 outgoing.1
  31.7 19.7 %all_to_all.20.y = bf16[128,16,128]{2,1,0:T(8,128)(2,1)S(1)} all-to-all(bf16[128,16,128]{2,1,0:T(8,128)(2,1)S(1)} %bitcast.7), channel_id=1, replica_groups=mesh['row'=32,'ch'=4] {'ch','row'}, dimensions={0} | all-to-all | bytes 1048576 | tf_op jit(solution)/shard_map/all_to_all | solution.py:296
  51.4 2.2 %middle.1 = (f32[16,128,128]{2,1,0:T(8,128)S(1)}, bf16[16,128,128]{2,1,0:T(8,128)(2,1)S(1)}, bf16[128,2,16,128]{3,2,1,0:T(8,128)(2,1)S(1)}) custom-call(bf16[128,16,128]{2,1,0:T(8,128)(2,1)S(1)} %all_to_all.20.y, f32[16,128,128]{2,1,0:T(8,128)S(1)} %copy-done.1, f32[16,128,128]{2,1,0:T(8,128)S(1)} %get-tuple-element.18._gate.gate, ...), custom_call_target="tpu_custom_call" | custom-call | tf_op jit(solution)/shard_map/middle/pallas_call | solution.py:225
  53.6 23.7 %all_to_all.21.b = bf16[128,2,16,128]{3,2,1,0:T(8,128)(2,1)S(1)} all-to-all(bf16[128,2,16,128]{3,2,1,0:T(8,128)(2,1)S(1)} %get-tuple-element.22), channel_id=1, replica_groups=mesh['row'=32,'ch'=4] {'ch','row'}, dimensions={0} | all-to-all | bytes 2097152 | tf_op jit(solution)/shard_map/all_to_all | solution.py:304
  77.3 0.7 incoming.1
  78.0 18.0 %all_to_all.22.y = bf16[128,16,128]{2,1,0:T(8,128)(2,1)S(1)} all-to-all(bf16[128,16,128]{2,1,0:T(8,128)(2,1)S(1)} %bitcast.6), channel_id=1, replica_groups=mesh['row'=32,'ch'=4] {'ch','row'}, dimensions={0} | all-to-all | bytes 1048576 | tf_op jit(solution)/shard_map/all_to_all | solution.py:306
  96.0 1.2 %last.1 = (bf16[8,128,128]{2,1,0:T(8,128)(2,1)S(1)}, bf16[8,128,128]{2,1,0:T(8,128)(2,1)S(1)}) custom-call(bf16[128,16,128]{2,1,0:T(8,128)(2,1)S(1)} %all_to_all.22.y, f32[16,128,128]{2,1,0:T(8,128)S(1)} %get-tuple-element.23.state, bf16[16,128,128]{2,1,0:T(8,128)(2,1)S(1)} %get-tuple-element.24.normed, bf16[2,128,128]{2,1,0:T(8,128)(2,1)S(1)} %copy-done.3, ...), custom_call_target="tpu_custom_call" | custom-call | tf_op jit(solution)/shard_map/last/pallas_call | solution.py:225
  97.2 0.6 collective-permute-start.3
  97.9 2.7 %collective-permute-start.5 = (bf16[8,128,128]{2,1,0:T(8,128)(2,1)S(1)}, bf16[8,128,128]{2,1,0:T(8,128)(2,1)S(1)}, u32[]{:S(2)}, u32[]{:S(2)}) collective-permute-start(bf16[8,128,128]{2,1,0:T(8,128)(2,1)S(1)} %get-tuple-element.26.own1), channel_id=1, source_target_pairs={{0,3},{1,0},{2,1},{3,2},{4,7},{5,4},{6,5},{7,6},{8,11},{9,8},{10,9... | collective-permute-start | bytes 786440 | tf_op jit(solution)/shard_map/ppermute | solution.py:315
  100.5 0.0 collective-permute-start.8
  100.6 2.0 %collective-permute-start.7 = (bf16[8,128,128]{2,1,0:T(8,128)(2,1)S(1)}, bf16[8,128,128]{2,1,0:T(8,128)(2,1)S(1)}, u32[]{:S(2)}, u32[]{:S(2)}) collective-permute-start(bf16[8,128,128]{2,1,0:T(8,128)(2,1)S(1)} %get-tuple-element.26.own1), channel_id=1, source_target_pairs={{0,1},{1,2},{2,3},{3,0},{4,5},{5,6},{6,7},{7,4},{8,9},{9,10},{10,1... | collective-permute-start | bytes 786440 | tf_op jit(solution)/shard_map/ppermute | solution.py:316
  102.6 5.2 %collective-permute-done.3.up0 = bf16[8,128,128]{2,1,0:T(8,128)(2,1)S(1)} collective-permute-done((bf16[8,128,128]{2,1,0:T(8,128)(2,1)S(1)}, bf16[8,128,128]{2,1,0:T(8,128)(2,1)S(1)}, u32[]{:S(2)}, u32[]{:S(2)}) %collective-permute-start.3) | collective-permute-done | bytes 262176 | tf_op jit(solution)/shard_map/ppermute | solution.py:315
  107.7 0.0 collective-permute-start.4
  107.7 3.2 %collective-permute-start.6 = (bf16[8,128,128]{2,1,0:T(8,128)(2,1)S(1)}, bf16[8,128,128]{2,1,0:T(8,128)(2,1)S(1)}, u32[]{:S(2)}, u32[]{:S(2)}) collective-permute-start(bf16[8,128,128]{2,1,0:T(8,128)(2,1)S(1)} %collective-permute-done.5.down1), channel_id=1, source_target_pairs={{0,3},{1,0},{2,1},{3,2},{4,7},{5,4},{6,5},{7,6},{8,11},{9,8},{10,9... | collective-permute-start | bytes 786440 | tf_op jit(solution)/shard_map/ppermute | solution.py:317
  111.0 1.9 %collective-permute-done.8.down0 = bf16[8,128,128]{2,1,0:T(8,128)(2,1)S(1)} collective-permute-done((bf16[8,128,128]{2,1,0:T(8,128)(2,1)S(1)}, bf16[8,128,128]{2,1,0:T(8,128)(2,1)S(1)}, u32[]{:S(2)}, u32[]{:S(2)}) %collective-permute-start.8) | collective-permute-done | bytes 262176 | tf_op jit(solution)/shard_map/ppermute | solution.py:316
  112.9 0.5 collective-permute-done.7.up1
  113.4 1.8 %spread_near.1._ = f32[16,512,128]{2,1,0:T(8,128)} custom-call(bf16[8,128,128]{2,1,0:T(8,128)(2,1)S(1)} %get-tuple-element.25.own0, bf16[8,128,128]{2,1,0:T(8,128)(2,1)S(1)} %get-tuple-element.26.own1, bf16[8,128,128]{2,1,0:T(8,128)(2,1)S(1)} %collective-permute-done.3.up0, bf16[8,128,128]{2,1,0:T(8,128)(2,1)S(1)} %collective-permute-done.7.up1, ...), custom_call_target="tpu_custom_call" | custom-call | tf_op jit(solution)/shard_map/spread_near/pallas_call | solution.py:319
  115.1 2.2 %collective-permute-done.4.far0 = bf16[8,128,128]{2,1,0:T(8,128)(2,1)S(1)} collective-permute-done((bf16[8,128,128]{2,1,0:T(8,128)(2,1)S(1)}, bf16[8,128,128]{2,1,0:T(8,128)(2,1)S(1)}, u32[]{:S(2)}, u32[]{:S(2)}) %collective-permute-start.4) | collective-permute-done | bytes 262176 | tf_op jit(solution)/shard_map/ppermute | solution.py:317
  117.4 0.0 collective-permute-done.6.far1
  117.4 1.0 spread_far.1
  (20 shorter events, 0.0 us)
Async XLA Ops:
  0.0 13.7 %copy-start.6 = (f32[2,128]{1,0:T(2,128)S(1)}, f32[2,128]{1,0:T(2,128)}, u32[]{:S(2)}) copy-start(f32[2,128]{1,0:T(2,128)} %in_bias.5) | copy-start | bytes 3076
  0.0 13.7 %copy-start.5 = (f32[2,128]{1,0:T(2,128)S(1)}, f32[2,128]{1,0:T(2,128)}, u32[]{:S(2)}) copy-start(f32[2,128]{1,0:T(2,128)} %in_gain.5) | copy-start | bytes 3076
  0.0 13.7 %copy-start.2 = (bf16[2,128,4,32]{1,3,2,0:T(8,128)(2,1)S(1)}, bf16[2,128,4,32]{1,3,2,0:T(8,128)(2,1)}, u32[]{:S(2)}) copy-start(bf16[2,128,4,32]{1,3,2,0:T(8,128)(2,1)} %param.13) | copy-start | bytes 196612
  0.0 13.7 %copy-start.7 = (s32[512]{0:T(512)S(1)}, s32[512]{0:T(512)}, u32[]{:S(2)}) copy-start(s32[512]{0:T(512)} %param.10) | copy-start | bytes 6148
  0.0 13.7 %copy-start.3 = (bf16[2,128,128]{2,1,0:T(8,128)(2,1)S(1)}, bf16[2,128,128]{2,1,0:T(8,128)(2,1)}, u32[]{:S(2)}) copy-start(bf16[2,128,128]{2,1,0:T(8,128)(2,1)} %w_gate.3) | copy-start | bytes 196612
  0.0 13.7 %copy-start.4 = (bf16[2,32,128]{2,1,0:T(8,128)(2,1)S(1)}, bf16[2,32,128]{2,1,0:T(8,128)(2,1)}, u32[]{:S(2)}) copy-start(bf16[2,32,128]{2,1,0:T(8,128)(2,1)} %w_out.1) | copy-start | bytes 49156
  0.0 13.7 %copy-start.9 = (f32[2,32]{1,0:T(2,128)S(1)}, f32[2,32]{1,0:T(2,128)}, u32[]{:S(2)}) copy-start(f32[2,32]{1,0:T(2,128)} %out_bias.1) | copy-start | bytes 772
  0.0 13.7 %copy-start.8 = (f32[2,32]{1,0:T(2,128)S(1)}, f32[2,32]{1,0:T(2,128)}, u32[]{:S(2)}) copy-start(f32[2,32]{1,0:T(2,128)} %out_gain.1) | copy-start | bytes 772
  5.2 25.8 %all-to-all-start = ((bf16[32,2,16,512]{3,2,1,0:T(8,128)(2,1)}), bf16[32,2,16,512]{3,2,1,0:T(8,128)(2,1)S(1)}, u32[]{:S(2)}, u32[]{:S(2)}) async-start(bf16[32,2,16,512]{3,2,1,0:T(8,128)(2,1)} %project0.1), calls=%async_computation | async-start | bytes 2097152 | tf_op jit(solution)/shard_map/all_to_all | solution.py:267
  15.7 1.0 copy-start
  16.7 5.6 %collective-permute-start.2 = (bf16[208,128]{1,0:T(8,128)(2,1)S(1)}, bf16[208,128]{1,0:T(8,128)(2,1)S(1)}, u32[]{:S(2)}, u32[]{:S(2)}) collective-permute-start(bf16[208,128]{1,0:T(8,128)(2,1)S(1)} %get-tuple-element.16.own), channel_id=1, source_target_pairs={{0,2},{1,3},{2,0},{3,1},{4,6},{5,7},{6,4},{7,5},{8,10},{9,11},{10,... | collective-permute-start | bytes 159752 | tf_op jit(solution)/shard_map/ppermute | solution.py:287
  19.7 4.1 %collective-permute-start.1 = (bf16[208,128]{1,0:T(8,128)(2,1)S(1)}, bf16[208,128]{1,0:T(8,128)(2,1)S(1)}, u32[]{:S(2)}, u32[]{:S(2)}) collective-permute-start(bf16[208,128]{1,0:T(8,128)(2,1)S(1)} %get-tuple-element.16.own), channel_id=1, source_target_pairs={{0,3},{1,0},{2,1},{3,2},{4,7},{5,4},{6,5},{7,6},{8,11},{9,8},{10,9... | collective-permute-start | bytes 159752 | tf_op jit(solution)/shard_map/ppermute | solution.py:287
  20.9 5.3 %collective-permute-start = (bf16[208,128]{1,0:T(8,128)(2,1)S(1)}, bf16[208,128]{1,0:T(8,128)(2,1)S(1)}, u32[]{:S(2)}, u32[]{:S(2)}) collective-permute-start(bf16[208,128]{1,0:T(8,128)(2,1)S(1)} %get-tuple-element.16.own), channel_id=1, source_target_pairs={{0,1},{1,2},{2,3},{3,0},{4,5},{5,6},{6,7},{7,4},{8,9},{9,10},{10,1... | collective-permute-start | bytes 159752 | tf_op jit(solution)/shard_map/ppermute | solution.py:287
  31.0 20.4 %copy-start.1 = (f32[16,128,128]{2,1,0:T(8,128)S(1)}, f32[16,128,128]{2,1,0:T(8,128)}, u32[]{:S(2)}) copy-start(f32[16,128,128]{2,1,0:T(8,128)} %copy-done) | copy-start | bytes 3145732
  97.2 10.5 %collective-permute-start.3 = (bf16[8,128,128]{2,1,0:T(8,128)(2,1)S(1)}, bf16[8,128,128]{2,1,0:T(8,128)(2,1)S(1)}, u32[]{:S(2)}, u32[]{:S(2)}) collective-permute-start(bf16[8,128,128]{2,1,0:T(8,128)(2,1)S(1)} %get-tuple-element.25.own0), channel_id=1, source_target_pairs={{0,1},{1,2},{2,3},{3,0},{4,5},{5,6},{6,7},{7,4},{8,9},{9,10},{10,1... | collective-permute-start | bytes 786440 | tf_op jit(solution)/shard_map/ppermute | solution.py:315
  97.9 9.9 %collective-permute-start.5 = (bf16[8,128,128]{2,1,0:T(8,128)(2,1)S(1)}, bf16[8,128,128]{2,1,0:T(8,128)(2,1)S(1)}, u32[]{:S(2)}, u32[]{:S(2)}) collective-permute-start(bf16[8,128,128]{2,1,0:T(8,128)(2,1)S(1)} %get-tuple-element.26.own1), channel_id=1, source_target_pairs={{0,3},{1,0},{2,1},{3,2},{4,7},{5,4},{6,5},{7,6},{8,11},{9,8},{10,9... | collective-permute-start | bytes 786440 | tf_op jit(solution)/shard_map/ppermute | solution.py:315
  100.5 12.4 %collective-permute-start.8 = (bf16[8,128,128]{2,1,0:T(8,128)(2,1)S(1)}, bf16[8,128,128]{2,1,0:T(8,128)(2,1)S(1)}, u32[]{:S(2)}, u32[]{:S(2)}) collective-permute-start(bf16[8,128,128]{2,1,0:T(8,128)(2,1)S(1)} %get-tuple-element.25.own0), channel_id=1, source_target_pairs={{0,3},{1,0},{2,1},{3,2},{4,7},{5,4},{6,5},{7,6},{8,11},{9,8},{10,9... | collective-permute-start | bytes 786440 | tf_op jit(solution)/shard_map/ppermute | solution.py:316
  100.6 12.8 %collective-permute-start.7 = (bf16[8,128,128]{2,1,0:T(8,128)(2,1)S(1)}, bf16[8,128,128]{2,1,0:T(8,128)(2,1)S(1)}, u32[]{:S(2)}, u32[]{:S(2)}) collective-permute-start(bf16[8,128,128]{2,1,0:T(8,128)(2,1)S(1)} %get-tuple-element.26.own1), channel_id=1, source_target_pairs={{0,1},{1,2},{2,3},{3,0},{4,5},{5,6},{6,7},{7,4},{8,9},{9,10},{10,1... | collective-permute-start | bytes 786440 | tf_op jit(solution)/shard_map/ppermute | solution.py:316
  107.7 9.6 %collective-permute-start.4 = (bf16[8,128,128]{2,1,0:T(8,128)(2,1)S(1)}, bf16[8,128,128]{2,1,0:T(8,128)(2,1)S(1)}, u32[]{:S(2)}, u32[]{:S(2)}) collective-permute-start(bf16[8,128,128]{2,1,0:T(8,128)(2,1)S(1)} %collective-permute-done.3.up0), channel_id=1, source_target_pairs={{0,1},{1,2},{2,3},{3,0},{4,5},{5,6},{6,7},{7,4},{8,9},{9,10},{10,1... | collective-permute-start | bytes 786440 | tf_op jit(solution)/shard_map/ppermute | solution.py:317
  107.7 9.6 %collective-permute-start.6 = (bf16[8,128,128]{2,1,0:T(8,128)(2,1)S(1)}, bf16[8,128,128]{2,1,0:T(8,128)(2,1)S(1)}, u32[]{:S(2)}, u32[]{:S(2)}) collective-permute-start(bf16[8,128,128]{2,1,0:T(8,128)(2,1)S(1)} %collective-permute-done.5.down1), channel_id=1, source_target_pairs={{0,3},{1,0},{2,1},{3,2},{4,7},{5,4},{6,5},{7,6},{8,11},{9,8},{10,9... | collective-permute-start | bytes 786440 | tf_op jit(solution)/shard_map/ppermute | solution.py:317

commit v6 on v5

--- a/solution.py
+++ b/solution.py
@@ -144,16 +144,22 @@
 
 def outgoing_kernel(a, _w, _gate, out):
     left = a[:, 0].reshape(N, N)
-    for h in range(G):
-        right = a[8 * h : 8 * h + 8, 1].reshape(T, N)
-        out[h] = dot(left, right, 1, 1).reshape(R, RB, T).astype(BF16)
+    for h in range(0, G, 4):
+        right = a[8 * h : 8 * (h + 4), 1].reshape(T * 4, N)
+        x = dot(left, right, 1, 1)
+        for k in range(4):
+            out[h + k] = x[:, T * k : T * k + T].reshape(R, RB, T).astype(BF16)
 
 
 def incoming_kernel(b, out):
-    left = jnp.concatenate([b[R * h : R * h + R, 0].reshape(N, T) for h in range(G)], 1)
-    for h in range(G):
-        right = b[R * h : R * h + R, 1].reshape(N, T)
-        out[h] = dot(left, right, 0, 0).reshape(R, RB, T).astype(BF16)
+    def columns(part, h, n):
+        return jnp.concatenate([b[R * k : R * k + R, part].reshape(N, T) for k in range(h, h + n)], 1)
+
+    left = columns(0, 0, G)
+    for h in range(0, G, 4):
+        x = dot(left, columns(1, h, 4), 0, 0)
+        for k in range(4):
+            out[h + k] = x[:, T * k : T * k + T].reshape(R, RB, T).astype(BF16)
 
 
 def middle_kernel(

time: 119 us -> 118 us (level)
  transfers between devices with their start and end apart: 10 -> 10, of which waited for: 8 -> 8; matrix products, arithmetic and copies ran while one was open for 0% -> 0% of each run, Pallas kernels for 3% -> 4%
where the time goes in v6:
time: 118 us
  blocking collectives  61.3 us (52%)
  starting transfers between devices  22 us (19%)
  waiting for transfers between devices  18.6 us (16%)
  Pallas kernels  14.7 us (12%)
    all_to_all x2, blocking collectives, on_device(): y = lax.all_to_all(x.reshape(G * R, RB, T), ('ch', 'row'), 0, 0)  37.6 us
    all_to_all x1, blocking collectives, on_device(): b = lax.all_to_all(b, ('ch', 'row'), 0, 0)  23.7 us
    pallas_call x7, Pallas kernels, call(): pl.pallas_call(kernel, out_shape=outs, in_specs=[pl.BlockSpec(memory_spac...  11.9 us
    all_to_all x1, starting transfers between devices, on_device(): sent = lax.all_to_all(a, 'row', 0, 0)  8.42 us
    ppermute x2, waiting for transfers between devices, on_device(): up0, down1 = (up(z0), down(z1))  5.19 us
    all_to_all x1, waiting for transfers between devices, on_device(): sent = lax.all_to_all(a, 'row', 0, 0)  4.36 us
    ppermute x2, starting transfers between devices, on_device(): up0, down1 = (up(z0), down(z1))  3.31 us
    ppermute x2, starting transfers between devices, on_device(): far0, far1 = (up(up0), down(down1))  3.24 us
  transfers between devices with their start and end apart: 10, of which 8 were waited for; matrix products, arithmetic and copies ran while one was open for 0% of the time, Pallas kernels for 4%

profile of v6, /device:TPU:0, one launch (start us, length us, event | category | flops | bytes accessed | tf_op | source)
XLA Modules:
  0.0 117.9 jit_solution(15812404297870887406)
XLA Ops:
  0.0 5.2 %project0.1 = bf16[32,2,16,512]{3,2,1,0:T(8,128)(2,1)} custom-call(f32[16,512,128]{2,1,0:T(8,128)} %pair.3, s32[1,512]{1,0:T(1,128)} %bitcast.10, f32[2,128]{1,0:T(2,128)} %in_gain.5, f32[2,128]{1,0:T(2,128)} %in_bias.5, bf16[2,128,128]{2,1,0:T(8,128)(2,1)} %bitcast.8), custom_call_target="tpu_custom_call" | custom-call | tf_op jit(solution)/shard_map/project0/pallas_call | solution.py:231
  5.2 8.4 %all-to-all-start = ((bf16[32,2,16,512]{3,2,1,0:T(8,128)(2,1)}), bf16[32,2,16,512]{3,2,1,0:T(8,128)(2,1)S(1)}, u32[]{:S(2)}, u32[]{:S(2)}) async-start(bf16[32,2,16,512]{3,2,1,0:T(8,128)(2,1)} %project0.1), calls=%async_computation | async-start | bytes 2097152 | tf_op jit(solution)/shard_map/all_to_all | solution.py:273
  13.7 2.0 %gate0.1 = (f32[16,128,128]{2,1,0:T(8,128)S(1)}, f32[16,128,128]{2,1,0:T(8,128)S(1)}, f32[16,128]{1,0:T(8,128)S(1)}, bf16[208,128]{1,0:T(8,128)(2,1)S(1)}) custom-call(f32[16,512,128]{2,1,0:T(8,128)} %pair.3, s32[1,512]{1,0:T(1,128)S(1)} %bitcast.11, f32[2,128]{1,0:T(2,128)S(1)} %copy-done.5, f32[2,128]{1,0:T(2,128)S(1)} %copy-done.6, ...), custom_call_target="tpu_custom_call" | custom-call | tf_op jit(solution)/shard_map/gate0/pallas_call | solution.py:231
  15.7 1.0 copy-done
  16.7 3.0 %collective-permute-start.2 = (bf16[208,128]{1,0:T(8,128)(2,1)S(1)}, bf16[208,128]{1,0:T(8,128)(2,1)S(1)}, u32[]{:S(2)}, u32[]{:S(2)}) collective-permute-start(bf16[208,128]{1,0:T(8,128)(2,1)S(1)} %get-tuple-element.16.own), channel_id=1, source_target_pairs={{0,2},{1,3},{2,0},{3,1},{4,6},{5,7},{6,4},{7,5},{8,10},{9,11},{10,... | collective-permute-start | bytes 159752 | tf_op jit(solution)/shard_map/ppermute | solution.py:293
  19.7 1.1 collective-permute-start.1
  20.9 0.9 collective-permute-start
  21.7 0.6 collective-permute-done.2.far
  22.3 1.5 %collective-permute-done.1.down = bf16[208,128]{1,0:T(8,128)(2,1)S(1)} collective-permute-done((bf16[208,128]{1,0:T(8,128)(2,1)S(1)}, bf16[208,128]{1,0:T(8,128)(2,1)S(1)}, u32[]{:S(2)}, u32[]{:S(2)}) %collective-permute-start.1) | collective-permute-done | bytes 53280 | tf_op jit(solution)/shard_map/ppermute | solution.py:293
  23.9 2.4 %collective-permute-done.up = bf16[208,128]{1,0:T(8,128)(2,1)S(1)} collective-permute-done((bf16[208,128]{1,0:T(8,128)(2,1)S(1)}, bf16[208,128]{1,0:T(8,128)(2,1)S(1)}, u32[]{:S(2)}, u32[]{:S(2)}) %collective-permute-start) | collective-permute-done | bytes 53280 | tf_op jit(solution)/shard_map/ppermute | solution.py:293
  26.2 0.4 weights.1
  26.6 4.4 %all-to-all-done.a = bf16[32,2,16,512]{3,2,1,0:T(8,128)(2,1)S(1)} async-done(((bf16[32,2,16,512]{3,2,1,0:T(8,128)(2,1)}), bf16[32,2,16,512]{3,2,1,0:T(8,128)(2,1)S(1)}, u32[]{:S(2)}, u32[]{:S(2)}) %all-to-all-start) | async-done | bytes 1048608 | tf_op jit(solution)/shard_map/all_to_all | solution.py:273
  31.0 0.5 outgoing.1
  31.5 19.7 %all_to_all.20.y = bf16[128,16,128]{2,1,0:T(8,128)(2,1)S(1)} all-to-all(bf16[128,16,128]{2,1,0:T(8,128)(2,1)S(1)} %bitcast.7), channel_id=1, replica_groups=mesh['row'=32,'ch'=4] {'ch','row'}, dimensions={0} | all-to-all | bytes 1048576 | tf_op jit(solution)/shard_map/all_to_all | solution.py:302
  51.1 2.2 %middle.1 = (f32[16,128,128]{2,1,0:T(8,128)S(1)}, bf16[16,128,128]{2,1,0:T(8,128)(2,1)S(1)}, bf16[128,2,16,128]{3,2,1,0:T(8,128)(2,1)S(1)}) custom-call(bf16[128,16,128]{2,1,0:T(8,128)(2,1)S(1)} %all_to_all.20.y, f32[16,128,128]{2,1,0:T(8,128)S(1)} %copy-done.1, f32[16,128,128]{2,1,0:T(8,128)S(1)} %get-tuple-element.18._gate.gate, ...), custom_call_target="tpu_custom_call" | custom-call | tf_op jit(solution)/shard_map/middle/pallas_call | solution.py:231
  53.4 23.7 %all_to_all.21.b = bf16[128,2,16,128]{3,2,1,0:T(8,128)(2,1)S(1)} all-to-all(bf16[128,2,16,128]{3,2,1,0:T(8,128)(2,1)S(1)} %get-tuple-element.22), channel_id=1, replica_groups=mesh['row'=32,'ch'=4] {'ch','row'}, dimensions={0} | all-to-all | bytes 2097152 | tf_op jit(solution)/shard_map/all_to_all | solution.py:310
  77.1 0.5 incoming.1
  77.5 18.0 %all_to_all.22.y = bf16[128,16,128]{2,1,0:T(8,128)(2,1)S(1)} all-to-all(bf16[128,16,128]{2,1,0:T(8,128)(2,1)S(1)} %bitcast.6), channel_id=1, replica_groups=mesh['row'=32,'ch'=4] {'ch','row'}, dimensions={0} | all-to-all | bytes 1048576 | tf_op jit(solution)/shard_map/all_to_all | solution.py:312
  95.5 1.2 %last.1 = (bf16[8,128,128]{2,1,0:T(8,128)(2,1)S(1)}, bf16[8,128,128]{2,1,0:T(8,128)(2,1)S(1)}) custom-call(bf16[128,16,128]{2,1,0:T(8,128)(2,1)S(1)} %all_to_all.22.y, f32[16,128,128]{2,1,0:T(8,128)S(1)} %get-tuple-element.23.state, bf16[16,128,128]{2,1,0:T(8,128)(2,1)S(1)} %get-tuple-element.24.normed, bf16[2,128,128]{2,1,0:T(8,128)(2,1)S(1)} %copy-done.3, ...), custom_call_target="tpu_custom_call" | custom-call | tf_op jit(solution)/shard_map/last/pallas_call | solution.py:231
  96.7 0.6 collective-permute-start.3
  97.4 2.7 %collective-permute-start.5 = (bf16[8,128,128]{2,1,0:T(8,128)(2,1)S(1)}, bf16[8,128,128]{2,1,0:T(8,128)(2,1)S(1)}, u32[]{:S(2)}, u32[]{:S(2)}) collective-permute-start(bf16[8,128,128]{2,1,0:T(8,128)(2,1)S(1)} %get-tuple-element.26.own1), channel_id=1, source_target_pairs={{0,3},{1,0},{2,1},{3,2},{4,7},{5,4},{6,5},{7,6},{8,11},{9,8},{10,9... | collective-permute-start | bytes 786440 | tf_op jit(solution)/shard_map/ppermute | solution.py:321
  100.0 0.0 collective-permute-start.8
  100.0 2.0 %collective-permute-start.7 = (bf16[8,128,128]{2,1,0:T(8,128)(2,1)S(1)}, bf16[8,128,128]{2,1,0:T(8,128)(2,1)S(1)}, u32[]{:S(2)}, u32[]{:S(2)}) collective-permute-start(bf16[8,128,128]{2,1,0:T(8,128)(2,1)S(1)} %get-tuple-element.26.own1), channel_id=1, source_target_pairs={{0,1},{1,2},{2,3},{3,0},{4,5},{5,6},{6,7},{7,4},{8,9},{9,10},{10,1... | collective-permute-start | bytes 786440 | tf_op jit(solution)/shard_map/ppermute | solution.py:322
  102.0 5.2 %collective-permute-done.3.up0 = bf16[8,128,128]{2,1,0:T(8,128)(2,1)S(1)} collective-permute-done((bf16[8,128,128]{2,1,0:T(8,128)(2,1)S(1)}, bf16[8,128,128]{2,1,0:T(8,128)(2,1)S(1)}, u32[]{:S(2)}, u32[]{:S(2)}) %collective-permute-start.3) | collective-permute-done | bytes 262176 | tf_op jit(solution)/shard_map/ppermute | solution.py:321
  107.2 0.0 collective-permute-start.4
  107.2 0.0 collective-permute-done.5.down1
  107.2 3.2 %collective-permute-start.6 = (bf16[8,128,128]{2,1,0:T(8,128)(2,1)S(1)}, bf16[8,128,128]{2,1,0:T(8,128)(2,1)S(1)}, u32[]{:S(2)}, u32[]{:S(2)}) collective-permute-start(bf16[8,128,128]{2,1,0:T(8,128)(2,1)S(1)} %collective-permute-done.5.down1), channel_id=1, source_target_pairs={{0,3},{1,0},{2,1},{3,2},{4,7},{5,4},{6,5},{7,6},{8,11},{9,8},{10,9... | collective-permute-start | bytes 786440 | tf_op jit(solution)/shard_map/ppermute | solution.py:323
  110.5 1.9 %collective-permute-done.8.down0 = bf16[8,128,128]{2,1,0:T(8,128)(2,1)S(1)} collective-permute-done((bf16[8,128,128]{2,1,0:T(8,128)(2,1)S(1)}, bf16[8,128,128]{2,1,0:T(8,128)(2,1)S(1)}, u32[]{:S(2)}, u32[]{:S(2)}) %collective-permute-start.8) | collective-permute-done | bytes 262176 | tf_op jit(solution)/shard_map/ppermute | solution.py:322
  112.4 0.5 collective-permute-done.7.up1
  112.8 1.8 %spread_near.1._ = f32[16,512,128]{2,1,0:T(8,128)} custom-call(bf16[8,128,128]{2,1,0:T(8,128)(2,1)S(1)} %get-tuple-element.25.own0, bf16[8,128,128]{2,1,0:T(8,128)(2,1)S(1)} %get-tuple-element.26.own1, bf16[8,128,128]{2,1,0:T(8,128)(2,1)S(1)} %collective-permute-done.3.up0, bf16[8,128,128]{2,1,0:T(8,128)(2,1)S(1)} %collective-permute-done.7.up1, ...), custom_call_target="tpu_custom_call" | custom-call | tf_op jit(solution)/shard_map/spread_near/pallas_call | solution.py:325
  114.6 2.2 %collective-permute-done.4.far0 = bf16[8,128,128]{2,1,0:T(8,128)(2,1)S(1)} collective-permute-done((bf16[8,128,128]{2,1,0:T(8,128)(2,1)S(1)}, bf16[8,128,128]{2,1,0:T(8,128)(2,1)S(1)}, u32[]{:S(2)}, u32[]{:S(2)}) %collective-permute-start.4) | collective-permute-done | bytes 262176 | tf_op jit(solution)/shard_map/ppermute | solution.py:323
  116.8 1.0 spread_far.1
  (20 shorter events, 0.0 us)
Async XLA Ops:
  0.0 13.7 %copy-start.6 = (f32[2,128]{1,0:T(2,128)S(1)}, f32[2,128]{1,0:T(2,128)}, u32[]{:S(2)}) copy-start(f32[2,128]{1,0:T(2,128)} %in_bias.5) | copy-start | bytes 3076
  0.0 13.7 %copy-start.5 = (f32[2,128]{1,0:T(2,128)S(1)}, f32[2,128]{1,0:T(2,128)}, u32[]{:S(2)}) copy-start(f32[2,128]{1,0:T(2,128)} %in_gain.5) | copy-start | bytes 3076
  0.0 13.7 %copy-start.2 = (bf16[2,128,4,32]{1,3,2,0:T(8,128)(2,1)S(1)}, bf16[2,128,4,32]{1,3,2,0:T(8,128)(2,1)}, u32[]{:S(2)}) copy-start(bf16[2,128,4,32]{1,3,2,0:T(8,128)(2,1)} %param.13) | copy-start | bytes 196612
  0.0 13.7 %copy-start.7 = (s32[512]{0:T(512)S(1)}, s32[512]{0:T(512)}, u32[]{:S(2)}) copy-start(s32[512]{0:T(512)} %param.10) | copy-start | bytes 6148
  0.0 13.7 %copy-start.3 = (bf16[2,128,128]{2,1,0:T(8,128)(2,1)S(1)}, bf16[2,128,128]{2,1,0:T(8,128)(2,1)}, u32[]{:S(2)}) copy-start(bf16[2,128,128]{2,1,0:T(8,128)(2,1)} %w_gate.3) | copy-start | bytes 196612
  0.0 13.7 %copy-start.4 = (bf16[2,32,128]{2,1,0:T(8,128)(2,1)S(1)}, bf16[2,32,128]{2,1,0:T(8,128)(2,1)}, u32[]{:S(2)}) copy-start(bf16[2,32,128]{2,1,0:T(8,128)(2,1)} %w_out.1) | copy-start | bytes 49156
  0.0 13.7 %copy-start.9 = (f32[2,32]{1,0:T(2,128)S(1)}, f32[2,32]{1,0:T(2,128)}, u32[]{:S(2)}) copy-start(f32[2,32]{1,0:T(2,128)} %out_bias.1) | copy-start | bytes 772
  0.0 13.7 %copy-start.8 = (f32[2,32]{1,0:T(2,128)S(1)}, f32[2,32]{1,0:T(2,128)}, u32[]{:S(2)}) copy-start(f32[2,32]{1,0:T(2,128)} %out_gain.1) | copy-start | bytes 772
  5.2 25.8 %all-to-all-start = ((bf16[32,2,16,512]{3,2,1,0:T(8,128)(2,1)}), bf16[32,2,16,512]{3,2,1,0:T(8,128)(2,1)S(1)}, u32[]{:S(2)}, u32[]{:S(2)}) async-start(bf16[32,2,16,512]{3,2,1,0:T(8,128)(2,1)} %project0.1), calls=%async_computation | async-start | bytes 2097152 | tf_op jit(solution)/shard_map/all_to_all | solution.py:273
  15.7 1.0 copy-start
  16.7 5.6 %collective-permute-start.2 = (bf16[208,128]{1,0:T(8,128)(2,1)S(1)}, bf16[208,128]{1,0:T(8,128)(2,1)S(1)}, u32[]{:S(2)}, u32[]{:S(2)}) collective-permute-start(bf16[208,128]{1,0:T(8,128)(2,1)S(1)} %get-tuple-element.16.own), channel_id=1, source_target_pairs={{0,2},{1,3},{2,0},{3,1},{4,6},{5,7},{6,4},{7,5},{8,10},{9,11},{10,... | collective-permute-start | bytes 159752 | tf_op jit(solution)/shard_map/ppermute | solution.py:293
  19.7 4.1 %collective-permute-start.1 = (bf16[208,128]{1,0:T(8,128)(2,1)S(1)}, bf16[208,128]{1,0:T(8,128)(2,1)S(1)}, u32[]{:S(2)}, u32[]{:S(2)}) collective-permute-start(bf16[208,128]{1,0:T(8,128)(2,1)S(1)} %get-tuple-element.16.own), channel_id=1, source_target_pairs={{0,3},{1,0},{2,1},{3,2},{4,7},{5,4},{6,5},{7,6},{8,11},{9,8},{10,9... | collective-permute-start | bytes 159752 | tf_op jit(solution)/shard_map/ppermute | solution.py:293
  20.9 5.3 %collective-permute-start = (bf16[208,128]{1,0:T(8,128)(2,1)S(1)}, bf16[208,128]{1,0:T(8,128)(2,1)S(1)}, u32[]{:S(2)}, u32[]{:S(2)}) collective-permute-start(bf16[208,128]{1,0:T(8,128)(2,1)S(1)} %get-tuple-element.16.own), channel_id=1, source_target_pairs={{0,1},{1,2},{2,3},{3,0},{4,5},{5,6},{6,7},{7,4},{8,9},{9,10},{10,1... | collective-permute-start | bytes 159752 | tf_op jit(solution)/shard_map/ppermute | solution.py:293
  31.0 20.1 %copy-start.1 = (f32[16,128,128]{2,1,0:T(8,128)S(1)}, f32[16,128,128]{2,1,0:T(8,128)}, u32[]{:S(2)}) copy-start(f32[16,128,128]{2,1,0:T(8,128)} %copy-done) | copy-start | bytes 3145732
  96.7 10.5 %collective-permute-start.3 = (bf16[8,128,128]{2,1,0:T(8,128)(2,1)S(1)}, bf16[8,128,128]{2,1,0:T(8,128)(2,1)S(1)}, u32[]{:S(2)}, u32[]{:S(2)}) collective-permute-start(bf16[8,128,128]{2,1,0:T(8,128)(2,1)S(1)} %get-tuple-element.25.own0), channel_id=1, source_target_pairs={{0,1},{1,2},{2,3},{3,0},{4,5},{5,6},{6,7},{7,4},{8,9},{9,10},{10,1... | collective-permute-start | bytes 786440 | tf_op jit(solution)/shard_map/ppermute | solution.py:321
  97.4 9.9 %collective-permute-start.5 = (bf16[8,128,128]{2,1,0:T(8,128)(2,1)S(1)}, bf16[8,128,128]{2,1,0:T(8,128)(2,1)S(1)}, u32[]{:S(2)}, u32[]{:S(2)}) collective-permute-start(bf16[8,128,128]{2,1,0:T(8,128)(2,1)S(1)} %get-tuple-element.26.own1), channel_id=1, source_target_pairs={{0,3},{1,0},{2,1},{3,2},{4,7},{5,4},{6,5},{7,6},{8,11},{9,8},{10,9... | collective-permute-start | bytes 786440 | tf_op jit(solution)/shard_map/ppermute | solution.py:321
  100.0 12.4 %collective-permute-start.8 = (bf16[8,128,128]{2,1,0:T(8,128)(2,1)S(1)}, bf16[8,128,128]{2,1,0:T(8,128)(2,1)S(1)}, u32[]{:S(2)}, u32[]{:S(2)}) collective-permute-start(bf16[8,128,128]{2,1,0:T(8,128)(2,1)S(1)} %get-tuple-element.25.own0), channel_id=1, source_target_pairs={{0,3},{1,0},{2,1},{3,2},{4,7},{5,4},{6,5},{7,6},{8,11},{9,8},{10,9... | collective-permute-start | bytes 786440 | tf_op jit(solution)/shard_map/ppermute | solution.py:322
  100.0 12.8 %collective-permute-start.7 = (bf16[8,128,128]{2,1,0:T(8,128)(2,1)S(1)}, bf16[8,128,128]{2,1,0:T(8,128)(2,1)S(1)}, u32[]{:S(2)}, u32[]{:S(2)}) collective-permute-start(bf16[8,128,128]{2,1,0:T(8,128)(2,1)S(1)} %get-tuple-element.26.own1), channel_id=1, source_target_pairs={{0,1},{1,2},{2,3},{3,0},{4,5},{5,6},{6,7},{7,4},{8,9},{9,10},{10,1... | collective-permute-start | bytes 786440 | tf_op jit(solution)/shard_map/ppermute | solution.py:322
  107.2 9.6 %collective-permute-start.4 = (bf16[8,128,128]{2,1,0:T(8,128)(2,1)S(1)}, bf16[8,128,128]{2,1,0:T(8,128)(2,1)S(1)}, u32[]{:S(2)}, u32[]{:S(2)}) collective-permute-start(bf16[8,128,128]{2,1,0:T(8,128)(2,1)S(1)} %collective-permute-done.3.up0), channel_id=1, source_target_pairs={{0,1},{1,2},{2,3},{3,0},{4,5},{5,6},{6,7},{7,4},{8,9},{9,10},{10,1... | collective-permute-start | bytes 786440 | tf_op jit(solution)/shard_map/ppermute | solution.py:323
  107.2 9.6 %collective-permute-start.6 = (bf16[8,128,128]{2,1,0:T(8,128)(2,1)S(1)}, bf16[8,128,128]{2,1,0:T(8,128)(2,1)S(1)}, u32[]{:S(2)}, u32[]{:S(2)}) collective-permute-start(bf16[8,128,128]{2,1,0:T(8,128)(2,1)S(1)} %collective-permute-done.5.down1), channel_id=1, source_target_pairs={{0,3},{1,0},{2,1},{3,2},{4,7},{5,4},{6,5},{7,6},{8,11},{9,8},{10,9... | collective-permute-start | bytes 786440 | tf_op jit(solution)/shard_map/ppermute | solution.py:323

commit v7 on v6

--- a/solution.py
+++ b/solution.py
@@ -210,17 +210,12 @@
         copy.wait()
 
 
-def spread_far_kernel(far0, far1, _, out, buf, sems):
+def spread_far_kernel(row, far, _, out, buf, sem):
     at = pl.multiple_of(lax.rem(lax.axis_index("ch") + 2, G) * T, T)
-    copies = []
-    for k, far in enumerate((far0, far1)):
-        buf[k] = far[...].astype(F32)
-        copies.append(
-            pltpu.make_async_copy(buf.at[k], out.at[pl.ds(k * HB, HB), pl.ds(at, T), :], sems.at[k])
-        )
-        copies[-1].start()
-    for copy in copies:
-        copy.wait()
+    buf[...] = far[...].astype(F32)
+    copy = pltpu.make_async_copy(buf, out.at[pl.ds(row, HB), pl.ds(at, T), :], sem)
+    copy.start()
+    copy.wait()
 
 
 def params(limit=VMEM_LIMIT):
@@ -331,16 +326,18 @@
         compiler_params=params(),
         name="spread_near",
     )(z0, z1, up0, up1, down0, down1)
-    return pl.pallas_call(
-        spread_far_kernel,
-        out_shape=whole,
-        in_specs=[pl.BlockSpec(memory_space=VMEM)] * 2 + [pl.BlockSpec(memory_space=HBM)],
-        out_specs=pl.BlockSpec(memory_space=HBM),
-        scratch_shapes=[pltpu.VMEM((2, HB, T, C), F32), dma((2,))],
-        input_output_aliases={2: 0},
-        compiler_params=params(),
-        name="spread_far",
-    )(far0, far1, near)
+    for row, far in ((0, far0), (HB, far1)):
+        near = pl.pallas_call(
+            functools.partial(spread_far_kernel, row),
+            out_shape=whole,
+            in_specs=[pl.BlockSpec(memory_space=VMEM), pl.BlockSpec(memory_space=HBM)],
+            out_specs=pl.BlockSpec(memory_space=HBM),
+            scratch_shapes=[pltpu.VMEM((HB, T, C), F32), dma],
+            input_output_aliases={1: 0},
+            compiler_params=params(),
+            name="spread_far",
+        )(far, near)
+    return near
 
 
 def solution(mesh):

time: 118 us -> 119 us (level)
  starting transfers between devices: 22 us -> 23.3 us
  waiting for transfers between devices: 18.6 us -> 17.4 us
    ppermute x2, starting transfers between devices: 2.03 us -> 3.24 us  [on_device(): up1, down0 = (up(z1), down(z0))]
    ppermute x2, waiting for transfers between devices: 5.19 us -> 3.98 us  [on_device(): up0, down1 = (up(z0), down(z1))]
  transfers between devices with their start and end apart: 10 -> 10, of which waited for: 8 -> 7; matrix products, arithmetic and copies ran while one was open for 0% -> 0% of each run, Pallas kernels for 4% -> 4%
where the time goes in v7:
time: 119 us
  blocking collectives  61.3 us (52%)
  starting transfers between devices  23.3 us (20%)
  waiting for transfers between devices  17.4 us (15%)
  Pallas kernels  15.4 us (13%)
    all_to_all x2, blocking collectives, on_device(): y = lax.all_to_all(x.reshape(G * R, RB, T), ('ch', 'row'), 0, 0)  37.6 us
    all_to_all x1, blocking collectives, on_device(): b = lax.all_to_all(b, ('ch', 'row'), 0, 0)  23.7 us
    pallas_call x7, Pallas kernels, call(): pl.pallas_call(kernel, out_shape=outs, in_specs=[pl.BlockSpec(memory_spac...  11.9 us
    all_to_all x1, starting transfers between devices, on_device(): sent = lax.all_to_all(a, 'row', 0, 0)  8.42 us
    all_to_all x1, waiting for transfers between devices, on_device(): sent = lax.all_to_all(a, 'row', 0, 0)  4.36 us
    ppermute x2, waiting for transfers between devices, on_device(): up0, down1 = (up(z0), down(z1))  3.98 us
    ppermute x2, starting transfers between devices, on_device(): up0, down1 = (up(z0), down(z1))  3.31 us
    ppermute x2, starting transfers between devices, on_device(): far0, far1 = (up(up0), down(down1))  3.24 us
  transfers between devices with their start and end apart: 10, of which 7 were waited for; matrix products, arithmetic and copies ran while one was open for 0% of the time, Pallas kernels for 4%

profile of v7, /device:TPU:0, one launch (start us, length us, event | category | flops | bytes accessed | tf_op | source)
XLA Modules:
  0.0 118.5 jit_solution(14505850265161983241)
XLA Ops:
  0.0 5.2 %project0.1 = bf16[32,2,16,512]{3,2,1,0:T(8,128)(2,1)} custom-call(f32[16,512,128]{2,1,0:T(8,128)} %pair.3, s32[1,512]{1,0:T(1,128)} %bitcast.10, f32[2,128]{1,0:T(2,128)} %in_gain.5, f32[2,128]{1,0:T(2,128)} %in_bias.5, bf16[2,128,128]{2,1,0:T(8,128)(2,1)} %bitcast.8), custom_call_target="tpu_custom_call" | custom-call | tf_op jit(solution)/shard_map/project0/pallas_call | solution.py:226
  5.2 8.4 %all-to-all-start = ((bf16[32,2,16,512]{3,2,1,0:T(8,128)(2,1)}), bf16[32,2,16,512]{3,2,1,0:T(8,128)(2,1)S(1)}, u32[]{:S(2)}, u32[]{:S(2)}) async-start(bf16[32,2,16,512]{3,2,1,0:T(8,128)(2,1)} %project0.1), calls=%async_computation | async-start | bytes 2097152 | tf_op jit(solution)/shard_map/all_to_all | solution.py:268
  13.7 2.0 %gate0.1 = (f32[16,128,128]{2,1,0:T(8,128)S(1)}, f32[16,128,128]{2,1,0:T(8,128)S(1)}, f32[16,128]{1,0:T(8,128)S(1)}, bf16[208,128]{1,0:T(8,128)(2,1)S(1)}) custom-call(f32[16,512,128]{2,1,0:T(8,128)} %pair.3, s32[1,512]{1,0:T(1,128)S(1)} %bitcast.11, f32[2,128]{1,0:T(2,128)S(1)} %copy-done.5, f32[2,128]{1,0:T(2,128)S(1)} %copy-done.6, ...), custom_call_target="tpu_custom_call" | custom-call | tf_op jit(solution)/shard_map/gate0/pallas_call | solution.py:226
  15.7 1.0 copy-done
  16.7 3.0 %collective-permute-start.2 = (bf16[208,128]{1,0:T(8,128)(2,1)S(1)}, bf16[208,128]{1,0:T(8,128)(2,1)S(1)}, u32[]{:S(2)}, u32[]{:S(2)}) collective-permute-start(bf16[208,128]{1,0:T(8,128)(2,1)S(1)} %get-tuple-element.16.own), channel_id=1, source_target_pairs={{0,2},{1,3},{2,0},{3,1},{4,6},{5,7},{6,4},{7,5},{8,10},{9,11},{10,... | collective-permute-start | bytes 159752 | tf_op jit(solution)/shard_map/ppermute | solution.py:288
  19.7 1.1 collective-permute-start.1
  20.9 0.9 collective-permute-start
  21.7 0.6 collective-permute-done.2.far
  22.3 1.5 %collective-permute-done.1.down = bf16[208,128]{1,0:T(8,128)(2,1)S(1)} collective-permute-done((bf16[208,128]{1,0:T(8,128)(2,1)S(1)}, bf16[208,128]{1,0:T(8,128)(2,1)S(1)}, u32[]{:S(2)}, u32[]{:S(2)}) %collective-permute-start.1) | collective-permute-done | bytes 53280 | tf_op jit(solution)/shard_map/ppermute | solution.py:288
  23.9 2.4 %collective-permute-done.up = bf16[208,128]{1,0:T(8,128)(2,1)S(1)} collective-permute-done((bf16[208,128]{1,0:T(8,128)(2,1)S(1)}, bf16[208,128]{1,0:T(8,128)(2,1)S(1)}, u32[]{:S(2)}, u32[]{:S(2)}) %collective-permute-start) | collective-permute-done | bytes 53280 | tf_op jit(solution)/shard_map/ppermute | solution.py:288
  26.2 0.4 weights.1
  26.6 4.4 %all-to-all-done.a = bf16[32,2,16,512]{3,2,1,0:T(8,128)(2,1)S(1)} async-done(((bf16[32,2,16,512]{3,2,1,0:T(8,128)(2,1)}), bf16[32,2,16,512]{3,2,1,0:T(8,128)(2,1)S(1)}, u32[]{:S(2)}, u32[]{:S(2)}) %all-to-all-start) | async-done | bytes 1048608 | tf_op jit(solution)/shard_map/all_to_all | solution.py:268
  31.0 0.5 outgoing.1
  31.5 19.7 %all_to_all.20.y = bf16[128,16,128]{2,1,0:T(8,128)(2,1)S(1)} all-to-all(bf16[128,16,128]{2,1,0:T(8,128)(2,1)S(1)} %bitcast.7), channel_id=1, replica_groups=mesh['row'=32,'ch'=4] {'ch','row'}, dimensions={0} | all-to-all | bytes 1048576 | tf_op jit(solution)/shard_map/all_to_all | solution.py:297
  51.1 2.2 %middle.1 = (f32[16,128,128]{2,1,0:T(8,128)S(1)}, bf16[16,128,128]{2,1,0:T(8,128)(2,1)S(1)}, bf16[128,2,16,128]{3,2,1,0:T(8,128)(2,1)S(1)}) custom-call(bf16[128,16,128]{2,1,0:T(8,128)(2,1)S(1)} %all_to_all.20.y, f32[16,128,128]{2,1,0:T(8,128)S(1)} %copy-done.1, f32[16,128,128]{2,1,0:T(8,128)S(1)} %get-tuple-element.18._gate.gate, ...), custom_call_target="tpu_custom_call" | custom-call | tf_op jit(solution)/shard_map/middle/pallas_call | solution.py:226
  53.4 23.7 %all_to_all.21.b = bf16[128,2,16,128]{3,2,1,0:T(8,128)(2,1)S(1)} all-to-all(bf16[128,2,16,128]{3,2,1,0:T(8,128)(2,1)S(1)} %get-tuple-element.22), channel_id=1, replica_groups=mesh['row'=32,'ch'=4] {'ch','row'}, dimensions={0} | all-to-all | bytes 2097152 | tf_op jit(solution)/shard_map/all_to_all | solution.py:305
  77.1 0.5 incoming.1
  77.5 18.0 %all_to_all.22.y = bf16[128,16,128]{2,1,0:T(8,128)(2,1)S(1)} all-to-all(bf16[128,16,128]{2,1,0:T(8,128)(2,1)S(1)} %bitcast.6), channel_id=1, replica_groups=mesh['row'=32,'ch'=4] {'ch','row'}, dimensions={0} | all-to-all | bytes 1048576 | tf_op jit(solution)/shard_map/all_to_all | solution.py:307
  95.5 1.2 %last.1 = (bf16[8,128,128]{2,1,0:T(8,128)(2,1)S(1)}, bf16[8,128,128]{2,1,0:T(8,128)(2,1)S(1)}) custom-call(bf16[128,16,128]{2,1,0:T(8,128)(2,1)S(1)} %all_to_all.22.y, f32[16,128,128]{2,1,0:T(8,128)S(1)} %get-tuple-element.23.state, bf16[16,128,128]{2,1,0:T(8,128)(2,1)S(1)} %get-tuple-element.24.normed, bf16[2,128,128]{2,1,0:T(8,128)(2,1)S(1)} %copy-done.3, ...), custom_call_target="tpu_custom_call" | custom-call | tf_op jit(solution)/shard_map/last/pallas_call | solution.py:226
  96.7 0.6 collective-permute-start.5
  97.4 2.7 %collective-permute-start.3 = (bf16[8,128,128]{2,1,0:T(8,128)(2,1)S(1)}, bf16[8,128,128]{2,1,0:T(8,128)(2,1)S(1)}, u32[]{:S(2)}, u32[]{:S(2)}) collective-permute-start(bf16[8,128,128]{2,1,0:T(8,128)(2,1)S(1)} %get-tuple-element.25.own1), channel_id=1, source_target_pairs={{0,3},{1,0},{2,1},{3,2},{4,7},{5,4},{6,5},{7,6},{8,11},{9,8},{10,9... | collective-permute-start | bytes 786440 | tf_op jit(solution)/shard_map/ppermute | solution.py:316
  100.0 0.0 collective-permute-start.7
  100.0 3.2 %collective-permute-start.8 = (bf16[8,128,128]{2,1,0:T(8,128)(2,1)S(1)}, bf16[8,128,128]{2,1,0:T(8,128)(2,1)S(1)}, u32[]{:S(2)}, u32[]{:S(2)}) collective-permute-start(bf16[8,128,128]{2,1,0:T(8,128)(2,1)S(1)} %get-tuple-element.26.own0), channel_id=1, source_target_pairs={{0,3},{1,0},{2,1},{3,2},{4,7},{5,4},{6,5},{7,6},{8,11},{9,8},{10,9... | collective-permute-start | bytes 786440 | tf_op jit(solution)/shard_map/ppermute | solution.py:317
  103.2 4.0 %collective-permute-done.5.up0 = bf16[8,128,128]{2,1,0:T(8,128)(2,1)S(1)} collective-permute-done((bf16[8,128,128]{2,1,0:T(8,128)(2,1)S(1)}, bf16[8,128,128]{2,1,0:T(8,128)(2,1)S(1)}, u32[]{:S(2)}, u32[]{:S(2)}) %collective-permute-start.5) | collective-permute-done | bytes 262176 | tf_op jit(solution)/shard_map/ppermute | solution.py:316
  107.2 0.0 collective-permute-start.6
  107.2 0.0 collective-permute-done.3.down1
  107.2 3.2 %collective-permute-start.4 = (bf16[8,128,128]{2,1,0:T(8,128)(2,1)S(1)}, bf16[8,128,128]{2,1,0:T(8,128)(2,1)S(1)}, u32[]{:S(2)}, u32[]{:S(2)}) collective-permute-start(bf16[8,128,128]{2,1,0:T(8,128)(2,1)S(1)} %collective-permute-done.3.down1), channel_id=1, source_target_pairs={{0,3},{1,0},{2,1},{3,2},{4,7},{5,4},{6,5},{7,6},{8,11},{9,8},{10,9... | collective-permute-start | bytes 786440 | tf_op jit(solution)/shard_map/ppermute | solution.py:318
  110.5 2.4 %collective-permute-done.7.up1 = bf16[8,128,128]{2,1,0:T(8,128)(2,1)S(1)} collective-permute-done((bf16[8,128,128]{2,1,0:T(8,128)(2,1)S(1)}, bf16[8,128,128]{2,1,0:T(8,128)(2,1)S(1)}, u32[]{:S(2)}, u32[]{:S(2)}) %collective-permute-start.7) | collective-permute-done | bytes 262176 | tf_op jit(solution)/shard_map/ppermute | solution.py:317
  112.8 1.8 %spread_near.1._ = f32[16,512,128]{2,1,0:T(8,128)} custom-call(bf16[8,128,128]{2,1,0:T(8,128)(2,1)S(1)} %get-tuple-element.26.own0, bf16[8,128,128]{2,1,0:T(8,128)(2,1)S(1)} %get-tuple-element.25.own1, bf16[8,128,128]{2,1,0:T(8,128)(2,1)S(1)} %collective-permute-done.5.up0, bf16[8,128,128]{2,1,0:T(8,128)(2,1)S(1)} %collective-permute-done.7.up1, ...), custom_call_target="tpu_custom_call" | custom-call | tf_op jit(solution)/shard_map/spread_near/pallas_call | solution.py:320
  114.6 2.2 %collective-permute-done.6.far = bf16[8,128,128]{2,1,0:T(8,128)(2,1)S(1)} collective-permute-done((bf16[8,128,128]{2,1,0:T(8,128)(2,1)S(1)}, bf16[8,128,128]{2,1,0:T(8,128)(2,1)S(1)}, u32[]{:S(2)}, u32[]{:S(2)}) %collective-permute-start.6) | collective-permute-done | bytes 262176 | tf_op jit(solution)/shard_map/ppermute | solution.py:318
  116.8 0.8 spread_far.2._
  117.7 0.8 spread_far.3
  (21 shorter events, 0.0 us)
Async XLA Ops:
  0.0 13.7 %copy-start.6 = (f32[2,128]{1,0:T(2,128)S(1)}, f32[2,128]{1,0:T(2,128)}, u32[]{:S(2)}) copy-start(f32[2,128]{1,0:T(2,128)} %in_bias.5) | copy-start | bytes 3076
  0.0 13.7 %copy-start.5 = (f32[2,128]{1,0:T(2,128)S(1)}, f32[2,128]{1,0:T(2,128)}, u32[]{:S(2)}) copy-start(f32[2,128]{1,0:T(2,128)} %in_gain.5) | copy-start | bytes 3076
  0.0 13.7 %copy-start.2 = (bf16[2,128,4,32]{1,3,2,0:T(8,128)(2,1)S(1)}, bf16[2,128,4,32]{1,3,2,0:T(8,128)(2,1)}, u32[]{:S(2)}) copy-start(bf16[2,128,4,32]{1,3,2,0:T(8,128)(2,1)} %param.13) | copy-start | bytes 196612
  0.0 13.7 %copy-start.7 = (s32[512]{0:T(512)S(1)}, s32[512]{0:T(512)}, u32[]{:S(2)}) copy-start(s32[512]{0:T(512)} %param.10) | copy-start | bytes 6148
  0.0 13.7 %copy-start.3 = (bf16[2,128,128]{2,1,0:T(8,128)(2,1)S(1)}, bf16[2,128,128]{2,1,0:T(8,128)(2,1)}, u32[]{:S(2)}) copy-start(bf16[2,128,128]{2,1,0:T(8,128)(2,1)} %w_gate.3) | copy-start | bytes 196612
  0.0 13.7 %copy-start.4 = (bf16[2,32,128]{2,1,0:T(8,128)(2,1)S(1)}, bf16[2,32,128]{2,1,0:T(8,128)(2,1)}, u32[]{:S(2)}) copy-start(bf16[2,32,128]{2,1,0:T(8,128)(2,1)} %w_out.1) | copy-start | bytes 49156
  0.0 13.7 %copy-start.9 = (f32[2,32]{1,0:T(2,128)S(1)}, f32[2,32]{1,0:T(2,128)}, u32[]{:S(2)}) copy-start(f32[2,32]{1,0:T(2,128)} %out_bias.1) | copy-start | bytes 772
  0.0 13.7 %copy-start.8 = (f32[2,32]{1,0:T(2,128)S(1)}, f32[2,32]{1,0:T(2,128)}, u32[]{:S(2)}) copy-start(f32[2,32]{1,0:T(2,128)} %out_gain.1) | copy-start | bytes 772
  5.2 25.8 %all-to-all-start = ((bf16[32,2,16,512]{3,2,1,0:T(8,128)(2,1)}), bf16[32,2,16,512]{3,2,1,0:T(8,128)(2,1)S(1)}, u32[]{:S(2)}, u32[]{:S(2)}) async-start(bf16[32,2,16,512]{3,2,1,0:T(8,128)(2,1)} %project0.1), calls=%async_computation | async-start | bytes 2097152 | tf_op jit(solution)/shard_map/all_to_all | solution.py:268
  15.7 1.0 copy-start
  16.7 5.6 %collective-permute-start.2 = (bf16[208,128]{1,0:T(8,128)(2,1)S(1)}, bf16[208,128]{1,0:T(8,128)(2,1)S(1)}, u32[]{:S(2)}, u32[]{:S(2)}) collective-permute-start(bf16[208,128]{1,0:T(8,128)(2,1)S(1)} %get-tuple-element.16.own), channel_id=1, source_target_pairs={{0,2},{1,3},{2,0},{3,1},{4,6},{5,7},{6,4},{7,5},{8,10},{9,11},{10,... | collective-permute-start | bytes 159752 | tf_op jit(solution)/shard_map/ppermute | solution.py:288
  19.7 4.1 %collective-permute-start.1 = (bf16[208,128]{1,0:T(8,128)(2,1)S(1)}, bf16[208,128]{1,0:T(8,128)(2,1)S(1)}, u32[]{:S(2)}, u32[]{:S(2)}) collective-permute-start(bf16[208,128]{1,0:T(8,128)(2,1)S(1)} %get-tuple-element.16.own), channel_id=1, source_target_pairs={{0,3},{1,0},{2,1},{3,2},{4,7},{5,4},{6,5},{7,6},{8,11},{9,8},{10,9... | collective-permute-start | bytes 159752 | tf_op jit(solution)/shard_map/ppermute | solution.py:288
  20.9 5.3 %collective-permute-start = (bf16[208,128]{1,0:T(8,128)(2,1)S(1)}, bf16[208,128]{1,0:T(8,128)(2,1)S(1)}, u32[]{:S(2)}, u32[]{:S(2)}) collective-permute-start(bf16[208,128]{1,0:T(8,128)(2,1)S(1)} %get-tuple-element.16.own), channel_id=1, source_target_pairs={{0,1},{1,2},{2,3},{3,0},{4,5},{5,6},{6,7},{7,4},{8,9},{9,10},{10,1... | collective-permute-start | bytes 159752 | tf_op jit(solution)/shard_map/ppermute | solution.py:288
  31.0 20.1 %copy-start.1 = (f32[16,128,128]{2,1,0:T(8,128)S(1)}, f32[16,128,128]{2,1,0:T(8,128)}, u32[]{:S(2)}) copy-start(f32[16,128,128]{2,1,0:T(8,128)} %copy-done) | copy-start | bytes 3145732
  96.7 10.5 %collective-permute-start.5 = (bf16[8,128,128]{2,1,0:T(8,128)(2,1)S(1)}, bf16[8,128,128]{2,1,0:T(8,128)(2,1)S(1)}, u32[]{:S(2)}, u32[]{:S(2)}) collective-permute-start(bf16[8,128,128]{2,1,0:T(8,128)(2,1)S(1)} %get-tuple-element.26.own0), channel_id=1, source_target_pairs={{0,1},{1,2},{2,3},{3,0},{4,5},{5,6},{6,7},{7,4},{8,9},{9,10},{10,1... | collective-permute-start | bytes 786440 | tf_op jit(solution)/shard_map/ppermute | solution.py:316
  97.4 9.9 %collective-permute-start.3 = (bf16[8,128,128]{2,1,0:T(8,128)(2,1)S(1)}, bf16[8,128,128]{2,1,0:T(8,128)(2,1)S(1)}, u32[]{:S(2)}, u32[]{:S(2)}) collective-permute-start(bf16[8,128,128]{2,1,0:T(8,128)(2,1)S(1)} %get-tuple-element.25.own1), channel_id=1, source_target_pairs={{0,3},{1,0},{2,1},{3,2},{4,7},{5,4},{6,5},{7,6},{8,11},{9,8},{10,9... | collective-permute-start | bytes 786440 | tf_op jit(solution)/shard_map/ppermute | solution.py:316
  100.0 12.8 %collective-permute-start.7 = (bf16[8,128,128]{2,1,0:T(8,128)(2,1)S(1)}, bf16[8,128,128]{2,1,0:T(8,128)(2,1)S(1)}, u32[]{:S(2)}, u32[]{:S(2)}) collective-permute-start(bf16[8,128,128]{2,1,0:T(8,128)(2,1)S(1)} %get-tuple-element.25.own1), channel_id=1, source_target_pairs={{0,1},{1,2},{2,3},{3,0},{4,5},{5,6},{6,7},{7,4},{8,9},{9,10},{10,1... | collective-permute-start | bytes 786440 | tf_op jit(solution)/shard_map/ppermute | solution.py:317
  100.0 12.8 %collective-permute-start.8 = (bf16[8,128,128]{2,1,0:T(8,128)(2,1)S(1)}, bf16[8,128,128]{2,1,0:T(8,128)(2,1)S(1)}, u32[]{:S(2)}, u32[]{:S(2)}) collective-permute-start(bf16[8,128,128]{2,1,0:T(8,128)(2,1)S(1)} %get-tuple-element.26.own0), channel_id=1, source_target_pairs={{0,3},{1,0},{2,1},{3,2},{4,7},{5,4},{6,5},{7,6},{8,11},{9,8},{10,9... | collective-permute-start | bytes 786440 | tf_op jit(solution)/shard_map/ppermute | solution.py:317
  107.2 9.6 %collective-permute-start.6 = (bf16[8,128,128]{2,1,0:T(8,128)(2,1)S(1)}, bf16[8,128,128]{2,1,0:T(8,128)(2,1)S(1)}, u32[]{:S(2)}, u32[]{:S(2)}) collective-permute-start(bf16[8,128,128]{2,1,0:T(8,128)(2,1)S(1)} %collective-permute-done.5.up0), channel_id=1, source_target_pairs={{0,1},{1,2},{2,3},{3,0},{4,5},{5,6},{6,7},{7,4},{8,9},{9,10},{10,1... | collective-permute-start | bytes 786440 | tf_op jit(solution)/shard_map/ppermute | solution.py:318
  107.2 10.5 %collective-permute-start.4 = (bf16[8,128,128]{2,1,0:T(8,128)(2,1)S(1)}, bf16[8,128,128]{2,1,0:T(8,128)(2,1)S(1)}, u32[]{:S(2)}, u32[]{:S(2)}) collective-permute-start(bf16[8,128,128]{2,1,0:T(8,128)(2,1)S(1)} %collective-permute-done.3.down1), channel_id=1, source_target_pairs={{0,3},{1,0},{2,1},{3,2},{4,7},{5,4},{6,5},{7,6},{8,11},{9,8},{10,9... | collective-permute-start | bytes 786440 | tf_op jit(solution)/shard_map/ppermute | solution.py:318

commit v8 on v6

--- a/solution.py
+++ b/solution.py
@@ -40,8 +40,14 @@
     return 0.5 * jnp.tanh(0.5 * v) + 0.5
 
 
-def gated(gate, value, half_mask):
-    return (jnp.tanh(0.5 * gate) + 1.0) * (value * half_mask)
+def gated(half_gate, value, half_mask):
+    return (jnp.tanh(half_gate) + 1.0) * (value * half_mask)
+
+
+def halve_gates(w):
+    row = lax.broadcasted_iota(jnp.int32, w.shape, 0)
+    is_gate = (row < D) | ((row >= 2 * D) & (row < 3 * D))
+    return jnp.where(is_gate, 0.5 * w.astype(F32), w.astype(F32)).astype(BF16)
 
 
 def project0_kernel(
@@ -65,6 +71,7 @@
         if h == 1:
             for copy in copies[2:few]:
                 copy.wait()
+            w_v[...] = halve_gates(w_v[...])
             cols = mask_v[...].astype(F32) * 0.5
         for i in range(0, RB, 2):
             if h < G:
@@ -120,14 +127,14 @@
         gate[i] = sigmoid(dot(w_g, norm_cols(z, gain, bias).astype(BF16)))
 
 
-def weights_kernel(own, up, down, far, in_gain, in_bias, w, norms, pk):
+def weights_kernel(own, up, down, far, in_gain, in_bias, w_gate, w, norms, pk):
     g = lax.axis_index("ch")
     pk[g] = own[...]
     pk[lax.rem(g + 3, G)] = up[...]
     pk[lax.rem(g + 1, G)] = down[...]
     pk[lax.rem(g + 2, G)] = far[...]
     for k in range(G):
-        w[k] = pk[k, PK_PROJ : PK_PROJ + C]
+        w[k] = halve_gates(pk[k, PK_PROJ : PK_PROJ + C])
     for k in range(G):
         parts = pk[k, PK_NORM:].astype(F32)
         parts = parts[0:4] + parts[4:8] + parts[8:12]
@@ -137,12 +144,13 @@
         rows = jnp.concatenate(
             [pk[k, PK_OUT + D * layer : PK_OUT + D * (layer + 1)] for k in range(G)], 0
         )
-        w[G + layer] = rows.astype(F32).T.astype(BF16)
+        w[G + layer] = (rows.astype(F32).T * (1.0, 0.5)[layer]).astype(BF16)
+    w[G + 2] = (0.5 * w_gate[1].astype(F32).T).astype(BF16)
     norms[4] = column(in_gain[1:2, :])
     norms[5] = column(in_bias[1:2, :])
 
 
-def outgoing_kernel(a, _w, _gate, out):
+def outgoing_kernel(a, _w, _gate, _state, _norms, _half, out):
     left = a[:, 0].reshape(N, N)
     for h in range(0, G, 4):
         right = a[8 * h : 8 * (h + 4), 1].reshape(T * 4, N)
@@ -186,13 +194,12 @@
     out[:, 1] = right_s[...].reshape(C, RB, T).astype(BF16)
 
 
-def last_kernel(y, state, normed, w_gate, w, norms, out0, out1, ys):
-    w_g = w_gate[1].astype(F32).T.astype(BF16)
+def last_kernel(y, state, normed, w, norms, out0, out1, ys):
     ys[...] = y[...].astype(F32).reshape(C * RB, T)
     for i in range(RB):
         hidden = norm_cols(ys[pl.ds(i, C, stride=RB), :], norms[1], norms[3]).astype(BF16)
-        gate = sigmoid(dot(w_g, normed[i]))
-        z = state[i] + gate * dot(w[G + 1], hidden)
+        twice_gate = jnp.tanh(dot(w[G + 2], normed[i])) + 1.0
+        z = state[i] + twice_gate * dot(w[G + 1], hidden)
         out = (out0, out1)[i // HB]
         out[i % HB] = z.T.astype(BF16)
 
@@ -288,16 +295,16 @@
     w, norms = call(
         weights_kernel,
         "weights",
-        (arr((G + 2, C, C), BF16), arr((6, C, T), F32)),
+        (arr((G + 3, C, C), BF16), arr((6, C, T), F32)),
         [pltpu.VMEM((G, PK, C), BF16)],
-        [(v, VMEM) for v in (own, up(own), down(own), cross(own), in_gain, in_bias)],
+        [(v, VMEM) for v in (own, up(own), down(own), cross(own), in_gain, in_bias, w_gate)],
     )
     x = call(
         outgoing_kernel,
         "outgoing",
         arr((G, R, RB, T), BF16),
         [],
-        [(sent, VMEM)] + [(v, pl.ANY) for v in (w, gate)],
+        [(sent, VMEM)] + [(v, pl.ANY) for v in (w, gate, state, norms, half_mask)],
     )
     y = lax.all_to_all(x.reshape(G * R, RB, T), ("ch", "row"), 0, 0)
     state, normed, b = call(
@@ -316,7 +323,7 @@
         "last",
         (half, half),
         [pltpu.VMEM((C * RB, T), F32)],
-        [(v, VMEM) for v in (y, state, normed, w_gate, w, norms)],
+        [(v, VMEM) for v in (y, state, normed, w, norms)],
     )
     up0, down1 = up(z0), down(z1)
     up1, down0 = up(z1), down(z0)

time: 118 us -> 119 us (level)
  no operation moved by 1% of the time
where the time goes in v8:
time: 119 us
  blocking collectives  61.3 us (52%)
  starting transfers between devices  22.1 us (19%)
  waiting for transfers between devices  18.8 us (16%)
  Pallas kernels  14.7 us (12%)
  local copies, waits for them, and re-layouts  1.67 us (1%)
    all_to_all x2, blocking collectives, on_device(): y = lax.all_to_all(x.reshape(G * R, RB, T), ('ch', 'row'), 0, 0)  37.6 us
    all_to_all x1, blocking collectives, on_device(): b = lax.all_to_all(b, ('ch', 'row'), 0, 0)  23.7 us
    pallas_call x7, Pallas kernels, call(): pl.pallas_call(kernel, out_shape=outs, in_specs=[pl.BlockSpec(memory_spac...  11.9 us
    all_to_all x1, starting transfers between devices, on_device(): sent = lax.all_to_all(a, 'row', 0, 0)  8.43 us
    ppermute x2, waiting for transfers between devices, on_device(): up0, down1 = (up(z0), down(z1))  5.19 us
    all_to_all x1, waiting for transfers between devices, on_device(): sent = lax.all_to_all(a, 'row', 0, 0)  4.52 us
    ppermute x2, starting transfers between devices, on_device(): up0, down1 = (up(z0), down(z1))  3.31 us
    ppermute x2, starting transfers between devices, on_device(): far0, far1 = (up(up0), down(down1))  3.24 us
  transfers between devices with their start and end apart: 10, of which 8 were waited for; matrix products, arithmetic and copies ran while one was open for 0% of the time, Pallas kernels for 4%

profile of v8, /device:TPU:0, one launch (start us, length us, event | category | flops | bytes accessed | tf_op | source)
XLA Modules:
  0.0 118.7 jit_solution(8870284939452753864)
XLA Ops:
  0.0 5.1 %project0.1 = bf16[32,2,16,512]{3,2,1,0:T(8,128)(2,1)} custom-call(f32[16,512,128]{2,1,0:T(8,128)} %pair.3, s32[1,512]{1,0:T(1,128)} %bitcast.10, f32[2,128]{1,0:T(2,128)} %in_gain.5, f32[2,128]{1,0:T(2,128)} %in_bias.5, bf16[2,128,128]{2,1,0:T(8,128)(2,1)} %bitcast.8), custom_call_target="tpu_custom_call" | custom-call | tf_op jit(solution)/shard_map/project0/pallas_call | solution.py:238
  5.2 8.4 %all-to-all-start = ((bf16[32,2,16,512]{3,2,1,0:T(8,128)(2,1)}), bf16[32,2,16,512]{3,2,1,0:T(8,128)(2,1)S(1)}, u32[]{:S(2)}, u32[]{:S(2)}) async-start(bf16[32,2,16,512]{3,2,1,0:T(8,128)(2,1)} %project0.1), calls=%async_computation | async-start | bytes 2097152 | tf_op jit(solution)/shard_map/all_to_all | solution.py:280
  13.7 0.0 copy-start.5
  13.7 2.0 %gate0.1 = (f32[16,128,128]{2,1,0:T(8,128)S(1)}, f32[16,128,128]{2,1,0:T(8,128)S(1)}, f32[16,128]{1,0:T(8,128)S(1)}, bf16[208,128]{1,0:T(8,128)(2,1)S(1)}) custom-call(f32[16,512,128]{2,1,0:T(8,128)} %pair.3, s32[1,512]{1,0:T(1,128)S(1)} %bitcast.11, f32[2,128]{1,0:T(2,128)S(1)} %copy-done.7, f32[2,128]{1,0:T(2,128)S(1)} %copy-done.8, ...), custom_call_target="tpu_custom_call" | custom-call | tf_op jit(solution)/shard_map/gate0/pallas_call | solution.py:238
  15.7 3.1 %collective-permute-start.2 = (bf16[208,128]{1,0:T(8,128)(2,1)S(1)}, bf16[208,128]{1,0:T(8,128)(2,1)S(1)}, u32[]{:S(2)}, u32[]{:S(2)}) collective-permute-start(bf16[208,128]{1,0:T(8,128)(2,1)S(1)} %get-tuple-element.16.own), channel_id=1, source_target_pairs={{0,2},{1,3},{2,0},{3,1},{4,6},{5,7},{6,4},{7,5},{8,10},{9,11},{10,... | collective-permute-start | bytes 159752 | tf_op jit(solution)/shard_map/ppermute | solution.py:300
  18.8 1.1 collective-permute-start.1
  20.0 0.9 collective-permute-start
  20.9 0.6 collective-permute-done.2.far
  21.4 1.5 %collective-permute-done.1.down = bf16[208,128]{1,0:T(8,128)(2,1)S(1)} collective-permute-done((bf16[208,128]{1,0:T(8,128)(2,1)S(1)}, bf16[208,128]{1,0:T(8,128)(2,1)S(1)}, u32[]{:S(2)}, u32[]{:S(2)}) %collective-permute-start.1) | collective-permute-done | bytes 53280 | tf_op jit(solution)/shard_map/ppermute | solution.py:300
  23.0 2.3 %collective-permute-done.up = bf16[208,128]{1,0:T(8,128)(2,1)S(1)} collective-permute-done((bf16[208,128]{1,0:T(8,128)(2,1)S(1)}, bf16[208,128]{1,0:T(8,128)(2,1)S(1)}, u32[]{:S(2)}, u32[]{:S(2)}) %collective-permute-start) | collective-permute-done | bytes 53280 | tf_op jit(solution)/shard_map/ppermute | solution.py:300
  25.3 0.4 weights.1
  25.8 0.7 copy-done
  26.4 4.5 %all-to-all-done.a = bf16[32,2,16,512]{3,2,1,0:T(8,128)(2,1)S(1)} async-done(((bf16[32,2,16,512]{3,2,1,0:T(8,128)(2,1)}), bf16[32,2,16,512]{3,2,1,0:T(8,128)(2,1)S(1)}, u32[]{:S(2)}, u32[]{:S(2)}) %all-to-all-start) | async-done | bytes 1048608 | tf_op jit(solution)/shard_map/all_to_all | solution.py:280
  31.0 0.9 copy-done.1
  31.9 0.5 outgoing.1
  32.4 19.7 %all_to_all.20.y = bf16[128,16,128]{2,1,0:T(8,128)(2,1)S(1)} all-to-all(bf16[128,16,128]{2,1,0:T(8,128)(2,1)S(1)} %bitcast.7), channel_id=1, replica_groups=mesh['row'=32,'ch'=4] {'ch','row'}, dimensions={0} | all-to-all | bytes 1048576 | tf_op jit(solution)/shard_map/all_to_all | solution.py:309
  52.0 2.2 %middle.1 = (f32[16,128,128]{2,1,0:T(8,128)S(1)}, bf16[16,128,128]{2,1,0:T(8,128)(2,1)S(1)}, bf16[128,2,16,128]{3,2,1,0:T(8,128)(2,1)S(1)}) custom-call(bf16[128,16,128]{2,1,0:T(8,128)(2,1)S(1)} %all_to_all.20.y, f32[16,128,128]{2,1,0:T(8,128)S(1)} %get-tuple-element.19._state.z0, f32[16,128,128]{2,1,0:T(8,128)S(1)} %get-tuple-element.18._gate.gate, ...), custom_call_target="tpu_custom_call" | custom-call | tf_op jit(solution)/shard_map/middle/pallas_call | solution.py:238
  54.3 23.7 %all_to_all.21.b = bf16[128,2,16,128]{3,2,1,0:T(8,128)(2,1)S(1)} all-to-all(bf16[128,2,16,128]{3,2,1,0:T(8,128)(2,1)S(1)} %get-tuple-element.22), channel_id=1, replica_groups=mesh['row'=32,'ch'=4] {'ch','row'}, dimensions={0} | all-to-all | bytes 2097152 | tf_op jit(solution)/shard_map/all_to_all | solution.py:317
  78.0 0.5 incoming.1
  78.4 18.0 %all_to_all.22.y = bf16[128,16,128]{2,1,0:T(8,128)(2,1)S(1)} all-to-all(bf16[128,16,128]{2,1,0:T(8,128)(2,1)S(1)} %bitcast.6), channel_id=1, replica_groups=mesh['row'=32,'ch'=4] {'ch','row'}, dimensions={0} | all-to-all | bytes 1048576 | tf_op jit(solution)/shard_map/all_to_all | solution.py:319
  96.4 1.2 last.1
  97.6 0.6 collective-permute-start.3
  98.2 2.7 %collective-permute-start.5 = (bf16[8,128,128]{2,1,0:T(8,128)(2,1)S(1)}, bf16[8,128,128]{2,1,0:T(8,128)(2,1)S(1)}, u32[]{:S(2)}, u32[]{:S(2)}) collective-permute-start(bf16[8,128,128]{2,1,0:T(8,128)(2,1)S(1)} %get-tuple-element.26.own1), channel_id=1, source_target_pairs={{0,3},{1,0},{2,1},{3,2},{4,7},{5,4},{6,5},{7,6},{8,11},{9,8},{10,9... | collective-permute-start | bytes 786440 | tf_op jit(solution)/shard_map/ppermute | solution.py:328
  100.9 0.0 collective-permute-start.8
  100.9 2.0 %collective-permute-start.7 = (bf16[8,128,128]{2,1,0:T(8,128)(2,1)S(1)}, bf16[8,128,128]{2,1,0:T(8,128)(2,1)S(1)}, u32[]{:S(2)}, u32[]{:S(2)}) collective-permute-start(bf16[8,128,128]{2,1,0:T(8,128)(2,1)S(1)} %get-tuple-element.26.own1), channel_id=1, source_target_pairs={{0,1},{1,2},{2,3},{3,0},{4,5},{5,6},{6,7},{7,4},{8,9},{9,10},{10,1... | collective-permute-start | bytes 786440 | tf_op jit(solution)/shard_map/ppermute | solution.py:329
  102.9 5.2 %collective-permute-done.3.up0 = bf16[8,128,128]{2,1,0:T(8,128)(2,1)S(1)} collective-permute-done((bf16[8,128,128]{2,1,0:T(8,128)(2,1)S(1)}, bf16[8,128,128]{2,1,0:T(8,128)(2,1)S(1)}, u32[]{:S(2)}, u32[]{:S(2)}) %collective-permute-start.3) | collective-permute-done | bytes 262176 | tf_op jit(solution)/shard_map/ppermute | solution.py:328
  108.1 3.2 %collective-permute-start.6 = (bf16[8,128,128]{2,1,0:T(8,128)(2,1)S(1)}, bf16[8,128,128]{2,1,0:T(8,128)(2,1)S(1)}, u32[]{:S(2)}, u32[]{:S(2)}) collective-permute-start(bf16[8,128,128]{2,1,0:T(8,128)(2,1)S(1)} %collective-permute-done.5.down1), channel_id=1, source_target_pairs={{0,3},{1,0},{2,1},{3,2},{4,7},{5,4},{6,5},{7,6},{8,11},{9,8},{10,9... | collective-permute-start | bytes 786440 | tf_op jit(solution)/shard_map/ppermute | solution.py:330
  111.3 1.9 %collective-permute-done.8.down0 = bf16[8,128,128]{2,1,0:T(8,128)(2,1)S(1)} collective-permute-done((bf16[8,128,128]{2,1,0:T(8,128)(2,1)S(1)}, bf16[8,128,128]{2,1,0:T(8,128)(2,1)S(1)}, u32[]{:S(2)}, u32[]{:S(2)}) %collective-permute-start.8) | collective-permute-done | bytes 262176 | tf_op jit(solution)/shard_map/ppermute | solution.py:329
  113.3 0.5 collective-permute-done.7.up1
  113.7 1.8 %spread_near.1._ = f32[16,512,128]{2,1,0:T(8,128)} custom-call(bf16[8,128,128]{2,1,0:T(8,128)(2,1)S(1)} %get-tuple-element.25.own0, bf16[8,128,128]{2,1,0:T(8,128)(2,1)S(1)} %get-tuple-element.26.own1, bf16[8,128,128]{2,1,0:T(8,128)(2,1)S(1)} %collective-permute-done.3.up0, bf16[8,128,128]{2,1,0:T(8,128)(2,1)S(1)} %collective-permute-done.7.up1, ...), custom_call_target="tpu_custom_call" | custom-call | tf_op jit(solution)/shard_map/spread_near/pallas_call | solution.py:332
  115.5 2.2 %collective-permute-done.4.far0 = bf16[8,128,128]{2,1,0:T(8,128)(2,1)S(1)} collective-permute-done((bf16[8,128,128]{2,1,0:T(8,128)(2,1)S(1)}, bf16[8,128,128]{2,1,0:T(8,128)(2,1)S(1)}, u32[]{:S(2)}, u32[]{:S(2)}) %collective-permute-start.4) | collective-permute-done | bytes 262176 | tf_op jit(solution)/shard_map/ppermute | solution.py:330
  117.7 1.0 spread_far.1
  (24 shorter events, 0.0 us)
Async XLA Ops:
  0.0 13.6 %copy-start.8 = (f32[2,128]{1,0:T(2,128)S(1)}, f32[2,128]{1,0:T(2,128)}, u32[]{:S(2)}) copy-start(f32[2,128]{1,0:T(2,128)} %in_bias.5) | copy-start | bytes 3076
  0.0 13.6 %copy-start.7 = (f32[2,128]{1,0:T(2,128)S(1)}, f32[2,128]{1,0:T(2,128)}, u32[]{:S(2)}) copy-start(f32[2,128]{1,0:T(2,128)} %in_gain.5) | copy-start | bytes 3076
  0.0 13.7 %copy-start.3 = (bf16[2,128,4,32]{1,3,2,0:T(8,128)(2,1)S(1)}, bf16[2,128,4,32]{1,3,2,0:T(8,128)(2,1)}, u32[]{:S(2)}) copy-start(bf16[2,128,4,32]{1,3,2,0:T(8,128)(2,1)} %param.13) | copy-start | bytes 196612
  0.0 13.7 %copy-start.9 = (s32[512]{0:T(512)S(1)}, s32[512]{0:T(512)}, u32[]{:S(2)}) copy-start(s32[512]{0:T(512)} %param.10) | copy-start | bytes 6148
  0.0 13.7 %copy-start.4 = (bf16[2,128,128]{2,1,0:T(8,128)(2,1)S(1)}, bf16[2,128,128]{2,1,0:T(8,128)(2,1)}, u32[]{:S(2)}) copy-start(bf16[2,128,128]{2,1,0:T(8,128)(2,1)} %w_gate.3) | copy-start | bytes 196612
  0.0 13.7 %copy-start.6 = (bf16[2,32,128]{2,1,0:T(8,128)(2,1)S(1)}, bf16[2,32,128]{2,1,0:T(8,128)(2,1)}, u32[]{:S(2)}) copy-start(bf16[2,32,128]{2,1,0:T(8,128)(2,1)} %w_out.1) | copy-start | bytes 49156
  0.0 13.7 %copy-start.11 = (f32[2,32]{1,0:T(2,128)S(1)}, f32[2,32]{1,0:T(2,128)}, u32[]{:S(2)}) copy-start(f32[2,32]{1,0:T(2,128)} %out_bias.1) | copy-start | bytes 772
  0.0 13.7 %copy-start.10 = (f32[2,32]{1,0:T(2,128)S(1)}, f32[2,32]{1,0:T(2,128)}, u32[]{:S(2)}) copy-start(f32[2,32]{1,0:T(2,128)} %out_gain.1) | copy-start | bytes 772
  5.2 25.8 %all-to-all-start = ((bf16[32,2,16,512]{3,2,1,0:T(8,128)(2,1)}), bf16[32,2,16,512]{3,2,1,0:T(8,128)(2,1)S(1)}, u32[]{:S(2)}, u32[]{:S(2)}) async-start(bf16[32,2,16,512]{3,2,1,0:T(8,128)(2,1)} %project0.1), calls=%async_computation | async-start | bytes 2097152 | tf_op jit(solution)/shard_map/all_to_all | solution.py:280
  13.7 11.6 %copy-start.5 = (bf16[2,128,128]{2,1,0:T(8,128)(2,1)S(1)}, bf16[2,128,128]{2,1,0:T(8,128)(2,1)}, u32[]{:S(2)}) copy-start(bf16[2,128,128]{2,1,0:T(8,128)(2,1)} %w_gate.3) | copy-start | bytes 196612
  15.7 5.7 %collective-permute-start.2 = (bf16[208,128]{1,0:T(8,128)(2,1)S(1)}, bf16[208,128]{1,0:T(8,128)(2,1)S(1)}, u32[]{:S(2)}, u32[]{:S(2)}) collective-permute-start(bf16[208,128]{1,0:T(8,128)(2,1)S(1)} %get-tuple-element.16.own), channel_id=1, source_target_pairs={{0,2},{1,3},{2,0},{3,1},{4,6},{5,7},{6,4},{7,5},{8,10},{9,11},{10,... | collective-permute-start | bytes 159752 | tf_op jit(solution)/shard_map/ppermute | solution.py:300
  18.8 4.1 %collective-permute-start.1 = (bf16[208,128]{1,0:T(8,128)(2,1)S(1)}, bf16[208,128]{1,0:T(8,128)(2,1)S(1)}, u32[]{:S(2)}, u32[]{:S(2)}) collective-permute-start(bf16[208,128]{1,0:T(8,128)(2,1)S(1)} %get-tuple-element.16.own), channel_id=1, source_target_pairs={{0,3},{1,0},{2,1},{3,2},{4,7},{5,4},{6,5},{7,6},{8,11},{9,8},{10,9... | collective-permute-start | bytes 159752 | tf_op jit(solution)/shard_map/ppermute | solution.py:300
  20.0 5.3 %collective-permute-start = (bf16[208,128]{1,0:T(8,128)(2,1)S(1)}, bf16[208,128]{1,0:T(8,128)(2,1)S(1)}, u32[]{:S(2)}, u32[]{:S(2)}) collective-permute-start(bf16[208,128]{1,0:T(8,128)(2,1)S(1)} %get-tuple-element.16.own), channel_id=1, source_target_pairs={{0,1},{1,2},{2,3},{3,0},{4,5},{5,6},{6,7},{7,4},{8,9},{9,10},{10,1... | collective-permute-start | bytes 159752 | tf_op jit(solution)/shard_map/ppermute | solution.py:300
  25.8 0.7 copy-start
  31.0 0.9 copy-start.1
  52.0 44.4 %copy-start.2 = (bf16[7,128,128]{2,1,0:T(8,128)(2,1)S(1)}, bf16[7,128,128]{2,1,0:T(8,128)(2,1)}, u32[]{:S(2)}) copy-start(bf16[7,128,128]{2,1,0:T(8,128)(2,1)} %copy-done) | copy-start | bytes 688132
  97.6 10.5 %collective-permute-start.3 = (bf16[8,128,128]{2,1,0:T(8,128)(2,1)S(1)}, bf16[8,128,128]{2,1,0:T(8,128)(2,1)S(1)}, u32[]{:S(2)}, u32[]{:S(2)}) collective-permute-start(bf16[8,128,128]{2,1,0:T(8,128)(2,1)S(1)} %get-tuple-element.25.own0), channel_id=1, source_target_pairs={{0,1},{1,2},{2,3},{3,0},{4,5},{5,6},{6,7},{7,4},{8,9},{9,10},{10,1... | collective-permute-start | bytes 786440 | tf_op jit(solution)/shard_map/ppermute | solution.py:328
  98.2 9.9 %collective-permute-start.5 = (bf16[8,128,128]{2,1,0:T(8,128)(2,1)S(1)}, bf16[8,128,128]{2,1,0:T(8,128)(2,1)S(1)}, u32[]{:S(2)}, u32[]{:S(2)}) collective-permute-start(bf16[8,128,128]{2,1,0:T(8,128)(2,1)S(1)} %get-tuple-element.26.own1), channel_id=1, source_target_pairs={{0,3},{1,0},{2,1},{3,2},{4,7},{5,4},{6,5},{7,6},{8,11},{9,8},{10,9... | collective-permute-start | bytes 786440 | tf_op jit(solution)/shard_map/ppermute | solution.py:328
  100.9 12.4 %collective-permute-start.8 = (bf16[8,128,128]{2,1,0:T(8,128)(2,1)S(1)}, bf16[8,128,128]{2,1,0:T(8,128)(2,1)S(1)}, u32[]{:S(2)}, u32[]{:S(2)}) collective-permute-start(bf16[8,128,128]{2,1,0:T(8,128)(2,1)S(1)} %get-tuple-element.25.own0), channel_id=1, source_target_pairs={{0,3},{1,0},{2,1},{3,2},{4,7},{5,4},{6,5},{7,6},{8,11},{9,8},{10,9... | collective-permute-start | bytes 786440 | tf_op jit(solution)/shard_map/ppermute | solution.py:329
  100.9 12.8 %collective-permute-start.7 = (bf16[8,128,128]{2,1,0:T(8,128)(2,1)S(1)}, bf16[8,128,128]{2,1,0:T(8,128)(2,1)S(1)}, u32[]{:S(2)}, u32[]{:S(2)}) collective-permute-start(bf16[8,128,128]{2,1,0:T(8,128)(2,1)S(1)} %get-tuple-element.26.own1), channel_id=1, source_target_pairs={{0,1},{1,2},{2,3},{3,0},{4,5},{5,6},{6,7},{7,4},{8,9},{9,10},{10,1... | collective-permute-start | bytes 786440 | tf_op jit(solution)/shard_map/ppermute | solution.py:329
  108.1 9.6 %collective-permute-start.4 = (bf16[8,128,128]{2,1,0:T(8,128)(2,1)S(1)}, bf16[8,128,128]{2,1,0:T(8,128)(2,1)S(1)}, u32[]{:S(2)}, u32[]{:S(2)}) collective-permute-start(bf16[8,128,128]{2,1,0:T(8,128)(2,1)S(1)} %collective-permute-done.3.up0), channel_id=1, source_target_pairs={{0,1},{1,2},{2,3},{3,0},{4,5},{5,6},{6,7},{7,4},{8,9},{9,10},{10,1... | collective-permute-start | bytes 786440 | tf_op jit(solution)/shard_map/ppermute | solution.py:330
  108.1 9.6 %collective-permute-start.6 = (bf16[8,128,128]{2,1,0:T(8,128)(2,1)S(1)}, bf16[8,128,128]{2,1,0:T(8,128)(2,1)S(1)}, u32[]{:S(2)}, u32[]{:S(2)}) collective-permute-start(bf16[8,128,128]{2,1,0:T(8,128)(2,1)S(1)} %collective-permute-done.5.down1), channel_id=1, source_target_pairs={{0,3},{1,0},{2,1},{3,2},{4,7},{5,4},{6,5},{7,6},{8,11},{9,8},{10,9... | collective-permute-start | bytes 786440 | tf_op jit(solution)/shard_map/ppermute | solution.py:330
